TPU v7x, 32 devices: a whole 2x2x4 slice. The times are simulated.
32 devices in a mesh: pipe: 2 (over y), tx: 4 (over z), ty: 4 (over x, core).
Axes of the slice: x: 2, y: 2, z: 4, core: 2. Of those that a mesh axis runs over, the one named last changes fastest.
Arguments:
- section_input: bfloat16 [2, 48, 8192], P('pipe', 'tx', 'ty'), may hold values from -6 to 6
- saved_input: bfloat16 [2, 48, 8192], P('pipe', 'tx', 'ty'), may hold values from -6 to 6
- out_grad: bfloat16 [2, 48, 8192], P('pipe', 'tx', 'ty'), may hold values from -6 to 6
- gate_weight: bfloat16 [2, 8192, 29568], P('pipe', 'ty', 'tx'), may hold values from -0.0625 to 0.0625
- up_weight: bfloat16 [2, 8192, 29568], P('pipe', 'ty', 'tx'), may hold values from -0.0625 to 0.0625
- down_weight: bfloat16 [2, 29568, 8192], P('pipe', 'tx', 'ty'), may hold values from -0.03125 to 0.03125
Outputs:
- next_input: bfloat16 [2, 48, 8192], P('pipe', 'tx', 'ty')
- prev_grad: bfloat16 [2, 48, 8192], P('pipe', 'tx', 'ty')
All inputs are finite; a program needn't handle non-finite values.
Results may differ from a plain program's by a relative error of at most 0.0038.
Values may be sent and summed in bfloat16 or wider, within the bound.
No kernel may reach another device: no remote copies, remote signals or barrier semaphores. Data moves between devices by JAX's collectives and lax.ppermute only.
A program may use at most 192 MiB of HBM per device.

v0:
```python
import jax
import jax.numpy as jnp
from jax import lax
from jax.sharding import PartitionSpec as P


def passed_along(value, axis, steps):
    count = lax.axis_size(axis)
    pairs = [(source, (source + steps) % count) for source in range(count)]
    return lax.ppermute(value, axis, pairs)


def activate(gate, up, saved_gate, saved_up, hidden_grad):
    hidden = (jax.nn.silu(gate) * up).astype(jnp.bfloat16)
    sigma = jax.nn.sigmoid(saved_gate)
    gate_grad = (hidden_grad * saved_up * sigma * (1.0 + saved_gate * (1.0 - sigma))).astype(
        jnp.bfloat16
    )
    up_grad = (hidden_grad * saved_gate * sigma).astype(jnp.bfloat16)
    return (hidden, gate_grad, up_grad)


def local(section_input, saved_input, out_grad, gate_weight, up_weight, down_weight):
    own_input = section_input[0]
    own_grad = out_grad[0]
    wgate = gate_weight[0]
    wup = up_weight[0]
    wdown = down_weight[0]
    width_local = own_input.shape[1]
    inputs, saved, grads = (
        lax.all_gather(own_input, "tx", axis=0, tiled=True),
        lax.all_gather(saved_input[0], "tx", axis=0, tiled=True),
        lax.all_gather(own_grad, "tx", axis=0, tiled=True),
    )
    dims = (((1,), (1,)), ((), ()))
    part_gate = jnp.dot(inputs, wgate, preferred_element_type=jnp.float32)
    part_up = jnp.dot(inputs, wup, preferred_element_type=jnp.float32)
    part_sgate = jnp.dot(saved, wgate, preferred_element_type=jnp.float32)
    part_sup = jnp.dot(saved, wup, preferred_element_type=jnp.float32)
    part_hgrad = lax.dot_general(grads, wdown, dims, preferred_element_type=jnp.float32)
    partials = (part_gate, part_up, part_sgate, part_sup, part_hgrad)
    gate, up, saved_gate, saved_up, hidden_grad = lax.psum(
        (partials[0], partials[1], partials[2], partials[3], partials[4]), "ty"
    )
    hidden, gate_grad, up_grad = activate(gate, up, saved_gate, saved_up, hidden_grad)
    mixed = jnp.dot(hidden, wdown, preferred_element_type=jnp.float32)
    back = lax.dot_general(gate_grad, wgate, dims, preferred_element_type=jnp.float32)
    back = back + lax.dot_general(up_grad, wup, dims, preferred_element_type=jnp.float32)
    summed = lax.psum_scatter(
        jnp.concatenate([mixed, back], axis=1), "tx", scatter_dimension=0, tiled=True
    )
    forward_out = (own_input.astype(jnp.float32) + summed[:, :width_local]).astype(jnp.bfloat16)
    input_grad = (own_grad.astype(jnp.float32) + summed[:, width_local:]).astype(jnp.bfloat16)
    next_input = passed_along(forward_out, "pipe", 1)
    prev_grad = passed_along(input_grad, "pipe", -1)
    return (next_input[None], prev_grad[None])


def solution(mesh):
    return jax.shard_map(
        local,
        mesh=mesh,
        in_specs=(
            P("pipe", "tx", "ty"),
            P("pipe", "tx", "ty"),
            P("pipe", "tx", "ty"),
            P("pipe", "ty", "tx"),
            P("pipe", "ty", "tx"),
            P("pipe", "tx", "ty"),
        ),
        out_specs=(P("pipe", "tx", "ty"), P("pipe", "tx", "ty")),
        check_vma=False,
    )
```

profile of v0, /device:TPU:0, one launch (start us, length us, event | category | flops | bytes accessed | tf_op | source)
XLA Modules:
  0.0 370.0 jit_solution(1296855151683241010)
XLA Ops:
  7.2 0.9 copy.13
  8.1 16.2 %all-gather.2 = bf16[1,48,2048]{2,0,1:T(2,128)(2,1)S(1)} all-gather(bf16[1,12,2048]{2,0,1:T(2,128)(2,1)S(1)} %copy.13), channel_id=4, replica_groups=mesh['pipe'=2,'tx'=4,'ty'=4] {'tx'}, dimensions={1}, use_global_device_ids=true | all-gather | bytes 245760 | tf_op jit(solution)/shard_map/all_gather | solution.py:32
  24.4 0.9 copy.11
  25.3 15.4 %all-gather = bf16[1,48,2048]{2,0,1:T(2,128)(2,1)S(1)} all-gather(bf16[1,12,2048]{2,0,1:T(2,128)(2,1)S(1)} %copy.11), channel_id=2, replica_groups=mesh['pipe'=2,'tx'=4,'ty'=4] {'tx'}, dimensions={1}, use_global_device_ids=true | all-gather | bytes 245760 | tf_op jit(solution)/shard_map/all_gather | solution.py:31
  40.7 15.7 %fusion.12 = f32[48,7392]{1,0:T(8,128)} fusion(bf16[1,2048,7392]{1,2,0:T(8,128)(2,1)} %param.9, bf16[1,48,2048]{2,0,1:T(2,128)(2,1)S(1)} %all-gather.2), kind=kOutput, calls=%fused_computation.12 | convolution fusion | flops 1453326336 | bytes 31893504 | tf_op jit(solution)/shard_map/dot_general | solution.py:38
  56.4 15.7 %fusion.14 = f32[48,7392]{1,0:T(8,128)} fusion(bf16[1,2048,7392]{1,2,0:T(8,128)(2,1)} %param.9, bf16[1,48,2048]{2,0,1:T(2,128)(2,1)S(1)} %all-gather), kind=kOutput, calls=%fused_computation.14 | convolution fusion | flops 1453326336 | bytes 31893504 | tf_op jit(solution)/shard_map/dot_general | solution.py:36
  72.1 15.7 %fusion.6 = f32[48,7392]{1,0:T(8,128)} fusion(bf16[1,2048,7392]{1,2,0:T(8,128)(2,1)} %param.10, bf16[1,48,2048]{2,0,1:T(2,128)(2,1)S(1)} %all-gather.2), kind=kOutput, calls=%fused_computation.6 | convolution fusion | flops 1453326336 | bytes 31893504 | tf_op jit(solution)/shard_map/dot_general | solution.py:39
  87.8 15.7 %fusion.8 = f32[48,7392]{1,0:T(8,128)} fusion(bf16[1,2048,7392]{1,2,0:T(8,128)(2,1)} %param.10, bf16[1,48,2048]{2,0,1:T(2,128)(2,1)S(1)} %all-gather), kind=kOutput, calls=%fused_computation.8 | convolution fusion | flops 1453326336 | bytes 31893504 | tf_op jit(solution)/shard_map/dot_general | solution.py:37
  103.6 14.4 %all-gather.1 = bf16[1,48,2048]{2,0,1:T(2,128)(2,1)S(1)} all-gather(bf16[1,12,2048]{2,0,1:T(2,128)(2,1)S(1)} %copy.12), channel_id=3, replica_groups=mesh['pipe'=2,'tx'=4,'ty'=4] {'tx'}, dimensions={1}, use_global_device_ids=true | all-gather | bytes 245760 | tf_op jit(solution)/shard_map/all_gather | solution.py:33
  118.0 15.7 %fusion = f32[48,7392]{1,0:T(8,128)} fusion(bf16[1,7392,2048]{2,1,0:T(8,128)(2,1)} %param.11, bf16[1,48,2048]{2,0,1:T(2,128)(2,1)S(1)} %all-gather.1), kind=kOutput, calls=%fused_computation | convolution fusion | flops 1453326336 | bytes 31893504 | tf_op jit(solution)/shard_map/dot_general | solution.py:40
  133.8 135.6 %all-reduce.7.cloned.1.call-done = (f32[48,7392]{1,0:T(8,128)}, f32[48,7392]{1,0:T(8,128)}, f32[48,7392]{1,0:T(8,128)}, f32[48,7392]{1,0:T(8,128)}, f32[48,7392]{1,0:T(8,128)}) async-done(((f32[48,7392]{1,0:T(8,128)}, f32[48,7392]{1,0:T(8,128)}, f32[48,7392]{1,0:T(8,128)}, f32[48,7392]{1,0:T(8,128)}, f32[48,7392]{1,0:T(8,128)}), (f32[48,7392]{1,0:T(8,128)}, f32[48,7392]{1,0:T(8,128)}, f32[48,7392]{1,0:T(8,128)}, ...) | async-done | bytes 7096336 | tf_op jit(solution)/shard_map/psum | solution.py:42
  269.5 15.7 %fusion.4 = f32[48,2048]{1,0:T(8,128)S(1)} fusion(bf16[1,2048,7392]{1,2,0:T(8,128)(2,1)} %param.10, f32[48,7392]{1,0:T(8,128)} %get-tuple-element.2, f32[48,7392]{1,0:T(8,128)} %get-tuple-element.3), kind=kOutput, calls=%fused_computation.4 | convolution fusion | flops 1455455232 | bytes 33509376 | tf_op jit(solution)/shard_map/dot_general | solution.py:48
  285.2 12.5 %fusion.16 = f32[48,2048]{1,0:T(8,128)S(1)} fusion(f32[48,2048]{1,0:T(8,128)S(1)} %fusion.4, bf16[1,2048,7392]{1,2,0:T(8,128)(2,1)} %param.9, f32[48,7392]{1,0:T(8,128)S(1)} %copy-done.1, f32[48,7392]{1,0:T(8,128)S(1)} %copy-done, f32[48,7392]{1,0:T(8,128)S(1)} %copy-done.2), kind=kOutput, calls=%fused_computation.16 | convolution fusion | flops 1456972800 | bytes 35321856 | tf_op jit(solution)/shard_map/dot_general | solution.py:47
  297.7 12.3 %fusion.2 = f32[48,2048]{1,0:T(8,128)S(1)} fusion(bf16[1,7392,2048]{2,1,0:T(8,128)(2,1)} %param.11, f32[48,7392]{1,0:T(8,128)S(1)} %copy-done.3, f32[48,7392]{1,0:T(8,128)S(1)} %copy-done.4), kind=kOutput, calls=%fused_computation.2 | convolution fusion | flops 1455455232 | bytes 33509376 | tf_op jit(solution)/shard_map/dot_general | solution.py:46
  310.1 1.0 pad_maximum_fusion
  311.1 0.6 dynamic-slice
  312.3 42.7 %all-reduce.5.cloned.1.call-done = f32[48,4096]{1,0:T(8,128)} async-done(((f32[48,4096]{1,0:T(8,128)}), f32[48,4096]{1,0:T(8,128)}) %all-reduce.5.cloned.1.call-update) | async-done | bytes 786448
  355.0 1.1 fusion.28
  356.1 1.5 collective-permute-start
  357.7 0.6 collective-permute-start.1
  358.2 2.9 collective-permute-done
  361.1 0.8 collective-permute-done.1
  361.9 0.6 copy.45
  362.6 0.6 copy.46
  (21 shorter events, 0.2 us)
Async XLA Ops:
  7.2 262.3 %all-reduce.7.cloned.1.call-start = ((), (), s32[]{:S(2)}) async-start(), calls=%async_computation.1 | async-start | bytes 14254080 | tf_op jit(solution)/shard_map/psum | solution.py:42
  87.8 15.7 %copy-start.5 = (bf16[1,12,2048]{2,1,0:T(8,128)(2,1)S(1)}, bf16[1,12,2048]{2,1,0:T(8,128)(2,1)}, u32[]{:S(2)}) copy-start(bf16[1,12,2048]{2,1,0:T(8,128)(2,1)} %param.8) | copy-start | bytes 147460
  133.8 221.2 %all-reduce.5.cloned.1.call-start = ((), (), s32[]{:S(2)}) async-start(), calls=%async_computation | async-start | bytes 1572864
  269.5 15.7 %copy-start = (f32[48,7392]{1,0:T(8,128)S(1)}, f32[48,7392]{1,0:T(8,128)}, u32[]{:S(2)}) copy-start(f32[48,7392]{1,0:T(8,128)} %get-tuple-element.2) | copy-start | bytes 4257796
  269.5 15.7 %copy-start.1 = (f32[48,7392]{1,0:T(8,128)S(1)}, f32[48,7392]{1,0:T(8,128)}, u32[]{:S(2)}) copy-start(f32[48,7392]{1,0:T(8,128)} %get-tuple-element.3) | copy-start | bytes 4257796
  269.5 15.7 %copy-start.2 = (f32[48,7392]{1,0:T(8,128)S(1)}, f32[48,7392]{1,0:T(8,128)}, u32[]{:S(2)}) copy-start(f32[48,7392]{1,0:T(8,128)} %get-tuple-element.4) | copy-start | bytes 4257796
  285.2 12.5 %copy-start.3 = (f32[48,7392]{1,0:T(8,128)S(1)}, f32[48,7392]{1,0:T(8,128)}, u32[]{:S(2)}) copy-start(f32[48,7392]{1,0:T(8,128)} %get-tuple-element.5) | copy-start | bytes 4257796
  285.2 12.5 %copy-start.4 = (f32[48,7392]{1,0:T(8,128)S(1)}, f32[48,7392]{1,0:T(8,128)}, u32[]{:S(2)}) copy-start(f32[48,7392]{1,0:T(8,128)} %get-tuple-element.6) | copy-start | bytes 4257796
  310.0 1.0 copy-start.7
  310.1 44.9 %copy-start.6 = (bf16[1,12,2048]{2,1,0:T(8,128)(2,1)S(1)}, bf16[1,12,2048]{2,1,0:T(8,128)(2,1)}, u32[]{:S(2)}) copy-start(bf16[1,12,2048]{2,1,0:T(8,128)(2,1)} %param.6) | copy-start | bytes 147460
  356.1 5.0 %collective-permute-start = (bf16[12,2048]{1,0:T(8,128)(2,1)S(1)}, bf16[12,2048]{1,0:T(8,128)(2,1)S(1)}, u32[]{:S(2)}, u32[]{:S(2)}) collective-permute-start(bf16[12,2048]{1,0:T(8,128)(2,1)S(1)} %get-tuple-element.8), channel_id=1, source_target_pairs={{0,16},{16,0},{1,17},{17,1},{2,18},{18,2},{3,19},{19,3},{4,20},{20... | collective-permute-start | bytes 147464 | tf_op jit(solution)/shard_map/ppermute | solution.py:10
  357.7 4.3 %collective-permute-start.1 = (bf16[12,2048]{1,0:T(8,128)(2,1)S(1)}, bf16[12,2048]{1,0:T(8,128)(2,1)S(1)}, u32[]{:S(2)}, u32[]{:S(2)}) collective-permute-start(bf16[12,2048]{1,0:T(8,128)(2,1)S(1)} %get-tuple-element.7), channel_id=1, source_target_pairs={{0,16},{16,0},{1,17},{17,1},{2,18},{18,2},{3,19},{19,3},{4,20},{20... | collective-permute-start | bytes 147464 | tf_op jit(solution)/shard_map/ppermute | solution.py:10
Sparse Core Ops, SparseCore 0:
  133.9 135.5 all-reduce.6
  311.2 43.7 all-reduce.4
where the time goes:
time: 370 us
  waiting for transfers between devices  182 us (49%)
  matrix products  119 us (32%)
  blocking collectives  46.1 us (12%)
  between operations  14.8 us (4%)
  local copies, waits for them, and re-layouts  3.8 us (1%)
    psum x1, waiting for transfers between devices, local(): lax.psum((partials[0], partials[1], partials[2], partials[3], partials[4]...  136 us
    unnamed x3, waiting for transfers between devices  42.7 us
    all_gather x1, blocking collectives, local(): lax.all_gather(saved_input[0], 'tx', axis=0, tiled=True)  16.2 us
    dot_general x1, matrix products, local(): lax.dot_general(grads, wdown, dims, preferred_element_type=jnp.float32)  15.7 us
    dot_general x1, matrix products, local(): part_up = jnp.dot(inputs, wup, preferred_element_type=jnp.float32)  15.7 us
    dot_general x1, matrix products, local(): part_sgate = jnp.dot(saved, wgate, preferred_element_type=jnp.float32)  15.7 us
    dot_general x1, matrix products, local(): lax.dot_general(up_grad, wup, dims, preferred_element_type=jnp.float32)  15.7 us
    dot_general x1, matrix products, local(): part_gate = jnp.dot(inputs, wgate, preferred_element_type=jnp.float32)  15.7 us
  transfers between devices with their start and end apart: 4, of which 4 were waited for; matrix products, arithmetic and copies ran while one was open for 0% of the time, Pallas kernels for 0%

commit v1 on v0

v1 whole, which is shorter than its diff:
```python
import functools

import jax
import jax.numpy as jnp
from jax import lax
from jax.experimental import pallas as pl
from jax.experimental.pallas import tpu as pltpu
from jax.sharding import PartitionSpec as P

F32 = jnp.float32
BF16 = jnp.bfloat16
NN = (((1,), (0,)), ((), ()))
NT = (((1,), (1,)), ((), ()))
VM = pl.BlockSpec(memory_space=pltpu.VMEM)
HBM = pl.BlockSpec(memory_space=pltpu.HBM)
SM = pl.BlockSpec(memory_space=pltpu.SMEM)
STEP = 512
SLOTS = 5


def contract(a, b, dims):
    return lax.dot_general(a, b, dims, preferred_element_type=F32)


def params():
    return pltpu.CompilerParams(vmem_limit_bytes=4 * 2**20)


def cost(flops, moved):
    return pl.CostEstimate(flops=flops, bytes_accessed=moved, transcendentals=0)


def spans(size, step=STEP):
    return [(at, min(step, size - at)) for at in range(0, size, step)]


def up_to(value, unit):
    return -(-value // unit) * unit


def fetches(table_ref, stored, arena, loads, sems):
    copies = []
    for n, (at, rows, entry) in enumerate(loads):
        start = pl.multiple_of(table_ref[entry], 16)
        for i, source in enumerate(stored):
            target = arena.at[pl.ds(at + i * rows, rows), :]
            copies.append(pltpu.make_async_copy(source.at[pl.ds(start, rows), :], target, sems.at[n, i]))
    return copies


def begin(copies):
    for copy in copies:
        copy.start()


def end(copies):
    for copy in copies:
        copy.wait()


def call(body, operands, specs, shapes, arena, loads, table, stored, flops):
    body = functools.partial(body, loads)
    operands, specs, shapes = list(operands), list(specs), list(shapes)
    aliases, scratch, moved = {}, [], 0
    operands.append(table)
    specs.append(SM)
    if loads:
        operands += stored
        specs += [HBM] * 3
        scratch.append(pltpu.SemaphoreType.DMA((len(loads), 3)))
        moved = sum(6 * rows * stored[0].shape[1] for _, rows, _ in loads)
    if isinstance(arena, tuple):
        shape = arena
    else:
        shape = arena.shape
        aliases = {len(operands): len(shapes)}
        operands.append(arena)
        specs.append(VM)
    return pl.pallas_call(
        body,
        in_specs=specs,
        out_specs=[VM] * (len(shapes) + 1),
        out_shape=shapes + [pltpu.VMEM(shape, BF16)],
        scratch_shapes=scratch,
        input_output_aliases=aliases,
        compiler_params=params(),
        cost_estimate=cost(flops, moved),
    )(*operands)


def split(refs, loads, count, outs, carried):
    refs = list(refs)
    operands = refs[:count]
    table_ref, refs = refs[count], refs[count + 1 :]
    if loads:
        stored, refs = refs[:3], refs[3:]
    if carried:
        refs = refs[1:]
    results, arena = refs[:outs], refs[outs]
    copies = fetches(table_ref, stored, arena, loads, refs[outs + 1]) if loads else []
    return operands, results, arena, copies


def load_body(loads, *refs):
    copies = split(refs, loads, 0, 0, False)[3]
    begin(copies)
    end(copies)


def project_body(at, rows, has_more, loads, *refs):
    more, (out_ref,), arena, copies = split(refs, loads, has_more, 1, True)
    begin(copies)
    tokens = out_ref.shape[0] // 5
    base = arena.shape[0] - 3 * tokens
    for low, size in spans(rows):
        piece = pl.ds(low, size)
        for i, (first, count) in enumerate(((0, 2), (0, 2), (2, 1))):
            to = pl.ds(2 * i * tokens, count * tokens)
            lhs = arena[pl.ds(base + first * tokens, count * tokens), :]
            part = contract(lhs, arena[pl.ds(at + i * rows + low, size), :], NT)
            if has_more:
                part = part + more[0][to, piece]
            out_ref[to, piece] = part.astype(out_ref.dtype)
    end(copies)


def project(tokens, arena, slot, more, dtype, loads, table, stored):
    at, rows = slot
    width = arena.shape[1]
    operands = [more] if more is not None else []
    return call(
        functools.partial(project_body, at, rows, more is not None),
        operands,
        [VM] * len(operands),
        [jax.ShapeDtypeStruct((5 * tokens, rows), dtype)],
        arena,
        loads,
        table,
        stored,
        2 * 5 * tokens * rows * width,
    )


def activate_body(entry, others, loads, *refs):
    (own_ref, *got), (out_ref,), _, copies = split(refs, loads, 1 + others, 1, True)
    begin(copies)
    table_ref = refs[1 + others]
    t = own_ref.shape[0] // 5
    for low, size in spans(own_ref.shape[1], 256):
        piece = pl.ds(low, size)
        total = own_ref[:, piece]
        for ref in got:
            total = total + ref[:, piece].astype(F32)
        gate, saved_gate, up, saved_up, hidden_grad = [total[i * t : (i + 1) * t] for i in range(5)]
        column = lax.broadcasted_iota(jnp.int32, gate.shape, 1) + low
        mine = column >= table_ref[entry]
        hidden = gate * jax.nn.sigmoid(gate) * up
        sigma = jax.nn.sigmoid(saved_gate)
        gate_grad = hidden_grad * saved_up * sigma * (1.0 + saved_gate * (1.0 - sigma))
        up_grad = hidden_grad * saved_gate * sigma
        for i, value in enumerate((hidden, gate_grad, up_grad)):
            out_ref[i * t : (i + 1) * t, piece] = jnp.where(mine, value, 0.0).astype(BF16)
    end(copies)


def activate(entry, own, others, arena, loads, table, stored):
    rows, columns = own.shape
    operands = [own, *others]
    return call(
        functools.partial(activate_body, entry, len(others)),
        operands,
        [VM] * len(operands),
        [jax.ShapeDtypeStruct((rows // 5 * 3, columns), BF16)],
        arena,
        loads,
        table,
        stored,
        20 * rows * columns,
    )


def expand_body(slots, has_sum, parts, ends, loads, *refs):
    count = len(slots) + has_sum * len(parts)
    operands, outs, arena, copies = split(refs, loads, count, len(parts) * (1 + ends), True)
    begin(copies)
    held, sums = operands[: len(slots)], operands[len(slots) :]
    t = held[0].shape[0] // 3
    for low, size in spans(arena.shape[1]):
        piece = pl.ds(low, size)
        for i, part in enumerate(parts):
            value = sums[i][:, piece] if has_sum else 0.0
            for (at, rows), h_ref in zip(slots, held):
                for n in (0,) if part == "ahead" else (1, 2):
                    weight = arena[pl.ds(at + (n + 2) % 3 * rows, rows), piece]
                    value = value + contract(h_ref[pl.ds(n * t, t), :], weight, NN)
            if ends:
                outs[0][:, piece] = value[: t // 2]
                outs[1][:, piece] = value[t // 2 :].astype(BF16)
            else:
                outs[i][:, piece] = value
    end(copies)


def expand(held, arena, slots, sums, parts, ends, loads, table, stored):
    rows = sum(rows for _, rows in slots)
    t, width = held[0].shape[0] // 3, arena.shape[1]
    operands = held + (sums or [])
    shapes = [jax.ShapeDtypeStruct((t, width), F32)] * len(parts)
    if ends:
        shapes = [jax.ShapeDtypeStruct((t // 2, width), dtype) for dtype in (F32, BF16)]
    out = call(
        functools.partial(expand_body, slots, sums is not None, parts, ends),
        operands,
        [VM] * len(operands),
        shapes,
        arena,
        loads,
        table,
        stored,
        2 * (1 if len(parts) == 1 else 3) * t * rows * width,
    )
    return list(out[:-1]), out[-1]


def swap(value, axis, bit):
    return lax.ppermute(value, axis, [(i, i ^ bit) for i in range(lax.axis_size(axis))])


def to_chip(value, k):
    count = lax.axis_size("ty")
    return lax.ppermute(value, "ty", [(i, (i + 2 * k) % count) for i in range(count)])


def cross_pipe(value, step, bit):
    sections, count = lax.axis_size("pipe"), lax.axis_size("tx")
    pairs = [
        (p * count + i, (p + step) % sections * count + (i ^ bit))
        for p in range(sections)
        for i in range(count)
    ]
    return lax.ppermute(value, ("pipe", "tx"), pairs)


def finish(kept, gone, own, step):
    count = lax.axis_size("tx")
    t = own.shape[0]
    bit = 1
    while bit < count:
        if 2 * bit < count:
            kept = kept + swap(gone, "tx", bit).astype(F32)
            half = kept.shape[0] // 2
            kept, gone = kept[:half], kept[half:].astype(BF16)
        else:
            kept = cross_pipe(kept + own.astype(F32), step, 0) + cross_pipe(gone, step, bit).astype(F32)
        bit *= 2
    return kept.astype(BF16)


def gather_body(t, count, loads, *refs):
    blocks, _, arena, copies = split(refs, loads, count, 0, True)
    begin(copies)
    group = 16
    stack = jnp.concatenate([ref[...] for ref in blocks], axis=0)
    shape = (3 * count * t, stack.shape[0])
    row = lax.broadcasted_iota(jnp.int32, shape, 0)
    column = lax.broadcasted_iota(jnp.int32, shape, 1)
    kind, row = row // (count * t), row % (count * t)
    source = (row // t) * (3 * group) + kind * group + row % t
    pick = jnp.where(column == source, 1.0, 0.0).astype(BF16)
    base = arena.shape[0] - shape[0]
    for low, size in spans(stack.shape[1]):
        piece = pl.ds(low, size)
        arena[pl.ds(base, shape[0]), piece] = contract(pick, stack[:, low : low + size], NN).astype(BF16)
    end(copies)


def gathered(section, saved, grads, arena, loads, table, stored):
    count = lax.axis_size("tx")
    t, width = section.shape
    own = jnp.concatenate([jnp.pad(a, ((0, 16 - t), (0, 0))) for a in (section, saved, grads)])
    blocks = {0: own}
    bit = count // 2
    while bit:
        for i in list(blocks):
            blocks[i ^ bit] = swap(blocks[i], "tx", bit)
        bit //= 2
    bits = count.bit_length() - 1
    order = [int(format(n, f"0{bits}b")[::-1], 2) if bits else 0 for n in range(count)]
    operands = [blocks[i] for i in order]
    body = functools.partial(gather_body, t, count)
    return call(body, operands, [VM] * count, [], arena, loads, table, stored, 0)[0]


def residency(groups, slots, most):
    uses = [piece for group in groups for piece in group]

    def next_use(piece, after):
        return next((n for n in range(after, len(uses)) if uses[n] == piece), len(uses))

    begun = [(piece, slot) for slot, piece in enumerate(list(dict.fromkeys(uses))[:slots])]
    holds = {slot: piece for piece, slot in begun}
    loads_at, slot_at, after = [], [], 0
    for group in groups:
        after += len(group)
        slot_at.append([next(slot for slot, piece in holds.items() if piece == use) for use in group])
        loads = []
        for piece in dict.fromkeys(uses[after:]):
            if piece in holds.values() or len(loads) == most:
                continue
            slot = max((s for s in holds if s not in slot_at[-1]), key=lambda s: next_use(holds[s], after))
            if next_use(holds[slot], after) > next_use(piece, after):
                loads.append((piece, slot))
                holds[slot] = piece
        loads_at.append(loads)
    return begun, loads_at, slot_at


def local(section_input, saved_input, out_grad, gate_weight, up_weight, down_weight):
    count, tx = lax.axis_size("ty"), lax.axis_size("tx")
    chips = count // 2
    stored = [jnp.swapaxes(gate_weight[0], 0, 1), jnp.swapaxes(up_weight[0], 0, 1), down_weight[0]]
    units = up_to(stored[0].shape[0], 16)
    if units != stored[0].shape[0]:
        stored = [jnp.pad(w, ((0, units - w.shape[0]), (0, 0))) for w in stored]
    share = up_to(-(-units // count), 16)
    cut = share // 2 // 128 * 128
    subs = [(0, cut), (cut, share - cut)] if cut else [(0, share)]
    most = 3 * max(rows for _, rows in subs)

    me = lax.axis_index("ty")
    core, chip = me % 2, me // 2

    def share_of(k, mine):
        owner = (chip + k) % chips * 2 + (core if mine else 1 - core)
        return owner * share, jnp.minimum(owner * share, units - share)

    def place(k, mine, sub):
        return (share_of(k, mine)[1] + subs[sub][0]).astype(jnp.int32)

    def pieces(chip_order, core_order):
        return [(k, mine, sub) for k in chip_order for mine in core_order for sub in range(len(subs))]

    early = pieces(list(range(1, chips)) + [0], (False, True))
    late = pieces(range(chips), (True, False))
    groups = [[piece] for piece in early]
    groups += [late[n : n + len(subs)] for n in range(0, len(late), len(subs))]
    begun, loads_at, slot_at = residency(groups, SLOTS, 2)

    entries = {piece: n for n, piece in enumerate(early)}
    share_at, within = share_of(0, True)
    table = jnp.stack(
        [place(*piece) for piece in early]
        + [(share_at - within - at).astype(jnp.int32) for at, _ in subs]
    )

    def request(items):
        return [(slot * most, subs[piece[2]][1], entries[piece]) for piece, slot in items], table, stored

    tokens = tx * section_input.shape[1]
    (arena,) = call(load_body, [], [], [], (SLOTS * most + 3 * tokens, stored[0].shape[1]), *request(begun), 0)
    arena = gathered(section_input[0], saved_input[0], out_grad[0], arena, *request([]))
    passed, arrived, own = {}, {}, {}
    for n, (k, mine, sub) in enumerate(early):
        more = passed.pop((k, sub)) if mine else None
        dtype = BF16 if mine and k else F32
        slot = (slot_at[n][0] * most, subs[sub][1])
        part, arena = project(tokens, arena, slot, more, dtype, *request(loads_at[n]))
        if not mine:
            passed[k, sub] = swap(part, "ty", 1)
        elif k:
            arrived.setdefault(sub, []).append(to_chip(part, k))
        else:
            own[sub] = part

    h = {}
    for sub in range(len(subs)):
        h[0, True, sub], arena = activate(len(early) + sub, own[sub], arrived.get(sub, []), arena, *request([]))
        h[0, False, sub] = swap(h[0, True, sub], "ty", 1)
        for k in range(1, chips):
            h[k, True, sub] = to_chip(h[0, True, sub], chips - k)
            h[k, False, sub] = swap(h[k, True, sub], "ty", 1)

    sums = None
    both = ("ahead", "back")
    for n, group in enumerate(groups[len(early) :]):
        at = len(early) + n
        slots = [(slot * most, subs[piece[2]][1]) for slot, piece in zip(slot_at[at], group)]
        held = [h[piece] for piece in group]
        loads = request(loads_at[at])
        if at + 1 < len(groups):
            sums, arena = expand(held, arena, slots, sums, both, False, *loads)
        else:
            (kept, gone), arena = expand(held, arena, slots, sums[:1], both[:1], True, *loads)
            next_input = finish(kept, gone, section_input[0], 1)
            (kept, gone), arena = expand(held, arena, slots, sums[1:], both[1:], True, *request([]))
            prev_grad = finish(kept, gone, out_grad[0], -1)
    return (next_input[None], prev_grad[None])


def solution(mesh):
    return jax.shard_map(
        local,
        mesh=mesh,
        in_specs=(
            P("pipe", "tx", "ty"),
            P("pipe", "tx", "ty"),
            P("pipe", "tx", "ty"),
            P("pipe", "ty", "tx"),
            P("pipe", "ty", "tx"),
            P("pipe", "tx", "ty"),
        ),
        out_specs=(P("pipe", "tx", "ty"), P("pipe", "tx", "ty")),
        check_vma=False,
    )
```

time: 370 us -> 168 us (0.45)
  waiting for transfers between devices: 182 us -> 30.4 us
  matrix products: 119 us -> 0 us
  Pallas kernels: 0 us -> 101 us
  blocking collectives: 46.1 us -> 0 us
  starting transfers between devices: 2.17 us -> 23.1 us
  between operations: 14.8 us -> 0.93 us
  local copies, waits for them, and re-layouts: 3.8 us -> 9.04 us
    psum x1 -> x0, waiting for transfers between devices: 136 us -> none  [local(): lax.psum((partials[0], partials[1], partials[2], partials[3], partials[4]...]
    dot_general x8 -> x0, matrix products: 119 us -> none  [the longest x1 15.7 us: local(): lax.dot_general(grads, wdown, dims, preferred_element_type=jnp.float32)]
    pallas_call x0 -> x17, Pallas kernels: none -> 101 us  [call(): pl.pallas_call(body, in_specs=specs, out_specs=[VM] * (len(shapes) + 1),...]
    all_gather x3 -> x0, blocking collectives: 46.1 us -> none  [the longest x1 16.2 us: local(): lax.all_gather(saved_input[0], 'tx', axis=0, tiled=True)]
    unnamed x3 -> x0, waiting for transfers between devices: 42.7 us -> none
    ppermute x2 -> x21, waiting for transfers between devices: 3.71 us -> 30.4 us  [the longest x4 18.8 us: to_chip(): lax.ppermute(value, 'ty', [(i, (i + 2 * k) % count) for i in range(count)])]
    ppermute x2 -> x21, starting transfers between devices: 2.09 us -> 23.1 us  [the longest x13 10.3 us: swap(): lax.ppermute(value, axis, [(i, i ^ bit) for i in range(lax.axis_size(axis...]
    unnamed x22 -> x42, local copies, waits for them, and re-layouts: 3.8 us -> 8.38 us
  transfers between devices with their start and end apart: 4 -> 21, of which waited for: 4 -> 5; matrix products, arithmetic and copies ran while one was open for 0% -> 1% of each run, Pallas kernels for 0% -> 46%
where the time goes in v1:
time: 168 us
  Pallas kernels  101 us (60%)
  waiting for transfers between devices  30.4 us (18%)
  starting transfers between devices  23.1 us (14%)
  local copies, waits for them, and re-layouts  9.04 us (5%)
  other arithmetic  3.22 us (2%)
    pallas_call x17, Pallas kernels, call(): pl.pallas_call(body, in_specs=specs, out_specs=[VM] * (len(shapes) + 1),...  101 us
    ppermute x4, waiting for transfers between devices, to_chip(): lax.ppermute(value, 'ty', [(i, (i + 2 * k) % count) for i in range(count)])  18.8 us
    ppermute x13, starting transfers between devices, swap(): lax.ppermute(value, axis, [(i, i ^ bit) for i in range(lax.axis_size(axis...  10.3 us
    ppermute x4, starting transfers between devices, cross_pipe(): return lax.ppermute(value, ('pipe', 'tx'), pairs)  8.69 us
    unnamed x42, local copies, waits for them, and re-layouts  8.38 us
    ppermute x13, waiting for transfers between devices, swap(): lax.ppermute(value, axis, [(i, i ^ bit) for i in range(lax.axis_size(axis...  7.67 us
    ppermute x4, starting transfers between devices, to_chip(): lax.ppermute(value, 'ty', [(i, (i + 2 * k) % count) for i in range(count)])  4.05 us
    ppermute x4, waiting for transfers between devices, cross_pipe(): return lax.ppermute(value, ('pipe', 'tx'), pairs)  3.94 us
  transfers between devices with their start and end apart: 21, of which 5 were waited for; matrix products, arithmetic and copies ran while one was open for 1% of the time, Pallas kernels for 46%

profile of v1, /device:TPU:0, one launch (start us, length us, event | category | flops | bytes accessed | tf_op | source)
XLA Modules:
  0.0 167.5 jit_solution(9431120556917228137)
XLA Ops:
  1.6 4.1 %collective-permute-start = (bf16[48,2048]{1,0:T(8,128)(2,1)S(1)}, bf16[48,2048]{1,0:T(8,128)(2,1)S(1)}, u32[]{:S(2)}, u32[]{:S(2)}) collective-permute-start(bf16[48,2048]{1,0:T(8,128)(2,1)S(1)} %fusion.5.refs_0_), channel_id=1, source_target_pairs={{0,8},{4,12},{8,0},{12,4},{1,9},{5,13},{9,1},{13,5},{2,10},{6,14},... | collective-permute-start | bytes 589832 | tf_op jit(solution)/shard_map/ppermute | solution.py:226
  7.2 7.6 %collective-permute-done.refs_1_ = bf16[48,2048]{1,0:T(8,128)(2,1)S(1)} collective-permute-done((bf16[48,2048]{1,0:T(8,128)(2,1)S(1)}, bf16[48,2048]{1,0:T(8,128)(2,1)S(1)}, u32[]{:S(2)}, u32[]{:S(2)}) %collective-permute-start) | collective-permute-done | bytes 196640 | tf_op jit(solution)/shard_map/ppermute | solution.py:226
  16.1 18.0 %shard_map.77.refs_5_ = bf16[14544,2048]{1,0:T(8,128)(2,1)S(1)} custom-call(s32[10]{0:T(128)} %stack.43.refs_0_.refs_4_.refs_1_.refs_2_.refs_3_, bf16[7392,2048]{1,0:T(8,128)(2,1)} %bitcast.26, bf16[7392,2048]{1,0:T(8,128)(2,1)} %bitcast.33, bf16[7392,2048]{1,0:T(8,128)(2,1)} %bitcast.40), custom_call_target="tpu_custom_call" | custom-call | bytes 56623104 | tf_op jit(solution)/shard_map/pallas_call | solution.py:79
  37.1 4.9 %shard_map.79 = (f32[240,896]{1,0:T(8,128)}, bf16[14544,2048]{1,0:T(8,128)(2,1)S(1)}) custom-call(s32[10]{0:T(128)} %stack.43.refs_0_.refs_4_.refs_1_.refs_2_.refs_3_, bf16[14544,2048]{1,0:T(8,128)(2,1)S(1)} %shard_map.78.refs_1_), custom_call_target="tpu_custom_call", output_to_operand_aliasing={{1}: (1, {})} | custom-call | flops 880803840 | tf_op jit(solution)/shard_map/pallas_call | solution.py:79
  42.1 6.1 %shard_map.80 = (f32[240,960]{1,0:T(8,128)}, bf16[14544,2048]{1,0:T(8,128)(2,1)S(1)}) custom-call(s32[10]{0:T(128)} %stack.43.refs_0_.refs_4_.refs_1_.refs_2_.refs_3_, bf16[7392,2048]{1,0:T(8,128)(2,1)} %bitcast.27, bf16[7392,2048]{1,0:T(8,128)(2,1)} %bitcast.34, bf16[7392,2048]{1,0:T(8,128)(2,1)} %bitcast.41, ...), custom_call_target="tpu_custom_call", output_to_operand_aliasing={{1}: (4, {})} | custom-call | flops 943718400 | bytes 11796480 | tf_op jit(solution)/shard_map/pallas_call | solution.py:79
  49.7 6.2 %shard_map.81 = (bf16[240,896]{1,0:T(8,128)(2,1)}, bf16[14544,2048]{1,0:T(8,128)(2,1)S(1)}) custom-call(f32[240,896]{1,0:T(8,128)} %copy-done.5, s32[10]{0:T(128)} %stack.43.refs_0_.refs_4_.refs_1_.refs_2_.refs_3_, bf16[7392,2048]{1,0:T(8,128)(2,1)} %bitcast.28, bf16[7392,2048]{1,0:T(8,128)(2,1)} %bitcast.35, ...), custom_call_target="tpu_custom_call", output_to_operand_aliasing={{1}: (5, {})} | custom-call | flops 880803840 | bytes 11010048 | tf_op jit(solution)/shard_map/pallas_call | solution.py:79
  56.9 6.5 %shard_map.82 = (bf16[240,960]{1,0:T(8,128)(2,1)}, bf16[14544,2048]{1,0:T(8,128)(2,1)S(1)}) custom-call(f32[240,960]{1,0:T(8,128)} %copy-done.3, s32[10]{0:T(128)} %stack.43.refs_0_.refs_4_.refs_1_.refs_2_.refs_3_, bf16[7392,2048]{1,0:T(8,128)(2,1)} %bitcast.29, bf16[7392,2048]{1,0:T(8,128)(2,1)} %bitcast.36, ...), custom_call_target="tpu_custom_call", output_to_operand_aliasing={{1}: (5, {})} | custom-call | flops 943718400 | bytes 11796480 | tf_op jit(solution)/shard_map/pallas_call | solution.py:79
  63.4 5.8 %shard_map.83 = (f32[240,896]{1,0:T(8,128)}, bf16[14544,2048]{1,0:T(8,128)(2,1)S(1)}) custom-call(s32[10]{0:T(128)} %stack.43.refs_0_.refs_4_.refs_1_.refs_2_.refs_3_, bf16[7392,2048]{1,0:T(8,128)(2,1)} %bitcast.30, bf16[7392,2048]{1,0:T(8,128)(2,1)} %bitcast.37, bf16[7392,2048]{1,0:T(8,128)(2,1)} %bitcast.44, ...), custom_call_target="tpu_custom_call", output_to_operand_aliasing={{1}: (4, {})} | custom-call | flops 880803840 | bytes 11010048 | tf_op jit(solution)/shard_map/pallas_call | solution.py:79
  69.3 5.5 %shard_map.84 = (f32[240,960]{1,0:T(8,128)}, bf16[14544,2048]{1,0:T(8,128)(2,1)S(1)}) custom-call(s32[10]{0:T(128)} %stack.43.refs_0_.refs_4_.refs_1_.refs_2_.refs_3_, bf16[14544,2048]{1,0:T(8,128)(2,1)S(1)} %get-tuple-element.43.refs_1_), custom_call_target="tpu_custom_call", output_to_operand_aliasing={{1}: (1, {})} | custom-call | flops 943718400 | tf_op jit(solution)/shard_map/pallas_call | solution.py:79
  78.1 5.4 %shard_map.85 = (f32[240,896]{1,0:T(8,128)}, bf16[14544,2048]{1,0:T(8,128)(2,1)S(1)}) custom-call(f32[240,896]{1,0:T(8,128)} %copy-done.4, s32[10]{0:T(128)} %stack.43.refs_0_.refs_4_.refs_1_.refs_2_.refs_3_, bf16[14544,2048]{1,0:T(8,128)(2,1)S(1)} %get-tuple-element.44.refs_2_), custom_call_target="tpu_custom_call", output_to_operand_aliasing={{1}: (2, {})} | custom-call | flops 880803840 | tf_op jit(solution)/shard_map/pallas_call | solution.py:79
  84.5 5.7 %shard_map.86 = (f32[240,960]{1,0:T(8,128)}, bf16[14544,2048]{1,0:T(8,128)(2,1)S(1)}) custom-call(f32[240,960]{1,0:T(8,128)} %copy-done.2, s32[10]{0:T(128)} %stack.43.refs_0_.refs_4_.refs_1_.refs_2_.refs_3_, bf16[14544,2048]{1,0:T(8,128)(2,1)S(1)} %get-tuple-element.48.refs_2_), custom_call_target="tpu_custom_call", output_to_operand_aliasing={{1}: (2, {})} | custom-call | flops 943718400 | tf_op jit(solution)/shard_map/pallas_call | solution.py:79
  90.2 7.4 %collective-permute-done.6.refs_1_ = bf16[240,896]{1,0:T(8,128)(2,1)S(1)} collective-permute-done((bf16[240,896]{1,0:T(8,128)(2,1)}, bf16[240,896]{1,0:T(8,128)(2,1)S(1)}, u32[]{:S(2)}, u32[]{:S(2)}) %collective-permute-start.6) | collective-permute-done | bytes 430112 | tf_op jit(solution)/shard_map/ppermute | solution.py:231
  98.4 2.1 %shard_map.87 = (bf16[144,896]{1,0:T(8,128)(2,1)}, bf16[14544,2048]{1,0:T(8,128)(2,1)S(1)}) custom-call(f32[240,896]{1,0:T(8,128)} %get-tuple-element.45.refs_0_, bf16[240,896]{1,0:T(8,128)(2,1)} %copy-done.8, s32[10]{0:T(128)} %stack.43.refs_0_.refs_4_.refs_1_.refs_2_.refs_3_, ...), custom_call_target="tpu_custom_call", output_to_operand_aliasing={{1}: (3, {})} | custom-call | flops 4300800 | tf_op jit(solution)/shard_map/pallas_call | solution.py:79
  101.3 2.3 %shard_map.88 = (bf16[144,960]{1,0:T(8,128)(2,1)}, bf16[14544,2048]{1,0:T(8,128)(2,1)S(1)}) custom-call(f32[240,960]{1,0:T(8,128)} %get-tuple-element.51.refs_0_, bf16[240,960]{1,0:T(8,128)(2,1)} %copy-done.7, s32[10]{0:T(128)} %stack.43.refs_0_.refs_4_.refs_1_.refs_2_.refs_3_, ...), custom_call_target="tpu_custom_call", output_to_operand_aliasing={{1}: (3, {})} | custom-call | flops 4608000 | tf_op jit(solution)/shard_map/pallas_call | solution.py:79
  106.1 11.4 %collective-permute-done.8.refs_0_ = bf16[144,896]{1,0:T(8,128)(2,1)S(1)} collective-permute-done((bf16[144,896]{1,0:T(8,128)(2,1)S(1)}, bf16[144,896]{1,0:T(8,128)(2,1)S(1)}, u32[]{:S(2)}, u32[]{:S(2)}) %collective-permute-start.8) | collective-permute-done | bytes 258080 | tf_op jit(solution)/shard_map/ppermute | solution.py:231
  118.1 5.9 %shard_map.89 = (f32[48,2048]{1,0:T(8,128)}, f32[48,2048]{1,0:T(8,128)}, bf16[14544,2048]{1,0:T(8,128)(2,1)S(1)}) custom-call(bf16[144,896]{1,0:T(8,128)(2,1)} %get-tuple-element.50.refs_0_, bf16[144,960]{1,0:T(8,128)(2,1)} %get-tuple-element.54.refs_1_, s32[10]{0:T(128)} %stack.43.refs_0_.refs_4_.refs_1_.refs_2_.refs_3_, ...), custom_call_target="tpu_custom_call", output_to_operand_aliasing={{2}: (3, {})} | custom-call | flops 1094713344 | tf_op jit(solution)/shard_map/pallas_call | solution.py:79
  124.9 9.9 %shard_map.90 = (f32[48,2048]{1,0:T(8,128)}, f32[48,2048]{1,0:T(8,128)}, bf16[14544,2048]{1,0:T(8,128)(2,1)S(1)}) custom-call(bf16[144,896]{1,0:T(8,128)(2,1)} %copy-done.15, bf16[144,960]{1,0:T(8,128)(2,1)} %copy-done.10, f32[48,2048]{1,0:T(8,128)} %get-tuple-element.56.refs_2_, ...), custom_call_target="tpu_custom_call", output_to_operand_aliasing={{2}: (8, {})} | custom-call | flops 1094713344 | bytes 22806528 | tf_op jit(solution)/shard_map/pallas_call | solution.py:79
  134.8 6.7 %shard_map.91 = (f32[48,2048]{1,0:T(8,128)}, f32[48,2048]{1,0:T(8,128)}, bf16[14544,2048]{1,0:T(8,128)(2,1)S(1)}) custom-call(bf16[144,896]{1,0:T(8,128)(2,1)} %copy-done.13, bf16[144,960]{1,0:T(8,128)(2,1)} %copy-done.9, f32[48,2048]{1,0:T(8,128)} %get-tuple-element.59.refs_2_, ...), custom_call_target="tpu_custom_call", output_to_operand_aliasing={{2}: (8, {})} | custom-call | flops 1094713344 | bytes 11796480 | tf_op jit(solution)/shard_map/pallas_call | solution.py:79
  142.3 3.4 %shard_map.92 = (f32[24,2048]{1,0:T(8,128)}, bf16[24,2048]{1,0:T(8,128)(2,1)}, bf16[14544,2048]{1,0:T(8,128)(2,1)S(1)}) custom-call(bf16[144,896]{1,0:T(8,128)(2,1)} %copy-done.1, bf16[144,960]{1,0:T(8,128)(2,1)} %copy-done, f32[48,2048]{1,0:T(8,128)} %get-tuple-element.62.refs_2_, ...), custom_call_target="tpu_custom_call", output_to_operand_aliasing={{2}: (4, {})} | custom-call | flops 364904448 | tf_op jit(solution)/shard_map/pallas_call | solution.py:79
  147.2 4.7 %shard_map.93 = (f32[24,2048]{1,0:T(8,128)}, bf16[24,2048]{1,0:T(8,128)(2,1)}, bf16[14544,2048]{1,0:T(8,128)(2,1)S(1)}) custom-call(bf16[144,896]{1,0:T(8,128)(2,1)} %copy-done.1, bf16[144,960]{1,0:T(8,128)(2,1)} %copy-done, f32[48,2048]{1,0:T(8,128)} %get-tuple-element.66.refs_2_, ...), custom_call_target="tpu_custom_call", output_to_operand_aliasing={{2}: (4, {})} | custom-call | flops 364904448 | tf_op jit(solution)/shard_map/pallas_call | solution.py:79
  152.6 4.4 %collective-permute-start.17 = (bf16[12,2048]{1,0:T(8,128)(2,1)S(1)}, bf16[12,2048]{1,0:T(8,128)(2,1)S(1)}, u32[]{:S(2)}, u32[]{:S(2)}) collective-permute-start(bf16[12,2048]{1,0:T(8,128)(2,1)S(1)} %slice.27), channel_id=1, source_target_pairs={{0,24},{4,28},{8,16},{12,20},{16,8},{20,12},{24,0},{28,4},{1,25},{... | collective-permute-start | bytes 147464 | tf_op jit(solution)/shard_map/ppermute | solution.py:241
  158.5 3.4 %collective-permute-start.20 = (bf16[12,2048]{1,0:T(8,128)(2,1)S(1)}, bf16[12,2048]{1,0:T(8,128)(2,1)S(1)}, u32[]{:S(2)}, u32[]{:S(2)}) collective-permute-start(bf16[12,2048]{1,0:T(8,128)(2,1)S(1)} %slice.26), channel_id=1, source_target_pairs={{0,24},{4,28},{8,16},{12,20},{16,8},{20,12},{24,0},{28,4},{1,25},{... | collective-permute-start | bytes 147464 | tf_op jit(solution)/shard_map/ppermute | solution.py:241
  162.9 1.9 %collective-permute-done.20 = bf16[12,2048]{1,0:T(8,128)(2,1)S(1)} collective-permute-done((bf16[12,2048]{1,0:T(8,128)(2,1)S(1)}, bf16[12,2048]{1,0:T(8,128)(2,1)S(1)}, u32[]{:S(2)}, u32[]{:S(2)}) %collective-permute-start.20) | collective-permute-done | bytes 49184 | tf_op jit(solution)/shard_map/ppermute | solution.py:241
  164.8 2.0 %collective-permute-done.19 = f32[12,2048]{1,0:T(8,128)S(1)} collective-permute-done((f32[12,2048]{1,0:T(8,128)S(1)}, f32[12,2048]{1,0:T(8,128)S(1)}, u32[]{:S(2)}, u32[]{:S(2)}) %collective-permute-start.19) | collective-permute-done | bytes 98336 | tf_op jit(solution)/shard_map/ppermute | solution.py:241
  (87 shorter events, 25.1 us)
Async XLA Ops:
  1.6 32.6 %copy-start.6 = (bf16[48,2048]{1,0:T(8,128)(2,1)}, bf16[48,2048]{1,0:T(8,128)(2,1)S(1)}, u32[]{:S(2)}) copy-start(bf16[48,2048]{1,0:T(8,128)(2,1)S(1)} %fusion.5.refs_0_) | copy-start | bytes 589828
  1.6 13.3 %collective-permute-start = (bf16[48,2048]{1,0:T(8,128)(2,1)S(1)}, bf16[48,2048]{1,0:T(8,128)(2,1)S(1)}, u32[]{:S(2)}, u32[]{:S(2)}) collective-permute-start(bf16[48,2048]{1,0:T(8,128)(2,1)S(1)} %fusion.5.refs_0_), channel_id=1, source_target_pairs={{0,8},{4,12},{8,0},{12,4},{1,9},{5,13},{9,1},{13,5},{2,10},{6,14},... | collective-permute-start | bytes 589832 | tf_op jit(solution)/shard_map/ppermute | solution.py:226
  5.7 28.5 %collective-permute-start.1 = (bf16[48,2048]{1,0:T(8,128)(2,1)S(1)}, bf16[48,2048]{1,0:T(8,128)(2,1)S(1)}, u32[]{:S(2)}, u32[]{:S(2)}) collective-permute-start(bf16[48,2048]{1,0:T(8,128)(2,1)S(1)} %fusion.5.refs_0_), channel_id=1, source_target_pairs={{0,4},{4,0},{8,12},{12,8},{1,5},{5,1},{9,13},{13,9},{2,6},{6,2},{1... | collective-permute-start | bytes 589832 | tf_op jit(solution)/shard_map/ppermute | solution.py:226
  14.9 19.3 %copy-start.16 = (bf16[48,2048]{1,0:T(8,128)(2,1)}, bf16[48,2048]{1,0:T(8,128)(2,1)S(1)}, u32[]{:S(2)}) copy-start(bf16[48,2048]{1,0:T(8,128)(2,1)S(1)} %collective-permute-done.refs_1_) | copy-start | bytes 589828
  14.9 19.3 %collective-permute-start.2 = (bf16[48,2048]{1,0:T(8,128)(2,1)S(1)}, bf16[48,2048]{1,0:T(8,128)(2,1)S(1)}, u32[]{:S(2)}, u32[]{:S(2)}) collective-permute-start(bf16[48,2048]{1,0:T(8,128)(2,1)S(1)} %collective-permute-done.refs_1_), channel_id=1, source_target_pairs={{0,4},{4,0},{8,12},{12,8},{1,5},{5,1},{9,13},{13,9},{2,6},{6,2},{1... | collective-permute-start | bytes 589832 | tf_op jit(solution)/shard_map/ppermute | solution.py:226
  42.1 6.7 %collective-permute-start.4 = (f32[240,896]{1,0:T(8,128)}, f32[240,896]{1,0:T(8,128)S(1)}, u32[]{:S(2)}, u32[]{:S(2)}) collective-permute-start(f32[240,896]{1,0:T(8,128)} %get-tuple-element.38), channel_id=1, source_target_pairs={{0,1},{1,0},{2,3},{3,2},{4,5},{5,4},{6,7},{7,6},{8,9},{9,8},{10,11... | collective-permute-start | bytes 2580488 | tf_op jit(solution)/shard_map/ppermute | solution.py:226
  48.2 7.7 %collective-permute-start.3 = (f32[240,960]{1,0:T(8,128)}, f32[240,960]{1,0:T(8,128)S(1)}, u32[]{:S(2)}, u32[]{:S(2)}) collective-permute-start(f32[240,960]{1,0:T(8,128)} %get-tuple-element.37), channel_id=1, source_target_pairs={{0,1},{1,0},{2,3},{3,2},{4,5},{5,4},{6,7},{7,6},{8,9},{9,8},{10,11... | collective-permute-start | bytes 2764808 | tf_op jit(solution)/shard_map/ppermute | solution.py:226
  69.2 8.0 %collective-permute-start.5 = (f32[240,896]{1,0:T(8,128)}, f32[240,896]{1,0:T(8,128)S(1)}, u32[]{:S(2)}, u32[]{:S(2)}) collective-permute-start(f32[240,896]{1,0:T(8,128)} %get-tuple-element.42), channel_id=1, source_target_pairs={{0,1},{1,0},{2,3},{3,2},{4,5},{5,4},{6,7},{7,6},{8,9},{9,8},{10,11... | collective-permute-start | bytes 2580488 | tf_op jit(solution)/shard_map/ppermute | solution.py:226
  74.7 8.7 %collective-permute-start.7 = (f32[240,960]{1,0:T(8,128)}, f32[240,960]{1,0:T(8,128)S(1)}, u32[]{:S(2)}, u32[]{:S(2)}) collective-permute-start(f32[240,960]{1,0:T(8,128)} %get-tuple-element.47), channel_id=1, source_target_pairs={{0,1},{1,0},{2,3},{3,2},{4,5},{5,4},{6,7},{7,6},{8,9},{9,8},{10,11... | collective-permute-start | bytes 2764808 | tf_op jit(solution)/shard_map/ppermute | solution.py:226
  75.1 25.4 %collective-permute-start.10 = (bf16[240,960]{1,0:T(8,128)(2,1)S(1)}, bf16[240,960]{1,0:T(8,128)(2,1)S(1)}, u32[]{:S(2)}, u32[]{:S(2)}) collective-permute-start(bf16[240,960]{1,0:T(8,128)(2,1)S(1)} %copy-done.20), channel_id=1, source_target_pairs={{0,2},{1,3},{2,0},{3,1},{4,6},{5,7},{6,4},{7,5},{8,10},{9,11},{10,... | collective-permute-start | bytes 1382408 | tf_op jit(solution)/shard_map/ppermute | solution.py:231
  76.6 21.0 %collective-permute-start.6 = (bf16[240,896]{1,0:T(8,128)(2,1)}, bf16[240,896]{1,0:T(8,128)(2,1)S(1)}, u32[]{:S(2)}, u32[]{:S(2)}) collective-permute-start(bf16[240,896]{1,0:T(8,128)(2,1)} %get-tuple-element.46), channel_id=1, source_target_pairs={{0,2},{1,3},{2,0},{3,1},{4,6},{5,7},{6,4},{7,5},{8,10},{9,11},{10,... | collective-permute-start | bytes 1290248 | tf_op jit(solution)/shard_map/ppermute | solution.py:231
  103.6 14.0 %collective-permute-start.11 = (bf16[144,960]{1,0:T(8,128)(2,1)}, bf16[144,960]{1,0:T(8,128)(2,1)S(1)}, u32[]{:S(2)}, u32[]{:S(2)}) collective-permute-start(bf16[144,960]{1,0:T(8,128)(2,1)} %get-tuple-element.54.refs_1_), channel_id=1, source_target_pairs={{0,2},{1,3},{2,0},{3,1},{4,6},{5,7},{6,4},{7,5},{8,10},{9,11},{10,... | collective-permute-start | bytes 829448 | tf_op jit(solution)/shard_map/ppermute | solution.py:231
  105.1 12.5 %collective-permute-start.8 = (bf16[144,896]{1,0:T(8,128)(2,1)S(1)}, bf16[144,896]{1,0:T(8,128)(2,1)S(1)}, u32[]{:S(2)}, u32[]{:S(2)}) collective-permute-start(bf16[144,896]{1,0:T(8,128)(2,1)S(1)} %copy-done.14), channel_id=1, source_target_pairs={{0,2},{1,3},{2,0},{3,1},{4,6},{5,7},{6,4},{7,5},{8,10},{9,11},{10,... | collective-permute-start | bytes 774152 | tf_op jit(solution)/shard_map/ppermute | solution.py:231
  105.6 18.4 %collective-permute-start.14 = (bf16[144,960]{1,0:T(8,128)(2,1)}, bf16[144,960]{1,0:T(8,128)(2,1)S(1)}, u32[]{:S(2)}, u32[]{:S(2)}) collective-permute-start(bf16[144,960]{1,0:T(8,128)(2,1)} %get-tuple-element.54.refs_1_), channel_id=1, source_target_pairs={{0,1},{1,0},{2,3},{3,2},{4,5},{5,4},{6,7},{7,6},{8,9},{9,8},{10,11... | collective-permute-start | bytes 829448 | tf_op jit(solution)/shard_map/ppermute | solution.py:226
  105.6 18.4 %collective-permute-start.13 = (bf16[144,896]{1,0:T(8,128)(2,1)S(1)}, bf16[144,896]{1,0:T(8,128)(2,1)S(1)}, u32[]{:S(2)}, u32[]{:S(2)}) collective-permute-start(bf16[144,896]{1,0:T(8,128)(2,1)S(1)} %copy-done.14), channel_id=1, source_target_pairs={{0,1},{1,0},{2,3},{3,2},{4,5},{5,4},{6,7},{7,6},{8,9},{9,8},{10,11... | collective-permute-start | bytes 774152 | tf_op jit(solution)/shard_map/ppermute | solution.py:226
  117.5 17.2 %copy-start.13 = (bf16[144,896]{1,0:T(8,128)(2,1)}, bf16[144,896]{1,0:T(8,128)(2,1)S(1)}, u32[]{:S(2)}) copy-start(bf16[144,896]{1,0:T(8,128)(2,1)S(1)} %collective-permute-done.8.refs_0_) | copy-start | bytes 774148
  117.5 24.0 %collective-permute-start.9 = (bf16[144,896]{1,0:T(8,128)(2,1)S(1)}, bf16[144,896]{1,0:T(8,128)(2,1)S(1)}, u32[]{:S(2)}, u32[]{:S(2)}) collective-permute-start(bf16[144,896]{1,0:T(8,128)(2,1)S(1)} %collective-permute-done.8.refs_0_), channel_id=1, source_target_pairs={{0,1},{1,0},{2,3},{3,2},{4,5},{5,4},{6,7},{7,6},{8,9},{9,8},{10,11... | collective-permute-start | bytes 774152 | tf_op jit(solution)/shard_map/ppermute | solution.py:226
  117.6 24.0 %collective-permute-start.12 = (bf16[144,960]{1,0:T(8,128)(2,1)S(1)}, bf16[144,960]{1,0:T(8,128)(2,1)S(1)}, u32[]{:S(2)}, u32[]{:S(2)}) collective-permute-start(bf16[144,960]{1,0:T(8,128)(2,1)S(1)} %collective-permute-done.11.refs_1_), channel_id=1, source_target_pairs={{0,1},{1,0},{2,3},{3,2},{4,5},{5,4},{6,7},{7,6},{8,9},{9,8},{10,11... | collective-permute-start | bytes 829448 | tf_op jit(solution)/shard_map/ppermute | solution.py:226
  145.8 6.8 %collective-permute-start.15 = (bf16[24,2048]{1,0:T(8,128)(2,1)}, bf16[24,2048]{1,0:T(8,128)(2,1)S(1)}, u32[]{:S(2)}, u32[]{:S(2)}) collective-permute-start(bf16[24,2048]{1,0:T(8,128)(2,1)} %get-tuple-element.65), channel_id=1, source_target_pairs={{0,4},{4,0},{8,12},{12,8},{1,5},{5,1},{9,13},{13,9},{2,6},{6,2},{1... | collective-permute-start | bytes 294920 | tf_op jit(solution)/shard_map/ppermute | solution.py:226
  151.9 5.6 %collective-permute-start.18 = (bf16[24,2048]{1,0:T(8,128)(2,1)}, bf16[24,2048]{1,0:T(8,128)(2,1)S(1)}, u32[]{:S(2)}, u32[]{:S(2)}) collective-permute-start(bf16[24,2048]{1,0:T(8,128)(2,1)} %get-tuple-element.69), channel_id=1, source_target_pairs={{0,4},{4,0},{8,12},{12,8},{1,5},{5,1},{9,13},{13,9},{2,6},{6,2},{1... | collective-permute-start | bytes 294920 | tf_op jit(solution)/shard_map/ppermute | solution.py:226
  152.6 9.7 %collective-permute-start.17 = (bf16[12,2048]{1,0:T(8,128)(2,1)S(1)}, bf16[12,2048]{1,0:T(8,128)(2,1)S(1)}, u32[]{:S(2)}, u32[]{:S(2)}) collective-permute-start(bf16[12,2048]{1,0:T(8,128)(2,1)S(1)} %slice.27), channel_id=1, source_target_pairs={{0,24},{4,28},{8,16},{12,20},{16,8},{20,12},{24,0},{28,4},{1,25},{... | collective-permute-start | bytes 147464 | tf_op jit(solution)/shard_map/ppermute | solution.py:241
  157.0 5.3 %collective-permute-start.16 = (f32[12,2048]{1,0:T(8,128)S(1)}, f32[12,2048]{1,0:T(8,128)S(1)}, u32[]{:S(2)}, u32[]{:S(2)}) collective-permute-start(f32[12,2048]{1,0:T(8,128)S(1)} %slice_add_fusion.1), channel_id=1, source_target_pairs={{0,16},{4,20},{8,24},{12,28},{16,0},{20,4},{24,8},{28,12},{1,17},{... | collective-permute-start | bytes 294920 | tf_op jit(solution)/shard_map/ppermute | solution.py:241
  158.5 6.3 %collective-permute-start.20 = (bf16[12,2048]{1,0:T(8,128)(2,1)S(1)}, bf16[12,2048]{1,0:T(8,128)(2,1)S(1)}, u32[]{:S(2)}, u32[]{:S(2)}) collective-permute-start(bf16[12,2048]{1,0:T(8,128)(2,1)S(1)} %slice.26), channel_id=1, source_target_pairs={{0,24},{4,28},{8,16},{12,20},{16,8},{20,12},{24,0},{28,4},{1,25},{... | collective-permute-start | bytes 147464 | tf_op jit(solution)/shard_map/ppermute | solution.py:241
  161.9 5.0 %collective-permute-start.19 = (f32[12,2048]{1,0:T(8,128)S(1)}, f32[12,2048]{1,0:T(8,128)S(1)}, u32[]{:S(2)}, u32[]{:S(2)}) collective-permute-start(f32[12,2048]{1,0:T(8,128)S(1)} %slice_add_fusion), channel_id=1, source_target_pairs={{0,16},{4,20},{8,24},{12,28},{16,0},{20,4},{24,8},{28,12},{1,17},{... | collective-permute-start | bytes 294920 | tf_op jit(solution)/shard_map/ppermute | solution.py:241
  (18 other events, 70.6 us)

commit v2 on v0

v2 whole, which is shorter than its diff:
```python
import functools

import jax
import jax.numpy as jnp
from jax import lax
from jax.experimental import pallas as pl
from jax.experimental.pallas import tpu as pltpu
from jax.sharding import PartitionSpec as P

F32 = jnp.float32
BF16 = jnp.bfloat16
NN = (((1,), (0,)), ((), ()))
NT = (((1,), (1,)), ((), ()))
VM = pl.BlockSpec(memory_space=pltpu.VMEM)
HBM = pl.BlockSpec(memory_space=pltpu.HBM)
SM = pl.BlockSpec(memory_space=pltpu.SMEM)
STEP = 512
SLOTS = 5
SPLIT = (2, 2, 1)
HINT = 2 * 10**9


def contract(a, b, dims):
    return lax.dot_general(a, b, dims, preferred_element_type=F32)


def params():
    return pltpu.CompilerParams(vmem_limit_bytes=62 * 2**20 // 10)


def spans(size, step=STEP):
    return [(at, min(step, size - at)) for at in range(0, size, step)]


def up_to(value, unit):
    return -(-value // unit) * unit


def fetches(table_ref, stored, arena, loads, sems):
    copies = []
    for n, (at, rows, entry, _) in enumerate(loads):
        start = pl.multiple_of(table_ref[entry], 16)
        for i, source in enumerate(stored):
            target = arena.at[pl.ds(at + i * rows, rows), :]
            copies.append(pltpu.make_async_copy(source.at[pl.ds(start, rows), :], target, sems.at[n, i]))
    return copies


def begin(copies):
    for copy in copies:
        copy.start()


def end(copies):
    for copy in copies:
        copy.wait()


def call(body, operands, shapes, scratch, arena, loads, table, stored, spec=HBM, weight=1):
    operands, specs = [*operands, table], [spec] * len(operands) + [SM]
    aliases, scratch = {}, list(scratch)
    if loads:
        operands += stored
        specs += [HBM] * 3
        scratch.append(pltpu.SemaphoreType.DMA((len(loads), 3)))
    held = []
    if isinstance(arena, tuple):
        held = [pltpu.VMEM(arena, BF16)]
    elif arena is not None:
        held = [pltpu.VMEM(arena.shape, BF16)]
        aliases = {len(operands): len(shapes)}
        operands.append(arena)
        specs.append(VM)
    return pl.pallas_call(
        functools.partial(body, loads),
        in_specs=specs,
        out_specs=[spec] * len(shapes) + [VM] * len(held),
        out_shape=list(shapes) + held,
        scratch_shapes=scratch,
        input_output_aliases=aliases,
        compiler_params=params(),
        cost_estimate=pl.CostEstimate(flops=weight * HINT, bytes_accessed=0, transcendentals=0),
    )(*operands)


def split(refs, loads, count, outs, carried=True):
    operands, table, refs = refs[:count], refs[count], refs[count + 1 :]
    if loads:
        stored, refs = refs[:3], refs[3:]
    if carried:
        refs = refs[1:]
    results, arena, scratch = refs[:outs], refs[outs], refs[outs + 1 :]
    if carried is None:
        arena, scratch = None, refs[outs:]
    copies = []
    if loads:
        copies, scratch = fetches(table, stored, arena, loads, scratch[-1]), scratch[:-1]
    return operands, table, results, arena, scratch, copies


def load_body(carried, loads, *refs):
    copies = split(refs, loads, 0, 0, carried)[-1]
    begin(copies)
    end(copies)


def load(arena, loads, table, stored):
    carried = not isinstance(arena, tuple)
    return call(functools.partial(load_body, carried), [], [], [], arena, loads, table, stored)[0]


def products(arena, h_refs, slots, part, tokens, piece):
    value = 0.0
    for h_ref, (at, rows) in zip(h_refs, slots):
        for i in (1, 2) if part else (0,):
            lhs = h_ref[pl.ds(i * tokens, tokens), :]
            value = value + contract(lhs, arena[pl.ds(at + (i + 2) % 3 * rows, rows), piece], NN)
    return value


def sum_rows(arena, part, tokens):
    low = arena.shape[0] - 4 * tokens + 2 * part * tokens
    return pl.ds(low, tokens), pl.ds(low + tokens, tokens)


def keep(arena, value, part, tokens, piece):
    high, low = sum_rows(arena, part, tokens)
    rounded = value.astype(BF16)
    arena[high, piece] = rounded
    arena[low, piece] = (value - rounded.astype(F32)).astype(BF16)


def kept_sum(arena, part, tokens, piece):
    high, low = sum_rows(arena, part, tokens)
    return arena[high, piece].astype(F32) + arena[low, piece].astype(F32)


def project_body(at, rows, got, others, leave, tokens, entry, fresh, loads, *refs):
    outs = 1 if entry is not None else len(leave)
    operands, table, out_refs, arena, scratch, copies = split(refs, loads, len(got) + others, outs)
    part_ref, out_sems = scratch[:2]
    blocks = [pl.ds(0, 2 * tokens), pl.ds(2 * tokens, 2 * tokens), pl.ds(4 * tokens, tokens)]
    arrivals, held = [], scratch[2 : 2 + others + (1 if got else 0)]
    in_sems = scratch[2 + len(held)] if held else None
    targets, low = [], 0
    for count in got:
        targets.append(held[0].at[pl.ds(low, count * tokens), :])
        low += count * tokens
    targets += held[1 if got else 0 :]
    arrivals = [pltpu.make_async_copy(source, targets[i], in_sems.at[i]) for i, source in enumerate(operands)]
    begin(arrivals)
    if not arrivals:
        begin(copies)
    first_ref = scratch[-1] if arrivals and entry is None else part_ref
    h_ref = scratch[-1]
    base = arena.shape[0] - 7 * tokens
    leaving = []

    def finished(part, i, piece):
        for ref in held:
            part = part + ref[blocks[i], piece].astype(F32)
        return part

    def leaves(i):
        if entry is None:
            target = out_refs[0].at[blocks[i], :] if len(out_refs) == 1 else out_refs[i]
            leaving.append(pltpu.make_async_copy(part_ref.at[blocks[i], :], target, out_sems.at[i]))
            leaving[-1].start()

    for i, (first, count) in enumerate(((0, 2), (0, 2), (2, 1))):
        lhs = arena[pl.ds(base + first * tokens, count * tokens), :]
        for low, size in spans(rows):
            piece = pl.ds(low, size)
            part = contract(lhs, arena[pl.ds(at + i * rows + low, size), :], NT)
            if not i and arrivals:
                first_ref[blocks[0], piece] = part
                continue
            if i == 1 and not low and arrivals:
                end(arrivals)
                begin(copies)
            part_ref[blocks[i], piece] = finished(part, i, piece).astype(part_ref.dtype)
            if i == 2 and entry is not None:
                for at_column in range(low, low + size, 128):
                    columns = pl.ds(at_column, min(128, low + size - at_column))
                    gate, saved_gate, up, saved_up, hidden_grad = [
                        part_ref[pl.ds(n * tokens, tokens), columns] for n in range(5)
                    ]
                    mine = lax.broadcasted_iota(jnp.int32, gate.shape, 1) + at_column >= table[entry]
                    hidden = gate * jax.nn.sigmoid(gate) * up
                    sigma = jax.nn.sigmoid(saved_gate)
                    gate_grad = hidden_grad * saved_up * sigma * (1.0 + saved_gate * (1.0 - sigma))
                    up_grad = hidden_grad * saved_gate * sigma
                    for n, value in enumerate((hidden, gate_grad, up_grad)):
                        h_ref[pl.ds(n * tokens, tokens), columns] = jnp.where(mine, value, 0.0).astype(BF16)
        if i == 1 and arrivals:
            for low, size in spans(rows):
                piece = pl.ds(low, size)
                part = finished(first_ref[blocks[0], piece], 0, piece)
                part_ref[blocks[0], piece] = part.astype(part_ref.dtype)
            leaves(0)
        if i or not arrivals:
            leaves(i)
    if entry is not None:
        leaving.append(pltpu.make_async_copy(h_ref, out_refs[0], out_sems.at[0]))
        leaving[-1].start()
        for low, size in spans(arena.shape[1]):
            piece = pl.ds(low, size)
            for part in (0, 1):
                value = products(arena, [h_ref], [(at, rows)], part, tokens, piece)
                if not fresh:
                    value = value + kept_sum(arena, part, tokens, piece)
                keep(arena, value, part, tokens, piece)
    end(leaving)
    end(copies)


def project(tokens, arena, slot, more, others, leave, dtype, entry, fresh, loads, table, stored):
    at, rows = slot
    operands = more + others
    part = jax.ShapeDtypeStruct((5 * tokens, rows), dtype)
    shapes = [jax.ShapeDtypeStruct((count * tokens, rows), dtype) for count in leave]
    if entry is not None:
        shapes = [jax.ShapeDtypeStruct((3 * tokens, rows), BF16)]
    scratch = [pltpu.VMEM(part.shape, dtype), pltpu.SemaphoreType.DMA((3,))]
    scratch += [pltpu.VMEM(part.shape, F32)] * (1 if more else 0)
    scratch += [pltpu.VMEM(operand.shape, operand.dtype) for operand in others]
    if operands:
        scratch.append(pltpu.SemaphoreType.DMA((len(operands),)))
    if entry is not None:
        scratch.append(pltpu.VMEM(shapes[0].shape, BF16))
    elif operands:
        scratch.append(pltpu.VMEM((2 * tokens, rows), F32))
    got = [piece.shape[0] // tokens for piece in more]
    body = functools.partial(project_body, at, rows, got, len(others), leave, tokens, entry, fresh)
    *outs, arena = call(body, operands, shapes, scratch, arena, loads, table, stored, HBM, 1 if entry is None else 2)
    return outs, arena


def expand_body(slots, parts, ends, tokens, loads, *refs):
    operands, _, outs, arena, scratch, copies = split(refs, loads, len(slots), 2 * ends)
    in_sems, out_sems, *held = scratch
    arrivals = [pltpu.make_async_copy(operand, held[i], in_sems.at[i]) for i, operand in enumerate(operands)]
    begin(arrivals)
    total_ref, gone_ref = held[len(slots) :] if ends else (None, None)
    leaving = []
    for n, slot in enumerate(slots):
        if not n:
            end(arrivals)
        for i, copy in enumerate(copies):
            if loads[i // 3][3] == n:
                copy.start()
        for m, (low, size) in enumerate(spans(arena.shape[1])):
            piece = pl.ds(low, size)
            for part in parts:
                value = products(arena, [held[n]], [slot], part, tokens, piece)
                value = value + kept_sum(arena, part, tokens, piece)
                if not ends or n < len(slots) - 1:
                    keep(arena, value, part, tokens, piece)
                    continue
                total_ref[:, piece] = value[: tokens // 2]
                gone_ref[:, piece] = value[tokens // 2 :].astype(BF16)
                for k, source in enumerate((total_ref, gone_ref)):
                    copy = pltpu.make_async_copy(source.at[:, piece], outs[k].at[:, piece], out_sems.at[k, m])
                    leaving.append(copy)
                    copy.start()
    end(leaving)
    end(copies)


def expand(tokens, held, arena, slots, parts, ends, loads, table, stored):
    width = arena.shape[1]
    shapes = []
    scratch = [pltpu.SemaphoreType.DMA((len(held),)), pltpu.SemaphoreType.DMA((2, len(spans(width))))]
    scratch += [pltpu.VMEM(operand.shape, operand.dtype) for operand in held]
    if ends:
        shapes = [jax.ShapeDtypeStruct((tokens // 2, width), dtype) for dtype in (F32, BF16)]
        scratch += [pltpu.VMEM(shape.shape, shape.dtype) for shape in shapes]
    body = functools.partial(expand_body, slots, parts, ends, tokens)
    *outs, arena = call(body, held, shapes, scratch, arena, loads, table, stored)
    return outs, arena


def swap(value, axis, bit):
    return lax.ppermute(value, axis, [(i, i ^ bit) for i in range(lax.axis_size(axis))])


def to_chip(value, k):
    count = lax.axis_size("ty")
    return lax.ppermute(value, "ty", [(i, (i + 2 * k) % count) for i in range(count)])


def cross_pipe(value, step, bit):
    sections, count = lax.axis_size("pipe"), lax.axis_size("tx")
    pairs = [
        (p * count + i, (p + step) % sections * count + (i ^ bit))
        for p in range(sections)
        for i in range(count)
    ]
    return lax.ppermute(value, ("pipe", "tx"), pairs)


def meet_body(last, carried, loads, *refs):
    operands, _, (near_ref, gone_ref), _, (total_ref,), _ = split(refs, loads, 3, 2, carried)
    kept_ref, got_ref, own_ref = operands
    half = near_ref.shape[0]
    total_ref[...] = kept_ref[...] + got_ref[...].astype(F32)
    near = total_ref[pl.ds(0, half), :]
    near_ref[...] = near + own_ref[...].astype(F32) if last else near
    gone_ref[...] = total_ref[pl.ds(half, half), :].astype(BF16)


def meet(kept, got, own, last, arena, table, stored):
    half, width = kept.shape[0] // 2, kept.shape[1]
    shapes = [jax.ShapeDtypeStruct((half, width), dtype) for dtype in (F32, BF16)]
    scratch = [pltpu.VMEM(kept.shape, F32)]
    body = functools.partial(meet_body, last, None if arena is None else True)
    near, gone, *arena = call(body, [kept, got, own], shapes, scratch, arena, [], table, stored, VM)
    return near, gone, arena[0] if arena else None


def finish(kept, got, own, step, arena, table, stored):
    count = lax.axis_size("tx")
    bit = 1
    while 2 * bit < count:
        bit *= 2
        kept, gone, arena = meet(kept, got, own, 2 * bit == count, arena, table, stored)
        if 2 * bit < count:
            got = swap(gone, "tx", bit)
    far = cross_pipe(gone, step, bit).astype(F32)
    return (cross_pipe(kept, step, 0) + far).astype(BF16), arena


def gather_body(t, count, loads, *refs):
    operands, _, _, arena, _, copies = split(refs, loads, count, 0)
    begin(copies)
    shape = (3 * count * t, 3 * t)
    row = lax.broadcasted_iota(jnp.int32, shape, 0)
    column = lax.broadcasted_iota(jnp.int32, shape, 1)
    kind, row = row // (count * t), row % (count * t)
    source = kind * t + row % t
    picks = [
        jnp.where((row // t == i) & (column == source), 1.0, 0.0).astype(BF16) for i in range(count)
    ]
    base = arena.shape[0] - 7 * count * t
    for low, size in spans(arena.shape[1]):
        piece = pl.ds(low, size)
        rows = sum(contract(pick, operand[:, piece], NN) for pick, operand in zip(picks, operands))
        arena[pl.ds(base, shape[0]), piece] = rows.astype(BF16)
    end(copies)


def after(value, others):
    return lax.optimization_barrier((value, others))[0]


def gathered(section, saved, grads, shape, loads, table, stored):
    count = lax.axis_size("tx")
    t = section.shape[0]
    own = jnp.concatenate([section, saved, grads])
    bit = count // 2
    blocks, near = {0: own}, None
    if count > 1:
        near = swap(own, "tx", 1)
    arena = load(shape, loads[:-1], table, stored)
    while bit > 1:
        for i in list(blocks):
            blocks[i ^ bit] = swap(blocks[i], "tx", bit)
        bit //= 2
    if count > 1:
        far = [i for i in blocks if i]
        for i in far:
            blocks[i ^ 1] = swap(after(blocks[i], arena), "tx", 1)
        blocks[1] = near
    arena = load(arena, loads[-1:], table, stored)
    bits = count.bit_length() - 1
    order = [int(format(n, f"0{bits}b")[::-1], 2) if bits else 0 for n in range(count)]
    operands = [blocks[i] for i in order]
    body = functools.partial(gather_body, t, count)
    return call(body, operands, [], [], arena, [], table, stored, VM)[0]


def residency(groups, quiet, slots, first):
    uses = [piece for group in groups for piece in group]

    def next_use(piece, at):
        return next((n for n in range(at, len(uses)) if uses[n] == piece), len(uses))

    begun = [(piece, slot, 0) for slot, piece in enumerate(list(dict.fromkeys(uses))[:first])]
    holds = {slot: None for slot in range(slots)}
    holds.update((slot, piece) for piece, slot, _ in begun)
    loads_at, slot_at, at = [], [], 0
    for step, group in enumerate(groups):
        slot_at.append([next(slot for slot, piece in holds.items() if piece == use) for use in group])
        loads = []
        later = at + len(group)
        for stage in range(len(group)):
            busy = slot_at[-1][stage:]
            while True:
                wanted = next((p for p in uses[later:] if p not in holds.values()), None)
                urgent = step + 1 < len(groups) and wanted in groups[step + 1]
                free = [s for s in holds if s not in busy and s not in [slot for _, slot, _ in loads]]
                if wanted is None or not free or (loads or step in quiet) and not urgent:
                    break
                slot = max(free, key=lambda s: next_use(holds[s], later))
                if next_use(holds[slot], later) <= next_use(wanted, later):
                    break
                loads.append((wanted, slot, stage))
                holds[slot] = wanted
        loads_at.append(loads)
        at += len(group)
    return begun, loads_at, slot_at


def local(section_input, saved_input, out_grad, gate_weight, up_weight, down_weight):
    count, tx = lax.axis_size("ty"), lax.axis_size("tx")
    chips = count // 2
    stored = [jnp.swapaxes(gate_weight[0], 0, 1), jnp.swapaxes(up_weight[0], 0, 1), down_weight[0]]
    units = up_to(stored[0].shape[0], 16)
    if units != stored[0].shape[0]:
        stored = [jnp.pad(w, ((0, units - w.shape[0]), (0, 0))) for w in stored]
    share = up_to(-(-units // count), 16)
    cut = share - share // 2 // 128 * 128
    subs = [(0, cut), (cut, share - cut)] if cut < share else [(0, share)]
    most = 3 * max(rows for _, rows in subs)

    me = lax.axis_index("ty")
    core, chip = me % 2, me // 2

    def share_of(k, mine):
        owner = (chip + k) % chips * 2 + (core if mine else 1 - core)
        return owner * share, jnp.minimum(owner * share, units - share)

    def place(k, mine, sub):
        return (share_of(k, mine)[1] + subs[sub][0]).astype(jnp.int32)

    def pieces(chip_order, core_order):
        return [(k, mine, sub) for k in chip_order for mine in core_order for sub in range(len(subs))]

    steps = [("project", [piece]) for piece in pieces(range(1, chips), (False, True)) + pieces((0,), (False,))]
    steps += [("activate", [piece]) for piece in pieces((0,), (True,))]
    left = pieces((0,), (False,)) + pieces(range(1, chips), (True, False))
    last = min(len(left) - 1, len(subs) + 1)
    steps.append(("expand", left[:1]))
    steps += [("expand", left[n : min(n + 2, len(left) - last)]) for n in range(1, len(left) - last, 2)]
    steps.append(("end", left[-last:]))
    quiet = [n for n, (kind, group) in enumerate(steps) if kind == "project" and group[0][1]]
    begun, loads_at, slot_at = residency([group for _, group in steps], quiet, SLOTS, SLOTS - 2)

    entries = {piece: n for n, piece in enumerate(pieces(range(chips), (False, True)))}
    share_at, within = share_of(0, True)
    table = jnp.stack(
        [place(*piece) for piece in entries]
        + [(share_at - within - at).astype(jnp.int32) for at, _ in subs]
    )

    def request(items):
        loads = [(slot * most, subs[piece[2]][1], entries[piece], stage) for piece, slot, stage in items]
        return loads, table, stored

    tokens = tx * section_input.shape[1]
    shape = (SLOTS * most + 7 * tokens, stored[0].shape[1])
    arena = gathered(section_input[0], saved_input[0], out_grad[0], shape, *request(begun))
    passed, arrived, h, forwarded = {}, {}, {}, chips == 1
    for n, (kind, group) in enumerate(steps):
        slots = [(slot * most, subs[piece[2]][1]) for slot, piece in zip(slot_at[n], group)]
        loads = request(loads_at[n])
        k, mine, sub = group[0]
        if kind == "project":
            more = passed.pop((k, sub)) if mine else []
            leave, dtype = ((5,), BF16) if mine else ((5,) if k else SPLIT, F32)
            parts, arena = project(tokens, arena, slots[0], more, [], leave, dtype, None, False, *loads)
            if mine:
                arrived.setdefault(sub, []).append(to_chip(parts[0], k))
            else:
                passed[k, sub] = [swap(part, "ty", 1) for part in parts]
        elif kind == "activate":
            others, entry = arrived.get(sub, []), len(entries) + sub
            more = passed.pop((k, sub))
            (own,), arena = project(tokens, arena, slots[0], more, others, (), F32, entry, not sub, *loads)
            h[0, True, sub] = own
            for i in range(1, chips):
                h[i, True, sub] = to_chip(own, chips - i)
            h[0, False, sub] = swap(own, "ty", 1)
        elif kind == "expand":
            held = [h[piece] for piece in group]
            _, arena = expand(tokens, held, arena, slots, (0, 1), False, *loads)
            if not forwarded and len(h) == len(subs) * (chips + 1):
                forwarded = True
                for i in range(1, chips):
                    for j in range(len(subs)):
                        h[i, False, j] = swap(after(h[i, True, j], arena), "ty", 1)
        else:
            if not forwarded:
                for i in range(1, chips):
                    for j in range(len(subs)):
                        h[i, False, j] = swap(h[i, True, j], "ty", 1)
            held = [h[piece] for piece in group]
            (kept, gone), arena = expand(tokens, held, arena, slots, (0,), True, *loads)
            got = swap(gone, "tx", 1)
            _, arena = expand(tokens, held[:-1], arena, slots[:-1], (1,), False, *request([]))
            next_input, arena = finish(kept, got, section_input[0], 1, arena, table, stored)
            (kept, gone), arena = expand(tokens, held[-1:], arena, slots[-1:], (1,), True, *request([]))
            got = swap(gone, "tx", 1)
            prev_grad, _ = finish(after(kept, next_input), got, out_grad[0], -1, None, table, stored)
    return (next_input[None], prev_grad[None])


def solution(mesh):
    return jax.shard_map(
        local,
        mesh=mesh,
        in_specs=(
            P("pipe", "tx", "ty"),
            P("pipe", "tx", "ty"),
            P("pipe", "tx", "ty"),
            P("pipe", "ty", "tx"),
            P("pipe", "ty", "tx"),
            P("pipe", "tx", "ty"),
        ),
        out_specs=(P("pipe", "tx", "ty"), P("pipe", "tx", "ty")),
        check_vma=False,
    )
```

time: 370 us -> 124 us (0.34)
  waiting for transfers between devices: 182 us -> 6.74 us
  matrix products: 119 us -> 0 us
  Pallas kernels: 0 us -> 87.6 us
  blocking collectives: 46.1 us -> 0 us
  starting transfers between devices: 2.17 us -> 22.5 us
  between operations: 14.8 us -> 0.9 us
    psum x1 -> x0, waiting for transfers between devices: 136 us -> none  [local(): lax.psum((partials[0], partials[1], partials[2], partials[3], partials[4]...]
    dot_general x8 -> x0, matrix products: 119 us -> none  [the longest x1 15.7 us: local(): lax.dot_general(grads, wdown, dims, preferred_element_type=jnp.float32)]
    pallas_call x0 -> x18, Pallas kernels: none -> 87.6 us  [call(): pl.pallas_call(functools.partial(body, loads), in_specs=specs, out_specs=...]
    all_gather x3 -> x0, blocking collectives: 46.1 us -> none  [the longest x1 16.2 us: local(): lax.all_gather(saved_input[0], 'tx', axis=0, tiled=True)]
    unnamed x3 -> x0, waiting for transfers between devices: 42.7 us -> none
    ppermute x2 -> x25, starting transfers between devices: 2.09 us -> 22.5 us  [the longest x17 12.2 us: swap(): lax.ppermute(value, axis, [(i, i ^ bit) for i in range(lax.axis_size(axis...]
  transfers between devices with their start and end apart: 4 -> 25, of which waited for: 4 -> 5; matrix products, arithmetic and copies ran while one was open for 0% -> 2% of each run, Pallas kernels for 0% -> 60%
where the time goes in v2:
time: 124 us; the launch traced here: 123 us
  Pallas kernels  87.6 us (71%)
  starting transfers between devices  22.5 us (18%)
  waiting for transfers between devices  6.74 us (5%)
  other arithmetic  3.14 us (3%)
  local copies, waits for them, and re-layouts  2.16 us (2%)
    pallas_call x18, Pallas kernels, call(): pl.pallas_call(functools.partial(body, loads), in_specs=specs, out_specs=...  87.6 us
    ppermute x17, starting transfers between devices, swap(): lax.ppermute(value, axis, [(i, i ^ bit) for i in range(lax.axis_size(axis...  12.2 us
    ppermute x4, starting transfers between devices, cross_pipe(): return lax.ppermute(value, ('pipe', 'tx'), pairs)  5.92 us
    ppermute x4, waiting for transfers between devices, cross_pipe(): return lax.ppermute(value, ('pipe', 'tx'), pairs)  5.06 us
    ppermute x4, starting transfers between devices, to_chip(): lax.ppermute(value, 'ty', [(i, (i + 2 * k) % count) for i in range(count)])  4.36 us
  transfers between devices with their start and end apart: 25, of which 5 were waited for; matrix products, arithmetic and copies ran while one was open for 2% of the time, Pallas kernels for 60%

profile of v2, /device:TPU:0, one launch (start us, length us, event | category | flops | bytes accessed | tf_op | source)
XLA Modules:
  0.0 123.1 jit_solution(16622621462648336929)
XLA Ops:
  1.6 3.1 %collective-permute-start.1 = (bf16[36,2048]{1,0:T(8,128)(2,1)S(1)}, bf16[36,2048]{1,0:T(8,128)(2,1)}, u32[]{:S(2)}, u32[]{:S(2)}) collective-permute-start(bf16[36,2048]{1,0:T(8,128)(2,1)S(1)} %pad_maximum_fusion.refs_0_), channel_id=1, source_target_pairs={{0,4},{4,0},{8,12},{12,8},{1,5},{5,1},{9,13},{13,9},{2,6},{6,2},{1... | collective-permute-start | bytes 442376 | tf_op jit(solution)/shard_map/ppermute | solution.py:284
  4.7 2.6 %collective-permute-start = (bf16[36,2048]{1,0:T(8,128)(2,1)S(1)}, bf16[36,2048]{1,0:T(8,128)(2,1)}, u32[]{:S(2)}, u32[]{:S(2)}) collective-permute-start(bf16[36,2048]{1,0:T(8,128)(2,1)S(1)} %pad_maximum_fusion.refs_0_), channel_id=1, source_target_pairs={{0,8},{4,12},{8,0},{12,4},{1,9},{5,13},{9,1},{13,5},{2,10},{6,14},... | collective-permute-start | bytes 442376 | tf_op jit(solution)/shard_map/ppermute | solution.py:284
  7.8 8.3 %shard_map.77.refs_4_ = bf16[14736,2048]{1,0:T(8,128)(2,1)S(1)} custom-call(s32[10]{0:T(128)} %stack.43.refs_0_.refs_4_.refs_1_.refs_2_.refs_3_, bf16[7392,2048]{1,0:T(8,128)(2,1)} %bitcast.25, bf16[7392,2048]{1,0:T(8,128)(2,1)} %bitcast.35, bf16[7392,2048]{1,0:T(8,128)(2,1)} %bitcast.45), custom_call_target="tpu_custom_call" | custom-call | flops 2000000000 | tf_op jit(solution)/shard_map/pallas_call | solution.py:74
  16.7 5.2 %shard_map.78.refs_5_ = bf16[14736,2048]{1,0:T(8,128)(2,1)S(1)} custom-call(s32[10]{0:T(128)} %stack.43.refs_0_.refs_4_.refs_1_.refs_2_.refs_3_, bf16[7392,2048]{1,0:T(8,128)(2,1)} %bitcast.26, bf16[7392,2048]{1,0:T(8,128)(2,1)} %bitcast.36, bf16[7392,2048]{1,0:T(8,128)(2,1)} %bitcast.46, ...), custom_call_target="tpu_custom_call", output_to_operand_aliasing={{}: (4, {})} | custom-call | flops 2000000000 | tf_op jit(solution)/shard_map/pallas_call | solution.py:74
  21.9 2.0 %shard_map.79.refs_4_ = bf16[14736,2048]{1,0:T(8,128)(2,1)S(1)} custom-call(bf16[36,2048]{1,0:T(8,128)(2,1)} %copy-done.3, bf16[36,2048]{1,0:T(8,128)(2,1)} %collective-permute-done.refs_1_, bf16[36,2048]{1,0:T(8,128)(2,1)} %collective-permute-done.1.refs_2_, bf16[36,2048]{1,0:T(8,128)(2,1)} %collective-permute-done.2.refs_3_, ...), custom_call_target="tpu_custom_call", output_to_operand_aliasing={{}: (5, {})} | custom-call | flops 2000000000 | tf_op jit(solution)/shard_map/pallas_call | solution.py:74
  23.9 5.2 %shard_map.80 = (f32[240,960]{1,0:T(8,128)}, bf16[14736,2048]{1,0:T(8,128)(2,1)S(1)}) custom-call(s32[10]{0:T(128)} %stack.43.refs_0_.refs_4_.refs_1_.refs_2_.refs_3_, bf16[7392,2048]{1,0:T(8,128)(2,1)} %bitcast.27, bf16[7392,2048]{1,0:T(8,128)(2,1)} %bitcast.37, bf16[7392,2048]{1,0:T(8,128)(2,1)} %bitcast.47, ...), custom_call_target="tpu_custom_call", output_to_operand_aliasing={{1}: (4, {})} | custom-call | flops 2000000000 | tf_op jit(solution)/shard_map/pallas_call | solution.py:74
  29.2 5.5 %shard_map.81 = (f32[240,896]{1,0:T(8,128)}, bf16[14736,2048]{1,0:T(8,128)(2,1)S(1)}) custom-call(s32[10]{0:T(128)} %stack.43.refs_0_.refs_4_.refs_1_.refs_2_.refs_3_, bf16[7392,2048]{1,0:T(8,128)(2,1)} %bitcast.28, bf16[7392,2048]{1,0:T(8,128)(2,1)} %bitcast.38, bf16[7392,2048]{1,0:T(8,128)(2,1)} %bitcast.48, ...), custom_call_target="tpu_custom_call", output_to_operand_aliasing={{1}: (4, {})} | custom-call | flops 2000000000 | tf_op jit(solution)/shard_map/pallas_call | solution.py:74
  35.2 5.1 %shard_map.82 = (bf16[240,960]{1,0:T(8,128)(2,1)}, bf16[14736,2048]{1,0:T(8,128)(2,1)S(1)}) custom-call(f32[240,960]{1,0:T(8,128)} %collective-permute-done.4.refs_0_, s32[10]{0:T(128)} %stack.43.refs_0_.refs_4_.refs_1_.refs_2_.refs_3_, bf16[14736,2048]{1,0:T(8,128)(2,1)S(1)} %get-tuple-element.40.refs_2_), custom_call_target="tpu_custom_call", output_to_operand_aliasing={{1}: (2, {})} | custom-call | flops 2000000000 | tf_op jit(solution)/shard_map/pallas_call | solution.py:74
  40.3 1.6 %collective-permute-start.12 = (bf16[240,960]{1,0:T(8,128)(2,1)}, bf16[240,960]{1,0:T(8,128)(2,1)}, u32[]{:S(2)}, u32[]{:S(2)}) collective-permute-start(bf16[240,960]{1,0:T(8,128)(2,1)} %get-tuple-element.51), channel_id=1, source_target_pairs={{0,2},{1,3},{2,0},{3,1},{4,6},{5,7},{6,4},{7,5},{8,10},{9,11},{10,... | collective-permute-start | bytes 1382408 | tf_op jit(solution)/shard_map/ppermute | solution.py:289
  41.9 4.9 %shard_map.83 = (bf16[240,896]{1,0:T(8,128)(2,1)}, bf16[14736,2048]{1,0:T(8,128)(2,1)S(1)}) custom-call(f32[240,896]{1,0:T(8,128)} %collective-permute-done.3.refs_0_, s32[10]{0:T(128)} %stack.43.refs_0_.refs_4_.refs_1_.refs_2_.refs_3_, bf16[14736,2048]{1,0:T(8,128)(2,1)S(1)} %get-tuple-element.41.refs_2_), custom_call_target="tpu_custom_call", output_to_operand_aliasing={{1}: (2, {})} | custom-call | flops 2000000000 | tf_op jit(solution)/shard_map/pallas_call | solution.py:74
  46.8 5.2 %shard_map.84 = (f32[96,960]{1,0:T(8,128)}, f32[96,960]{1,0:T(8,128)}, f32[48,960]{1,0:T(8,128)}, bf16[14736,2048]{1,0:T(8,128)(2,1)S(1)}) custom-call(s32[10]{0:T(128)} %stack.43.refs_0_.refs_4_.refs_1_.refs_2_.refs_3_, bf16[7392,2048]{1,0:T(8,128)(2,1)} %bitcast.29, bf16[7392,2048]{1,0:T(8,128)(2,1)} %bitcast.39, ...), custom_call_target="tpu_custom_call", output_to_operand_aliasing={{3}: (4, {})} | custom-call | flops 2000000000 | tf_op jit(solution)/shard_map/pallas_call | solution.py:74
  53.1 5.5 %shard_map.85 = (f32[96,896]{1,0:T(8,128)}, f32[96,896]{1,0:T(8,128)}, f32[48,896]{1,0:T(8,128)}, bf16[14736,2048]{1,0:T(8,128)(2,1)S(1)}) custom-call(s32[10]{0:T(128)} %stack.43.refs_0_.refs_4_.refs_1_.refs_2_.refs_3_, bf16[7392,2048]{1,0:T(8,128)(2,1)} %bitcast.30, bf16[7392,2048]{1,0:T(8,128)(2,1)} %bitcast.40, ...), custom_call_target="tpu_custom_call", output_to_operand_aliasing={{3}: (4, {})} | custom-call | flops 2000000000 | tf_op jit(solution)/shard_map/pallas_call | solution.py:74
  59.7 6.7 %shard_map.86 = (bf16[144,960]{1,0:T(8,128)(2,1)}, bf16[14736,2048]{1,0:T(8,128)(2,1)S(1)}) custom-call(f32[96,960]{1,0:T(8,128)} %collective-permute-done.9.refs_0_, f32[96,960]{1,0:T(8,128)} %collective-permute-done.10.refs_1_, f32[48,960]{1,0:T(8,128)} %collective-permute-done.11.refs_2_, ...), custom_call_target="tpu_custom_call", output_to_operand_aliasing={{1}: (8, {})} | custom-call | flops 4000000000 | tf_op jit(solution)/shard_map/pallas_call | solution.py:74
  68.1 6.4 %shard_map.87 = (bf16[144,896]{1,0:T(8,128)(2,1)}, bf16[14736,2048]{1,0:T(8,128)(2,1)S(1)}) custom-call(f32[96,896]{1,0:T(8,128)} %collective-permute-done.5.refs_0_, f32[96,896]{1,0:T(8,128)} %collective-permute-done.6.refs_1_, f32[48,896]{1,0:T(8,128)} %copy-done.4, ...), custom_call_target="tpu_custom_call", output_to_operand_aliasing={{1}: (8, {})} | custom-call | flops 4000000000 | tf_op jit(solution)/shard_map/pallas_call | solution.py:74
  75.4 6.2 %shard_map.88.refs_6_ = bf16[14736,2048]{1,0:T(8,128)(2,1)S(1)} custom-call(bf16[144,960]{1,0:T(8,128)(2,1)} %collective-permute-done.15.refs_0_, s32[10]{0:T(128)} %stack.43.refs_0_.refs_4_.refs_1_.refs_2_.refs_3_, bf16[7392,2048]{1,0:T(8,128)(2,1)} %bitcast.33, bf16[7392,2048]{1,0:T(8,128)(2,1)} %bitcast.43, ...), custom_call_target="tpu_custom_call", output_to_operand_aliasing={{}: (5, {})} | custom-call | flops 2000000000 | tf_op jit(solution)/shard_map/pallas_call | solution.py:74
  83.2 6.3 %shard_map.89.refs_4_ = bf16[14736,2048]{1,0:T(8,128)(2,1)S(1)} custom-call(bf16[144,896]{1,0:T(8,128)(2,1)} %collective-permute-done.18.refs_0_, bf16[144,960]{1,0:T(8,128)(2,1)} %collective-permute-done.14.refs_1_, s32[10]{0:T(128)} %stack.43.refs_0_.refs_4_.refs_1_.refs_2_.refs_3_, bf16[7392,2048]{1,0:T(8,128)(2,1)} %bitcast.34, ...), custom_call_target="tpu_custom_call", output_to_operand_aliasing={{}: (6, {})} | custom-call | flops 2000000000 | tf_op jit(solution)/shard_map/pallas_call | solution.py:74
  89.5 4.7 %shard_map.90 = (f32[24,2048]{1,0:T(8,128)}, bf16[24,2048]{1,0:T(8,128)(2,1)}, bf16[14736,2048]{1,0:T(8,128)(2,1)S(1)}) custom-call(bf16[144,896]{1,0:T(8,128)(2,1)} %collective-permute-done.13.refs_0_, bf16[144,960]{1,0:T(8,128)(2,1)} %collective-permute-done.16.refs_1_, ...), custom_call_target="tpu_custom_call", output_to_operand_aliasing={{2}: (4, {})} | custom-call | flops 2000000000 | tf_op jit(solution)/shard_map/pallas_call | solution.py:74
  94.2 1.6 %collective-permute-start.19 = (bf16[24,2048]{1,0:T(8,128)(2,1)}, bf16[24,2048]{1,0:T(8,128)(2,1)S(1)}, u32[]{:S(2)}, u32[]{:S(2)}) collective-permute-start(bf16[24,2048]{1,0:T(8,128)(2,1)} %get-tuple-element.60), channel_id=1, source_target_pairs={{0,4},{4,0},{8,12},{12,8},{1,5},{5,1},{9,13},{13,9},{2,6},{6,2},{1... | collective-permute-start | bytes 294920 | tf_op jit(solution)/shard_map/ppermute | solution.py:284
  95.8 4.7 %shard_map.91.refs_4_ = bf16[14736,2048]{1,0:T(8,128)(2,1)S(1)} custom-call(bf16[144,896]{1,0:T(8,128)(2,1)} %collective-permute-done.13.refs_0_, bf16[144,960]{1,0:T(8,128)(2,1)} %collective-permute-done.16.refs_1_, s32[10]{0:T(128)} %stack.43.refs_0_.refs_4_.refs_1_.refs_2_.refs_3_, ...), custom_call_target="tpu_custom_call", output_to_operand_aliasing={{}: (3, {})} | custom-call | flops 2000000000 | tf_op jit(solution)/shard_map/pallas_call | solution.py:74
  101.2 1.7 %shard_map.92 = (f32[12,2048]{1,0:T(8,128)}, bf16[12,2048]{1,0:T(8,128)(2,1)}, bf16[14736,2048]{1,0:T(8,128)(2,1)S(1)}) custom-call(f32[24,2048]{1,0:T(8,128)} %get-tuple-element.59.refs_0_, bf16[24,2048]{1,0:T(8,128)(2,1)} %copy-done.5, bf16[12,2048]{1,0:T(8,128)(2,1)} %bitcast.56, ...), custom_call_target="tpu_custom_call", output_to_operand_aliasing={{2}: (4, {})} | custom-call | flops 2000000000 | tf_op jit(solution)/shard_map/pallas_call | solution.py:74
  104.7 3.7 %shard_map.93 = (f32[24,2048]{1,0:T(8,128)}, bf16[24,2048]{1,0:T(8,128)(2,1)}, bf16[14736,2048]{1,0:T(8,128)(2,1)S(1)}) custom-call(bf16[144,896]{1,0:T(8,128)(2,1)} %collective-permute-done.17.refs_2_.refs_0_, s32[10]{0:T(128)} %stack.43.refs_0_.refs_4_.refs_1_.refs_2_.refs_3_, ...), custom_call_target="tpu_custom_call", output_to_operand_aliasing={{2}: (2, {})} | custom-call | flops 2000000000 | tf_op jit(solution)/shard_map/pallas_call | solution.py:74
  114.8 1.6 %collective-permute-start.23 = (f32[12,2048]{1,0:T(8,128)S(1)}, f32[12,2048]{1,0:T(8,128)S(1)}, u32[]{:S(2)}, u32[]{:S(2)}) collective-permute-start(f32[12,2048]{1,0:T(8,128)S(1)} %get-tuple-element.68), channel_id=1, source_target_pairs={{0,16},{4,20},{8,24},{12,28},{16,0},{20,4},{24,8},{28,12},{1,17},{... | collective-permute-start | bytes 294920 | tf_op jit(solution)/shard_map/ppermute | solution.py:299
  116.4 2.5 %collective-permute-start.24 = (bf16[12,2048]{1,0:T(8,128)(2,1)S(1)}, bf16[12,2048]{1,0:T(8,128)(2,1)S(1)}, u32[]{:S(2)}, u32[]{:S(2)}) collective-permute-start(bf16[12,2048]{1,0:T(8,128)(2,1)S(1)} %get-tuple-element.69), channel_id=1, source_target_pairs={{0,24},{4,28},{8,16},{12,20},{16,8},{20,12},{24,0},{28,4},{1,25},{... | collective-permute-start | bytes 147464 | tf_op jit(solution)/shard_map/ppermute | solution.py:299
  118.9 3.5 %collective-permute-done.24 = bf16[12,2048]{1,0:T(8,128)(2,1)S(1)} collective-permute-done((bf16[12,2048]{1,0:T(8,128)(2,1)S(1)}, bf16[12,2048]{1,0:T(8,128)(2,1)S(1)}, u32[]{:S(2)}, u32[]{:S(2)}) %collective-permute-start.24) | collective-permute-done | bytes 49184 | tf_op jit(solution)/shard_map/ppermute | solution.py:299
  (60 shorter events, 18.6 us)
Async XLA Ops:
  1.6 20.3 %collective-permute-start.1 = (bf16[36,2048]{1,0:T(8,128)(2,1)S(1)}, bf16[36,2048]{1,0:T(8,128)(2,1)}, u32[]{:S(2)}, u32[]{:S(2)}) collective-permute-start(bf16[36,2048]{1,0:T(8,128)(2,1)S(1)} %pad_maximum_fusion.refs_0_), channel_id=1, source_target_pairs={{0,4},{4,0},{8,12},{12,8},{1,5},{5,1},{9,13},{13,9},{2,6},{6,2},{1... | collective-permute-start | bytes 442376 | tf_op jit(solution)/shard_map/ppermute | solution.py:284
  4.7 11.5 %collective-permute-start = (bf16[36,2048]{1,0:T(8,128)(2,1)S(1)}, bf16[36,2048]{1,0:T(8,128)(2,1)}, u32[]{:S(2)}, u32[]{:S(2)}) collective-permute-start(bf16[36,2048]{1,0:T(8,128)(2,1)S(1)} %pad_maximum_fusion.refs_0_), channel_id=1, source_target_pairs={{0,8},{4,12},{8,0},{12,4},{1,9},{5,13},{9,1},{13,5},{2,10},{6,14},... | collective-permute-start | bytes 442376 | tf_op jit(solution)/shard_map/ppermute | solution.py:284
  16.1 5.8 %collective-permute-start.2 = (bf16[36,2048]{1,0:T(8,128)(2,1)}, bf16[36,2048]{1,0:T(8,128)(2,1)}, u32[]{:S(2)}, u32[]{:S(2)}) collective-permute-start(bf16[36,2048]{1,0:T(8,128)(2,1)} %collective-permute-done.refs_1_), channel_id=1, source_target_pairs={{0,4},{4,0},{8,12},{12,8},{1,5},{5,1},{9,13},{13,9},{2,6},{6,2},{1... | collective-permute-start | bytes 442376 | tf_op jit(solution)/shard_map/ppermute | solution.py:284
  29.1 6.1 %collective-permute-start.4 = (f32[240,960]{1,0:T(8,128)}, f32[240,960]{1,0:T(8,128)}, u32[]{:S(2)}, u32[]{:S(2)}) collective-permute-start(f32[240,960]{1,0:T(8,128)} %get-tuple-element.39), channel_id=1, source_target_pairs={{0,1},{1,0},{2,3},{3,2},{4,5},{5,4},{6,7},{7,6},{8,9},{9,8},{10,11... | collective-permute-start | bytes 2764808 | tf_op jit(solution)/shard_map/ppermute | solution.py:284
  34.7 7.3 %collective-permute-start.3 = (f32[240,896]{1,0:T(8,128)}, f32[240,896]{1,0:T(8,128)}, u32[]{:S(2)}, u32[]{:S(2)}) collective-permute-start(f32[240,896]{1,0:T(8,128)} %get-tuple-element.38), channel_id=1, source_target_pairs={{0,1},{1,0},{2,3},{3,2},{4,5},{5,4},{6,7},{7,6},{8,9},{9,8},{10,11... | collective-permute-start | bytes 2580488 | tf_op jit(solution)/shard_map/ppermute | solution.py:284
  40.3 19.4 %collective-permute-start.12 = (bf16[240,960]{1,0:T(8,128)(2,1)}, bf16[240,960]{1,0:T(8,128)(2,1)}, u32[]{:S(2)}, u32[]{:S(2)}) collective-permute-start(bf16[240,960]{1,0:T(8,128)(2,1)} %get-tuple-element.51), channel_id=1, source_target_pairs={{0,2},{1,3},{2,0},{3,1},{4,6},{5,7},{6,4},{7,5},{8,10},{9,11},{10,... | collective-permute-start | bytes 1382408 | tf_op jit(solution)/shard_map/ppermute | solution.py:289
  52.0 7.1 %collective-permute-start.9 = (f32[96,960]{1,0:T(8,128)}, f32[96,960]{1,0:T(8,128)}, u32[]{:S(2)}, u32[]{:S(2)}) collective-permute-start(f32[96,960]{1,0:T(8,128)} %get-tuple-element.48), channel_id=1, source_target_pairs={{0,1},{1,0},{2,3},{3,2},{4,5},{5,4},{6,7},{7,6},{8,9},{9,8},{10,11... | collective-permute-start | bytes 1105928 | tf_op jit(solution)/shard_map/ppermute | solution.py:284
  52.1 7.1 %collective-permute-start.10 = (f32[96,960]{1,0:T(8,128)}, f32[96,960]{1,0:T(8,128)}, u32[]{:S(2)}, u32[]{:S(2)}) collective-permute-start(f32[96,960]{1,0:T(8,128)} %get-tuple-element.49), channel_id=1, source_target_pairs={{0,1},{1,0},{2,3},{3,2},{4,5},{5,4},{6,7},{7,6},{8,9},{9,8},{10,11... | collective-permute-start | bytes 1105928 | tf_op jit(solution)/shard_map/ppermute | solution.py:284
  52.6 15.5 %collective-permute-start.8 = (bf16[240,896]{1,0:T(8,128)(2,1)}, bf16[240,896]{1,0:T(8,128)(2,1)}, u32[]{:S(2)}, u32[]{:S(2)}) collective-permute-start(bf16[240,896]{1,0:T(8,128)(2,1)} %get-tuple-element.47), channel_id=1, source_target_pairs={{0,2},{1,3},{2,0},{3,1},{4,6},{5,7},{6,4},{7,5},{8,10},{9,11},{10,... | collective-permute-start | bytes 1290248 | tf_op jit(solution)/shard_map/ppermute | solution.py:289
  53.1 5.5 %collective-permute-start.11 = (f32[48,960]{1,0:T(8,128)}, f32[48,960]{1,0:T(8,128)}, u32[]{:S(2)}, u32[]{:S(2)}) collective-permute-start(f32[48,960]{1,0:T(8,128)} %get-tuple-element.50), channel_id=1, source_target_pairs={{0,1},{1,0},{2,3},{3,2},{4,5},{5,4},{6,7},{7,6},{8,9},{9,8},{10,11... | collective-permute-start | bytes 552968 | tf_op jit(solution)/shard_map/ppermute | solution.py:284
  58.6 8.0 %collective-permute-start.7 = (f32[48,896]{1,0:T(8,128)}, f32[48,896]{1,0:T(8,128)S(1)}, u32[]{:S(2)}, u32[]{:S(2)}) collective-permute-start(f32[48,896]{1,0:T(8,128)} %get-tuple-element.46), channel_id=1, source_target_pairs={{0,1},{1,0},{2,3},{3,2},{4,5},{5,4},{6,7},{7,6},{8,9},{9,8},{10,11... | collective-permute-start | bytes 516104 | tf_op jit(solution)/shard_map/ppermute | solution.py:284
  59.1 8.9 %collective-permute-start.5 = (f32[96,896]{1,0:T(8,128)}, f32[96,896]{1,0:T(8,128)}, u32[]{:S(2)}, u32[]{:S(2)}) collective-permute-start(f32[96,896]{1,0:T(8,128)} %get-tuple-element.44), channel_id=1, source_target_pairs={{0,1},{1,0},{2,3},{3,2},{4,5},{5,4},{6,7},{7,6},{8,9},{9,8},{10,11... | collective-permute-start | bytes 1032200 | tf_op jit(solution)/shard_map/ppermute | solution.py:284
  59.2 8.9 %collective-permute-start.6 = (f32[96,896]{1,0:T(8,128)}, f32[96,896]{1,0:T(8,128)}, u32[]{:S(2)}, u32[]{:S(2)}) collective-permute-start(f32[96,896]{1,0:T(8,128)} %get-tuple-element.45), channel_id=1, source_target_pairs={{0,1},{1,0},{2,3},{3,2},{4,5},{5,4},{6,7},{7,6},{8,9},{9,8},{10,11... | collective-permute-start | bytes 1032200 | tf_op jit(solution)/shard_map/ppermute | solution.py:284
  66.4 9.0 %collective-permute-start.15 = (bf16[144,960]{1,0:T(8,128)(2,1)}, bf16[144,960]{1,0:T(8,128)(2,1)}, u32[]{:S(2)}, u32[]{:S(2)}) collective-permute-start(bf16[144,960]{1,0:T(8,128)(2,1)} %get-tuple-element.55), channel_id=1, source_target_pairs={{0,1},{1,0},{2,3},{3,2},{4,5},{5,4},{6,7},{7,6},{8,9},{9,8},{10,11... | collective-permute-start | bytes 829448 | tf_op jit(solution)/shard_map/ppermute | solution.py:284
  66.5 15.1 %collective-permute-start.14 = (bf16[144,960]{1,0:T(8,128)(2,1)}, bf16[144,960]{1,0:T(8,128)(2,1)}, u32[]{:S(2)}, u32[]{:S(2)}) collective-permute-start(bf16[144,960]{1,0:T(8,128)(2,1)} %get-tuple-element.55), channel_id=1, source_target_pairs={{0,2},{1,3},{2,0},{3,1},{4,6},{5,7},{6,4},{7,5},{8,10},{9,11},{10,... | collective-permute-start | bytes 829448 | tf_op jit(solution)/shard_map/ppermute | solution.py:289
  74.6 8.7 %collective-permute-start.13 = (bf16[144,896]{1,0:T(8,128)(2,1)}, bf16[144,896]{1,0:T(8,128)(2,1)}, u32[]{:S(2)}, u32[]{:S(2)}) collective-permute-start(bf16[144,896]{1,0:T(8,128)(2,1)} %get-tuple-element.54), channel_id=1, source_target_pairs={{0,2},{1,3},{2,0},{3,1},{4,6},{5,7},{6,4},{7,5},{8,10},{9,11},{10,... | collective-permute-start | bytes 774152 | tf_op jit(solution)/shard_map/ppermute | solution.py:289
  75.3 8.0 %collective-permute-start.18 = (bf16[144,896]{1,0:T(8,128)(2,1)}, bf16[144,896]{1,0:T(8,128)(2,1)}, u32[]{:S(2)}, u32[]{:S(2)}) collective-permute-start(bf16[144,896]{1,0:T(8,128)(2,1)} %get-tuple-element.54), channel_id=1, source_target_pairs={{0,1},{1,0},{2,3},{3,2},{4,5},{5,4},{6,7},{7,6},{8,9},{9,8},{10,11... | collective-permute-start | bytes 774152 | tf_op jit(solution)/shard_map/ppermute | solution.py:284
  81.6 7.9 %collective-permute-start.16 = (bf16[144,960]{1,0:T(8,128)(2,1)}, bf16[144,960]{1,0:T(8,128)(2,1)}, u32[]{:S(2)}, u32[]{:S(2)}) collective-permute-start(bf16[144,960]{1,0:T(8,128)(2,1)} %collective-permute-done.14.refs_1_), channel_id=1, source_target_pairs={{0,1},{1,0},{2,3},{3,2},{4,5},{5,4},{6,7},{7,6},{8,9},{9,8},{10,11... | collective-permute-start | bytes 829448 | tf_op jit(solution)/shard_map/ppermute | solution.py:284
  83.2 6.3 %collective-permute-start.17 = (bf16[144,896]{1,0:T(8,128)(2,1)}, bf16[144,896]{1,0:T(8,128)(2,1)}, u32[]{:S(2)}, u32[]{:S(2)}) collective-permute-start(bf16[144,896]{1,0:T(8,128)(2,1)} %collective-permute-done.13.refs_0_), channel_id=1, source_target_pairs={{0,1},{1,0},{2,3},{3,2},{4,5},{5,4},{6,7},{7,6},{8,9},{9,8},{10,11... | collective-permute-start | bytes 774152 | tf_op jit(solution)/shard_map/ppermute | solution.py:284
  94.2 6.3 %collective-permute-start.19 = (bf16[24,2048]{1,0:T(8,128)(2,1)}, bf16[24,2048]{1,0:T(8,128)(2,1)S(1)}, u32[]{:S(2)}, u32[]{:S(2)}) collective-permute-start(bf16[24,2048]{1,0:T(8,128)(2,1)} %get-tuple-element.60), channel_id=1, source_target_pairs={{0,4},{4,0},{8,12},{12,8},{1,5},{5,1},{9,13},{13,9},{2,6},{6,2},{1... | collective-permute-start | bytes 294920 | tf_op jit(solution)/shard_map/ppermute | solution.py:284
  102.9 7.6 %collective-permute-start.21 = (bf16[12,2048]{1,0:T(8,128)(2,1)}, bf16[12,2048]{1,0:T(8,128)(2,1)S(1)}, u32[]{:S(2)}, u32[]{:S(2)}) collective-permute-start(bf16[12,2048]{1,0:T(8,128)(2,1)} %get-tuple-element.63), channel_id=1, source_target_pairs={{0,24},{4,28},{8,16},{12,20},{16,8},{20,12},{24,0},{28,4},{1,25},{... | collective-permute-start | bytes 147464 | tf_op jit(solution)/shard_map/ppermute | solution.py:299
  104.2 7.1 %collective-permute-start.20 = (f32[12,2048]{1,0:T(8,128)}, f32[12,2048]{1,0:T(8,128)}, u32[]{:S(2)}, u32[]{:S(2)}) collective-permute-start(f32[12,2048]{1,0:T(8,128)} %get-tuple-element.62), channel_id=1, source_target_pairs={{0,16},{4,20},{8,24},{12,28},{16,0},{20,4},{24,8},{28,12},{1,17},{... | collective-permute-start | bytes 294920 | tf_op jit(solution)/shard_map/ppermute | solution.py:299
  114.8 7.7 %collective-permute-start.23 = (f32[12,2048]{1,0:T(8,128)S(1)}, f32[12,2048]{1,0:T(8,128)S(1)}, u32[]{:S(2)}, u32[]{:S(2)}) collective-permute-start(f32[12,2048]{1,0:T(8,128)S(1)} %get-tuple-element.68), channel_id=1, source_target_pairs={{0,16},{4,20},{8,24},{12,28},{16,0},{20,4},{24,8},{28,12},{1,17},{... | collective-permute-start | bytes 294920 | tf_op jit(solution)/shard_map/ppermute | solution.py:299
  116.4 6.1 %collective-permute-start.24 = (bf16[12,2048]{1,0:T(8,128)(2,1)S(1)}, bf16[12,2048]{1,0:T(8,128)(2,1)S(1)}, u32[]{:S(2)}, u32[]{:S(2)}) collective-permute-start(bf16[12,2048]{1,0:T(8,128)(2,1)S(1)} %get-tuple-element.69), channel_id=1, source_target_pairs={{0,24},{4,28},{8,16},{12,20},{16,8},{20,12},{24,0},{28,4},{1,25},{... | collective-permute-start | bytes 147464 | tf_op jit(solution)/shard_map/ppermute | solution.py:299
  (7 other events, 46.8 us)

commit v3 on v2

--- a/solution.py
+++ b/solution.py
@@ -16,6 +16,7 @@
 SM = pl.BlockSpec(memory_space=pltpu.SMEM)
 STEP = 512
 SLOTS = 5
+BEGUN = 2
 SPLIT = (2, 2, 1)
 HINT = 2 * 10**9
 
@@ -135,51 +136,76 @@
     return arena[high, piece].astype(F32) + arena[low, piece].astype(F32)
 
 
-def project_body(at, rows, got, others, leave, tokens, entry, fresh, loads, *refs):
-    outs = 1 if entry is not None else len(leave)
-    operands, table, out_refs, arena, scratch, copies = split(refs, loads, len(got) + others, outs)
-    part_ref, out_sems = scratch[:2]
+def project_body(jobs, tokens, loads, *refs):
+    ins = sum(len(job["got"]) + job["others"] for job in jobs)
+    outs = sum(len(job["leave"]) or 1 for job in jobs)
+    operands, table, out_refs, arena, scratch, copies = split(refs, loads, ins, outs)
+    operands, out_refs, scratch = list(operands), list(out_refs), list(scratch)
     blocks = [pl.ds(0, 2 * tokens), pl.ds(2 * tokens, 2 * tokens), pl.ds(4 * tokens, tokens)]
-    arrivals, held = [], scratch[2 : 2 + others + (1 if got else 0)]
-    in_sems = scratch[2 + len(held)] if held else None
-    targets, low = [], 0
-    for count in got:
-        targets.append(held[0].at[pl.ds(low, count * tokens), :])
-        low += count * tokens
-    targets += held[1 if got else 0 :]
-    arrivals = [pltpu.make_async_copy(source, targets[i], in_sems.at[i]) for i, source in enumerate(operands)]
-    begin(arrivals)
-    if not arrivals:
+    base = arena.shape[0] - 7 * tokens
+    work = []
+    for job in jobs:
+        part_ref, out_sems = scratch.pop(0), scratch.pop(0)
+        held = [scratch.pop(0) for _ in range(job["others"] + bool(job["got"]))]
+        targets, low = [], 0
+        for count in job["got"]:
+            targets.append(held[0].at[pl.ds(low, count * tokens), :])
+            low += count * tokens
+        targets += held[bool(job["got"]) :]
+        in_sems = scratch.pop(0) if targets else None
+        arrivals = [
+            pltpu.make_async_copy(operands.pop(0), target, in_sems.at[i]) for i, target in enumerate(targets)
+        ]
+        begin(arrivals)
+        h_ref = scratch.pop(0) if job["entry"] is not None else None
+        first_ref = part_ref
+        if targets and h_ref is None:
+            first_ref = scratch.pop(0)
+        to = [out_refs.pop(0) for _ in range(len(job["leave"]) or 1)]
+        work.append((job, part_ref, out_sems, held, arrivals, h_ref, first_ref, to))
+    if not work[0][4]:
         begin(copies)
-    first_ref = scratch[-1] if arrivals and entry is None else part_ref
-    h_ref = scratch[-1]
-    base = arena.shape[0] - 7 * tokens
     leaving = []
 
-    def finished(part, i, piece):
-        for ref in held:
-            part = part + ref[blocks[i], piece].astype(F32)
-        return part
-
-    def leaves(i):
-        if entry is None:
-            target = out_refs[0].at[blocks[i], :] if len(out_refs) == 1 else out_refs[i]
-            leaving.append(pltpu.make_async_copy(part_ref.at[blocks[i], :], target, out_sems.at[i]))
-            leaving[-1].start()
-
-    for i, (first, count) in enumerate(((0, 2), (0, 2), (2, 1))):
-        lhs = arena[pl.ds(base + first * tokens, count * tokens), :]
-        for low, size in spans(rows):
-            piece = pl.ds(low, size)
-            part = contract(lhs, arena[pl.ds(at + i * rows + low, size), :], NT)
-            if not i and arrivals:
-                first_ref[blocks[0], piece] = part
-                continue
-            if i == 1 and not low and arrivals:
-                end(arrivals)
-                begin(copies)
-            part_ref[blocks[i], piece] = finished(part, i, piece).astype(part_ref.dtype)
-            if i == 2 and entry is not None:
+    for number, (job, part_ref, out_sems, held, arrivals, h_ref, first_ref, to) in enumerate(work):
+        at, rows, entry = job["at"], job["rows"], job["entry"]
+        pending = (0, 1, 2) if copies and entry is None and len(work) == 1 else (0,)
+        pending = pending if arrivals else ()
+        if arrivals and pending == (0, 1, 2) and not number:
+            begin(copies)
+
+        def finished(part, i, piece):
+            for ref in held:
+                part = part + ref[blocks[i], piece].astype(F32)
+            return part
+
+        def complete(i):
+            for low, size in spans(rows):
+                piece = pl.ds(low, size)
+                part = finished(first_ref[blocks[i], piece], i, piece)
+                part_ref[blocks[i], piece] = part.astype(part_ref.dtype)
+
+        def leaves(i):
+            if entry is None:
+                target = to[0].at[blocks[i], :] if len(to) == 1 else to[i]
+                leaving.append(pltpu.make_async_copy(part_ref.at[blocks[i], :], target, out_sems.at[i]))
+                leaving[-1].start()
+
+        for i, (first, count) in enumerate(((0, 2), (0, 2), (2, 1))):
+            lhs = arena[pl.ds(base + first * tokens, count * tokens), :]
+            for low, size in spans(rows):
+                piece = pl.ds(low, size)
+                part = contract(lhs, arena[pl.ds(at + i * rows + low, size), :], NT)
+                if i in pending:
+                    first_ref[blocks[i], piece] = part
+                    continue
+                if pending and i == 1 and not low:
+                    end(arrivals)
+                    if not number:
+                        begin(copies)
+                part_ref[blocks[i], piece] = finished(part, i, piece).astype(part_ref.dtype)
+                if i < 2 or entry is None:
+                    continue
                 for at_column in range(low, low + size, 128):
                     columns = pl.ds(at_column, min(128, low + size - at_column))
                     gate, saved_gate, up, saved_up, hidden_grad = [
@@ -192,63 +218,71 @@
                     up_grad = hidden_grad * saved_gate * sigma
                     for n, value in enumerate((hidden, gate_grad, up_grad)):
                         h_ref[pl.ds(n * tokens, tokens), columns] = jnp.where(mine, value, 0.0).astype(BF16)
-        if i == 1 and arrivals:
-            for low, size in spans(rows):
+            if i == 1 and pending == (0,):
+                complete(0)
+                leaves(0)
+            if i not in pending:
+                leaves(i)
+        if pending == (0, 1, 2):
+            end(arrivals)
+            for i in pending:
+                complete(i)
+                leaves(i)
+        if entry is not None:
+            leaving.append(pltpu.make_async_copy(h_ref, to[0], out_sems.at[0]))
+            leaving[-1].start()
+            for low, size in spans(arena.shape[1]):
                 piece = pl.ds(low, size)
-                part = finished(first_ref[blocks[0], piece], 0, piece)
-                part_ref[blocks[0], piece] = part.astype(part_ref.dtype)
-            leaves(0)
-        if i or not arrivals:
-            leaves(i)
-    if entry is not None:
-        leaving.append(pltpu.make_async_copy(h_ref, out_refs[0], out_sems.at[0]))
-        leaving[-1].start()
-        for low, size in spans(arena.shape[1]):
-            piece = pl.ds(low, size)
-            for part in (0, 1):
-                value = products(arena, [h_ref], [(at, rows)], part, tokens, piece)
-                if not fresh:
-                    value = value + kept_sum(arena, part, tokens, piece)
-                keep(arena, value, part, tokens, piece)
+                for part in (0, 1):
+                    value = products(arena, [h_ref], [(at, rows)], part, tokens, piece)
+                    if not job["fresh"]:
+                        value = value + kept_sum(arena, part, tokens, piece)
+                    keep(arena, value, part, tokens, piece)
     end(leaving)
     end(copies)
 
 
-def project(tokens, arena, slot, more, others, leave, dtype, entry, fresh, loads, table, stored):
-    at, rows = slot
-    operands = more + others
-    part = jax.ShapeDtypeStruct((5 * tokens, rows), dtype)
-    shapes = [jax.ShapeDtypeStruct((count * tokens, rows), dtype) for count in leave]
-    if entry is not None:
-        shapes = [jax.ShapeDtypeStruct((3 * tokens, rows), BF16)]
-    scratch = [pltpu.VMEM(part.shape, dtype), pltpu.SemaphoreType.DMA((3,))]
-    scratch += [pltpu.VMEM(part.shape, F32)] * (1 if more else 0)
-    scratch += [pltpu.VMEM(operand.shape, operand.dtype) for operand in others]
-    if operands:
-        scratch.append(pltpu.SemaphoreType.DMA((len(operands),)))
-    if entry is not None:
-        scratch.append(pltpu.VMEM(shapes[0].shape, BF16))
-    elif operands:
-        scratch.append(pltpu.VMEM((2 * tokens, rows), F32))
-    got = [piece.shape[0] // tokens for piece in more]
-    body = functools.partial(project_body, at, rows, got, len(others), leave, tokens, entry, fresh)
-    *outs, arena = call(body, operands, shapes, scratch, arena, loads, table, stored, HBM, 1 if entry is None else 2)
+def project(tokens, arena, jobs, loads, table, stored):
+    operands, shapes, scratch, static = [], [], [], []
+    for (at, rows), more, others, leave, dtype, entry, fresh in jobs:
+        operands += more + others
+        part = jax.ShapeDtypeStruct((5 * tokens, rows), dtype)
+        scratch += [pltpu.VMEM(part.shape, dtype), pltpu.SemaphoreType.DMA((3,))]
+        scratch += [pltpu.VMEM(part.shape, F32)] * (1 if more else 0)
+        scratch += [pltpu.VMEM(operand.shape, operand.dtype) for operand in others]
+        if more or others:
+            scratch.append(pltpu.SemaphoreType.DMA((len(more + others),)))
+        if entry is not None:
+            shapes.append(jax.ShapeDtypeStruct((3 * tokens, rows), BF16))
+            scratch.append(pltpu.VMEM(shapes[-1].shape, BF16))
+        else:
+            shapes += [jax.ShapeDtypeStruct((count * tokens, rows), dtype) for count in leave]
+            if more or others:
+                scratch.append(pltpu.VMEM(part.shape, F32))
+        got = [piece.shape[0] // tokens for piece in more]
+        static.append(dict(at=at, rows=rows, got=got, others=len(others), leave=leave, entry=entry, fresh=fresh))
+    weight = sum(1 if job["entry"] is None else 2 for job in static)
+    body = functools.partial(project_body, static, tokens)
+    *outs, arena = call(body, operands, shapes, scratch, arena, loads, table, stored, weight=weight)
     return outs, arena
 
 
 def expand_body(slots, parts, ends, tokens, loads, *refs):
     operands, _, outs, arena, scratch, copies = split(refs, loads, len(slots), 2 * ends)
-    in_sems, out_sems, *held = scratch
+    in_sems, *held = scratch
     arrivals = [pltpu.make_async_copy(operand, held[i], in_sems.at[i]) for i, operand in enumerate(operands)]
     begin(arrivals)
-    total_ref, gone_ref = held[len(slots) :] if ends else (None, None)
     leaving = []
+    if ends:
+        out_sems, *leave_refs = held[len(slots) :]
     for n, slot in enumerate(slots):
-        if not n:
+        if not n and len(slots) > 1:
             end(arrivals)
         for i, copy in enumerate(copies):
             if loads[i // 3][3] == n:
                 copy.start()
+        if not n and len(slots) == 1:
+            end(arrivals)
         for m, (low, size) in enumerate(spans(arena.shape[1])):
             piece = pl.ds(low, size)
             for part in parts:
@@ -257,9 +291,9 @@
                 if not ends or n < len(slots) - 1:
                     keep(arena, value, part, tokens, piece)
                     continue
-                total_ref[:, piece] = value[: tokens // 2]
-                gone_ref[:, piece] = value[tokens // 2 :].astype(BF16)
-                for k, source in enumerate((total_ref, gone_ref)):
+                leave_refs[0][:, piece] = value[: tokens // 2]
+                leave_refs[1][:, piece] = value[tokens // 2 :].astype(BF16)
+                for k, source in enumerate(leave_refs):
                     copy = pltpu.make_async_copy(source.at[:, piece], outs[k].at[:, piece], out_sems.at[k, m])
                     leaving.append(copy)
                     copy.start()
@@ -270,10 +304,11 @@
 def expand(tokens, held, arena, slots, parts, ends, loads, table, stored):
     width = arena.shape[1]
     shapes = []
-    scratch = [pltpu.SemaphoreType.DMA((len(held),)), pltpu.SemaphoreType.DMA((2, len(spans(width))))]
+    scratch = [pltpu.SemaphoreType.DMA((len(held),))]
     scratch += [pltpu.VMEM(operand.shape, operand.dtype) for operand in held]
     if ends:
         shapes = [jax.ShapeDtypeStruct((tokens // 2, width), dtype) for dtype in (F32, BF16)]
+        scratch.append(pltpu.SemaphoreType.DMA((2, len(spans(width)))))
         scratch += [pltpu.VMEM(shape.shape, shape.dtype) for shape in shapes]
     body = functools.partial(expand_body, slots, parts, ends, tokens)
     *outs, arena = call(body, held, shapes, scratch, arena, loads, table, stored)
@@ -299,35 +334,23 @@
     return lax.ppermute(value, ("pipe", "tx"), pairs)
 
 
-def meet_body(last, carried, loads, *refs):
-    operands, _, (near_ref, gone_ref), _, (total_ref,), _ = split(refs, loads, 3, 2, carried)
-    kept_ref, got_ref, own_ref = operands
-    half = near_ref.shape[0]
-    total_ref[...] = kept_ref[...] + got_ref[...].astype(F32)
-    near = total_ref[pl.ds(0, half), :]
-    near_ref[...] = near + own_ref[...].astype(F32) if last else near
-    gone_ref[...] = total_ref[pl.ds(half, half), :].astype(BF16)
-
-
-def meet(kept, got, own, last, arena, table, stored):
-    half, width = kept.shape[0] // 2, kept.shape[1]
-    shapes = [jax.ShapeDtypeStruct((half, width), dtype) for dtype in (F32, BF16)]
-    scratch = [pltpu.VMEM(kept.shape, F32)]
-    body = functools.partial(meet_body, last, None if arena is None else True)
-    near, gone, *arena = call(body, [kept, got, own], shapes, scratch, arena, [], table, stored, VM)
-    return near, gone, arena[0] if arena else None
-
-
-def finish(kept, got, own, step, arena, table, stored):
+def block_order(count):
+    bits = count.bit_length() - 1
+    return [int(format(n, f"0{bits}b")[::-1], 2) if bits else 0 for n in range(count)]
+
+
+def finish(kept, got, own, step):
     count = lax.axis_size("tx")
     bit = 1
     while 2 * bit < count:
+        kept = kept + got.astype(F32)
+        half = kept.shape[0] // 2
+        kept, gone = kept[:half], kept[half:].astype(BF16)
         bit *= 2
-        kept, gone, arena = meet(kept, got, own, 2 * bit == count, arena, table, stored)
         if 2 * bit < count:
             got = swap(gone, "tx", bit)
-    far = cross_pipe(gone, step, bit).astype(F32)
-    return (cross_pipe(kept, step, 0) + far).astype(BF16), arena
+    near = cross_pipe(kept + own.astype(F32), step, 0)
+    return (near + cross_pipe(gone, step, bit).astype(F32)).astype(BF16)
 
 
 def gather_body(t, count, loads, *refs):
@@ -360,7 +383,7 @@
     bit = count // 2
     blocks, near = {0: own}, None
     if count > 1:
-        near = swap(own, "tx", 1)
+        near = swap(after(own, table), "tx", 1)
     arena = load(shape, loads[:-1], table, stored)
     while bit > 1:
         for i in list(blocks):
@@ -372,8 +395,7 @@
             blocks[i ^ 1] = swap(after(blocks[i], arena), "tx", 1)
         blocks[1] = near
     arena = load(arena, loads[-1:], table, stored)
-    bits = count.bit_length() - 1
-    order = [int(format(n, f"0{bits}b")[::-1], 2) if bits else 0 for n in range(count)]
+    order = block_order(count)
     operands = [blocks[i] for i in order]
     body = functools.partial(gather_body, t, count)
     return call(body, operands, [], [], arena, [], table, stored, VM)[0]
@@ -437,14 +459,18 @@
         return [(k, mine, sub) for k in chip_order for mine in core_order for sub in range(len(subs))]
 
     steps = [("project", [piece]) for piece in pieces(range(1, chips), (False, True)) + pieces((0,), (False,))]
+    middle = len(steps) - len(subs) - 1
+    if chips > 1:
+        steps[middle : middle + 2] = [("project", steps[middle][1] + steps[middle + 1][1])]
     steps += [("activate", [piece]) for piece in pieces((0,), (True,))]
-    left = pieces((0,), (False,)) + pieces(range(1, chips), (True, False))
-    last = min(len(left) - 1, len(subs) + 1)
-    steps.append(("expand", left[:1]))
-    steps += [("expand", left[n : min(n + 2, len(left) - last)]) for n in range(1, len(left) - last, 2)]
+    near, far = pieces((0,), (False,)), pieces(range(1, chips), (True,))
+    steps += [("expand", near[n : n + 1] + far[n : n + 1]) for n in range(max(len(near), len(far)))]
+    left = pieces(range(1, chips), (False,))
+    last = len(subs)
+    steps += [("expand", left[n : min(n + 2, len(left) - last)]) for n in range(0, len(left) - last, 2)]
     steps.append(("end", left[-last:]))
-    quiet = [n for n, (kind, group) in enumerate(steps) if kind == "project" and group[0][1]]
-    begun, loads_at, slot_at = residency([group for _, group in steps], quiet, SLOTS, SLOTS - 2)
+    quiet = [n for n, (kind, group) in enumerate(steps) if kind == "project" and group[0][1] and len(group) == 1]
+    begun, loads_at, slot_at = residency([group for _, group in steps], quiet, SLOTS, BEGUN)
 
     entries = {piece: n for n, piece in enumerate(pieces(range(chips), (False, True)))}
     share_at, within = share_of(0, True)
@@ -464,23 +490,28 @@
     for n, (kind, group) in enumerate(steps):
         slots = [(slot * most, subs[piece[2]][1]) for slot, piece in zip(slot_at[n], group)]
         loads = request(loads_at[n])
-        k, mine, sub = group[0]
-        if kind == "project":
-            more = passed.pop((k, sub)) if mine else []
-            leave, dtype = ((5,), BF16) if mine else ((5,) if k else SPLIT, F32)
-            parts, arena = project(tokens, arena, slots[0], more, [], leave, dtype, None, False, *loads)
-            if mine:
-                arrived.setdefault(sub, []).append(to_chip(parts[0], k))
-            else:
-                passed[k, sub] = [swap(part, "ty", 1) for part in parts]
-        elif kind == "activate":
-            others, entry = arrived.get(sub, []), len(entries) + sub
-            more = passed.pop((k, sub))
-            (own,), arena = project(tokens, arena, slots[0], more, others, (), F32, entry, not sub, *loads)
-            h[0, True, sub] = own
-            for i in range(1, chips):
-                h[i, True, sub] = to_chip(own, chips - i)
-            h[0, False, sub] = swap(own, "ty", 1)
+        if kind in ("project", "activate"):
+            jobs = []
+            for slot, (k, mine, sub) in zip(slots, group):
+                more = passed.pop((k, sub)) if mine else []
+                if mine and not k:
+                    jobs.append((slot, more, arrived.get(sub, []), (), F32, len(entries) + sub, not sub))
+                else:
+                    leave, dtype = ((5,), BF16) if mine else ((5,) if k else SPLIT, F32)
+                    jobs.append((slot, more, [], leave, dtype, None, False))
+            parts, arena = project(tokens, arena, jobs, *loads)
+            for k, mine, sub in group:
+                if mine and not k:
+                    own = parts.pop(0)
+                    h[0, True, sub] = own
+                    for i in range(1, chips):
+                        h[i, True, sub] = to_chip(own, chips - i)
+                    h[0, False, sub] = swap(own, "ty", 1)
+                elif mine:
+                    arrived.setdefault(sub, []).append(to_chip(parts.pop(0), k))
+                else:
+                    count = 1 if k else len(SPLIT)
+                    passed[k, sub] = [swap(parts.pop(0), "ty", 1) for _ in range(count)]
         elif kind == "expand":
             held = [h[piece] for piece in group]
             _, arena = expand(tokens, held, arena, slots, (0, 1), False, *loads)
@@ -497,11 +528,9 @@
             held = [h[piece] for piece in group]
             (kept, gone), arena = expand(tokens, held, arena, slots, (0,), True, *loads)
             got = swap(gone, "tx", 1)
-            _, arena = expand(tokens, held[:-1], arena, slots[:-1], (1,), False, *request([]))
-            next_input, arena = finish(kept, got, section_input[0], 1, arena, table, stored)
-            (kept, gone), arena = expand(tokens, held[-1:], arena, slots[-1:], (1,), True, *request([]))
-            got = swap(gone, "tx", 1)
-            prev_grad, _ = finish(after(kept, next_input), got, out_grad[0], -1, None, table, stored)
+            (kept_back, gone), _ = expand(tokens, held, arena, slots, (1,), True, *request([]))
+            next_input = finish(kept, got, section_input[0], 1)
+            prev_grad = finish(kept_back, swap(gone, "tx", 1), out_grad[0], -1)
     return (next_input[None], prev_grad[None])
 
 

time: 124 us -> 114 us (0.919)
  Pallas kernels: 87.6 us -> 77.8 us
  starting transfers between devices: 22.5 us -> 24.2 us
  local copies, waits for them, and re-layouts: 2.16 us -> 0.62 us
    pallas_call x18 -> x14, Pallas kernels: 87.6 us -> 77.8 us  [call(): pl.pallas_call(functools.partial(body, loads), in_specs=specs, out_specs=...]
    ppermute x4, starting transfers between devices: 5.92 us -> 9.02 us  [cross_pipe(): return lax.ppermute(value, ('pipe', 'tx'), pairs)]
    add x0 -> x4, other arithmetic: none -> 2 us  [the longest x2 1.96 us: finish(): kept = kept + got.astype(F32)]
    unnamed x12 -> x8, local copies, waits for them, and re-layouts: 1.58 us -> 0.02 us
    convert_element_type x1 -> x0, other arithmetic: 1.55 us -> none  [finish(): return ((cross_pipe(kept, step, 0) + far).astype(BF16), arena)]
    ppermute x17, starting transfers between devices: 12.2 us -> 10.8 us  [swap(): lax.ppermute(value, axis, [(i, i ^ bit) for i in range(lax.axis_size(axis...]
    ppermute x4, waiting for transfers between devices: 5.06 us -> 3.81 us  [cross_pipe(): return lax.ppermute(value, ('pipe', 'tx'), pairs)]
  transfers between devices with their start and end apart: 25 -> 25, of which waited for: 5 -> 6; matrix products, arithmetic and copies ran while one was open for 2% -> 3% of each run, Pallas kernels for 60% -> 58%
where the time goes in v3:
time: 114 us
  Pallas kernels  77.8 us (68%)
  starting transfers between devices  24.2 us (21%)
  waiting for transfers between devices  5.96 us (5%)
  other arithmetic  4.24 us (4%)
    pallas_call x14, Pallas kernels, call(): pl.pallas_call(functools.partial(body, loads), in_specs=specs, out_specs=...  77.8 us
    ppermute x17, starting transfers between devices, swap(): lax.ppermute(value, axis, [(i, i ^ bit) for i in range(lax.axis_size(axis...  10.8 us
    ppermute x4, starting transfers between devices, cross_pipe(): return lax.ppermute(value, ('pipe', 'tx'), pairs)  9.02 us
    ppermute x4, starting transfers between devices, to_chip(): lax.ppermute(value, 'ty', [(i, (i + 2 * k) % count) for i in range(count)])  4.34 us
    ppermute x4, waiting for transfers between devices, cross_pipe(): return lax.ppermute(value, ('pipe', 'tx'), pairs)  3.81 us
  transfers between devices with their start and end apart: 25, of which 6 were waited for; matrix products, arithmetic and copies ran while one was open for 3% of the time, Pallas kernels for 58%

profile of v3, /device:TPU:0, one launch (start us, length us, event | category | flops | bytes accessed | tf_op | source)
XLA Modules:
  0.0 113.8 jit_solution(2083047258620273716)
XLA Ops:
  1.6 4.1 %collective-permute-start = (bf16[36,2048]{1,0:T(8,128)(2,1)S(1)}, bf16[36,2048]{1,0:T(8,128)(2,1)}, u32[]{:S(2)}, u32[]{:S(2)}) collective-permute-start(bf16[36,2048]{1,0:T(8,128)(2,1)S(1)} %pad_maximum_fusion.refs_0_), channel_id=1, source_target_pairs={{0,8},{4,12},{8,0},{12,4},{1,9},{5,13},{9,1},{13,5},{2,10},{6,14},... | collective-permute-start | bytes 442376 | tf_op jit(solution)/shard_map/ppermute | solution.py:319
  6.3 1.6 %collective-permute-start.1 = (bf16[36,2048]{1,0:T(8,128)(2,1)S(1)}, bf16[36,2048]{1,0:T(8,128)(2,1)}, u32[]{:S(2)}, u32[]{:S(2)}) collective-permute-start(bf16[36,2048]{1,0:T(8,128)(2,1)S(1)} %pad_maximum_fusion.refs_0_), channel_id=1, source_target_pairs={{0,4},{4,0},{8,12},{12,8},{1,5},{5,1},{9,13},{13,9},{2,6},{6,2},{1... | collective-permute-start | bytes 442376 | tf_op jit(solution)/shard_map/ppermute | solution.py:319
  7.8 5.1 %shard_map.77.refs_4_ = bf16[14736,2048]{1,0:T(8,128)(2,1)S(1)} custom-call(s32[10]{0:T(128)} %stack.43.refs_0_.refs_4_.refs_1_.refs_2_, bf16[7392,2048]{1,0:T(8,128)(2,1)} %bitcast.26, bf16[7392,2048]{1,0:T(8,128)(2,1)} %bitcast.37, bf16[7392,2048]{1,0:T(8,128)(2,1)} %bitcast.48), custom_call_target="tpu_custom_call" | custom-call | flops 2000000000 | tf_op jit(solution)/shard_map/pallas_call | solution.py:75
  14.1 4.9 %shard_map.78.refs_5_ = bf16[14736,2048]{1,0:T(8,128)(2,1)S(1)} custom-call(s32[10]{0:T(128)} %stack.43.refs_0_.refs_4_.refs_1_.refs_2_, bf16[7392,2048]{1,0:T(8,128)(2,1)} %bitcast.27, bf16[7392,2048]{1,0:T(8,128)(2,1)} %bitcast.38, bf16[7392,2048]{1,0:T(8,128)(2,1)} %bitcast.49, ...), custom_call_target="tpu_custom_call", output_to_operand_aliasing={{}: (4, {})} | custom-call | flops 2000000000 | tf_op jit(solution)/shard_map/pallas_call | solution.py:75
  19.2 2.0 %shard_map.79.refs_4_ = bf16[14736,2048]{1,0:T(8,128)(2,1)S(1)} custom-call(bf16[36,2048]{1,0:T(8,128)(2,1)} %copy-done, bf16[36,2048]{1,0:T(8,128)(2,1)} %collective-permute-done.refs_1_, bf16[36,2048]{1,0:T(8,128)(2,1)} %collective-permute-done.1.refs_2_, bf16[36,2048]{1,0:T(8,128)(2,1)} %collective-permute-done.2.refs_3_, ...), custom_call_target="tpu_custom_call", output_to_operand_aliasing={{}: (5, {})} | custom-call | flops 2000000000 | tf_op jit(solution)/shard_map/pallas_call | solution.py:75
  21.2 5.5 %shard_map.80 = (f32[240,960]{1,0:T(8,128)}, bf16[14736,2048]{1,0:T(8,128)(2,1)S(1)}) custom-call(s32[10]{0:T(128)} %stack.43.refs_0_.refs_4_.refs_1_.refs_2_, bf16[7392,2048]{1,0:T(8,128)(2,1)} %bitcast.28, bf16[7392,2048]{1,0:T(8,128)(2,1)} %bitcast.39, bf16[7392,2048]{1,0:T(8,128)(2,1)} %bitcast.50, ...), custom_call_target="tpu_custom_call", output_to_operand_aliasing={{1}: (4, {})} | custom-call | flops 2000000000 | tf_op jit(solution)/shard_map/pallas_call | solution.py:75
  26.8 5.2 %shard_map.81 = (f32[240,896]{1,0:T(8,128)}, bf16[14736,2048]{1,0:T(8,128)(2,1)S(1)}) custom-call(s32[10]{0:T(128)} %stack.43.refs_0_.refs_4_.refs_1_.refs_2_, bf16[7392,2048]{1,0:T(8,128)(2,1)} %bitcast.29, bf16[7392,2048]{1,0:T(8,128)(2,1)} %bitcast.40, bf16[7392,2048]{1,0:T(8,128)(2,1)} %bitcast.51, ...), custom_call_target="tpu_custom_call", output_to_operand_aliasing={{1}: (4, {})} | custom-call | flops 2000000000 | tf_op jit(solution)/shard_map/pallas_call | solution.py:75
  32.6 6.4 %shard_map.82 = (bf16[240,960]{1,0:T(8,128)(2,1)}, bf16[14736,2048]{1,0:T(8,128)(2,1)S(1)}) custom-call(f32[240,960]{1,0:T(8,128)} %collective-permute-done.4.refs_0_, s32[10]{0:T(128)} %stack.43.refs_0_.refs_4_.refs_1_.refs_2_, bf16[7392,2048]{1,0:T(8,128)(2,1)} %bitcast.30, bf16[7392,2048]{1,0:T(8,128)(2,1)} %bitcast.41, ...), custom_call_target="tpu_custom_call", output_to_operand_aliasing={{1}: (5, {})} | custom-call | flops 2000000000 | tf_op jit(solution)/shard_map/pallas_call | solution.py:75
  39.1 1.6 %collective-permute-start.8 = (bf16[240,960]{1,0:T(8,128)(2,1)}, bf16[240,960]{1,0:T(8,128)(2,1)}, u32[]{:S(2)}, u32[]{:S(2)}) collective-permute-start(bf16[240,960]{1,0:T(8,128)(2,1)} %get-tuple-element.40), channel_id=1, source_target_pairs={{0,2},{1,3},{2,0},{3,1},{4,6},{5,7},{6,4},{7,5},{8,10},{9,11},{10,... | collective-permute-start | bytes 1382408 | tf_op jit(solution)/shard_map/ppermute | solution.py:324
  40.7 8.5 %shard_map.83 = (bf16[240,896]{1,0:T(8,128)(2,1)}, f32[96,960]{1,0:T(8,128)}, f32[96,960]{1,0:T(8,128)}, f32[48,960]{1,0:T(8,128)}, bf16[14736,2048]{1,0:T(8,128)(2,1)S(1)}) custom-call(f32[240,896]{1,0:T(8,128)} %collective-permute-done.3.refs_0_, s32[10]{0:T(128)} %stack.43.refs_0_.refs_4_.refs_1_.refs_2_, ...), custom_call_target="tpu_custom_call", output_to_operand_aliasing={{4}: (5, {})} | custom-call | flops 4000000000 | tf_op jit(solution)/shard_map/pallas_call | solution.py:75
  50.4 5.5 %shard_map.84 = (f32[96,896]{1,0:T(8,128)}, f32[96,896]{1,0:T(8,128)}, f32[48,896]{1,0:T(8,128)}, bf16[14736,2048]{1,0:T(8,128)(2,1)S(1)}) custom-call(s32[10]{0:T(128)} %stack.43.refs_0_.refs_4_.refs_1_.refs_2_, bf16[7392,2048]{1,0:T(8,128)(2,1)} %bitcast.32, bf16[7392,2048]{1,0:T(8,128)(2,1)} %bitcast.43, ...), custom_call_target="tpu_custom_call", output_to_operand_aliasing={{3}: (4, {})} | custom-call | flops 2000000000 | tf_op jit(solution)/shard_map/pallas_call | solution.py:75
  56.6 6.7 %shard_map.85 = (bf16[144,960]{1,0:T(8,128)(2,1)}, bf16[14736,2048]{1,0:T(8,128)(2,1)S(1)}) custom-call(f32[96,960]{1,0:T(8,128)} %collective-permute-done.5.refs_0_, f32[96,960]{1,0:T(8,128)} %collective-permute-done.6.refs_1_, f32[48,960]{1,0:T(8,128)} %collective-permute-done.7.refs_2_, ...), custom_call_target="tpu_custom_call", output_to_operand_aliasing={{1}: (8, {})} | custom-call | flops 4000000000 | tf_op jit(solution)/shard_map/pallas_call | solution.py:75
  63.7 1.5 %collective-permute-start.9 = (bf16[144,960]{1,0:T(8,128)(2,1)}, bf16[144,960]{1,0:T(8,128)(2,1)}, u32[]{:S(2)}, u32[]{:S(2)}) collective-permute-start(bf16[144,960]{1,0:T(8,128)(2,1)} %get-tuple-element.43), channel_id=1, source_target_pairs={{0,2},{1,3},{2,0},{3,1},{4,6},{5,7},{6,4},{7,5},{8,10},{9,11},{10,... | collective-permute-start | bytes 829448 | tf_op jit(solution)/shard_map/ppermute | solution.py:324
  65.3 6.4 %shard_map.86 = (bf16[144,896]{1,0:T(8,128)(2,1)}, bf16[14736,2048]{1,0:T(8,128)(2,1)S(1)}) custom-call(f32[96,896]{1,0:T(8,128)} %collective-permute-done.11.refs_0_, f32[96,896]{1,0:T(8,128)} %collective-permute-done.12.refs_1_, f32[48,896]{1,0:T(8,128)} %copy-done.3, ...), custom_call_target="tpu_custom_call", output_to_operand_aliasing={{1}: (8, {})} | custom-call | flops 4000000000 | tf_op jit(solution)/shard_map/pallas_call | solution.py:75
  73.1 6.3 %shard_map.87.refs_6_ = bf16[14736,2048]{1,0:T(8,128)(2,1)S(1)} custom-call(bf16[144,960]{1,0:T(8,128)(2,1)} %collective-permute-done.10.refs_0_, bf16[144,960]{1,0:T(8,128)(2,1)} %collective-permute-done.9.refs_1_, s32[10]{0:T(128)} %stack.43.refs_0_.refs_4_.refs_1_.refs_2_, bf16[7392,2048]{1,0:T(8,128)(2,1)} %bitcast.35, ...), custom_call_target="tpu_custom_call", output_to_operand_aliasing={{}: (6, {})} | custom-call | flops 2000000000 | tf_op jit(solution)/shard_map/pallas_call | solution.py:75
  80.1 6.0 %shard_map.88.refs_3_ = bf16[14736,2048]{1,0:T(8,128)(2,1)S(1)} custom-call(bf16[144,896]{1,0:T(8,128)(2,1)} %collective-permute-done.18.refs_0_, bf16[144,896]{1,0:T(8,128)(2,1)} %collective-permute-done.16.refs_1_, s32[10]{0:T(128)} %stack.43.refs_0_.refs_4_.refs_1_.refs_2_, bf16[7392,2048]{1,0:T(8,128)(2,1)} %bitcast.36, ...), custom_call_target="tpu_custom_call", output_to_operand_aliasing={{}: (6, {})} | custom-call | flops 2000000000 | tf_op jit(solution)/shard_map/pallas_call | solution.py:75
  86.2 4.0 %shard_map.89 = (f32[24,2048]{1,0:T(8,128)}, bf16[24,2048]{1,0:T(8,128)(2,1)}, bf16[14736,2048]{1,0:T(8,128)(2,1)S(1)}) custom-call(bf16[144,960]{1,0:T(8,128)(2,1)} %collective-permute-done.15.refs_0_, bf16[144,896]{1,0:T(8,128)(2,1)} %collective-permute-done.17.refs_1_, s32[10]{0:T(128)} %stack.43.refs_0_.refs_4_.refs_1_.refs_2_, ...), custom_call_target="tpu_custom_call", output_to_operand_aliasing={{2}: (3, {})} | custom-call | flops 2000000000 | tf_op jit(solution)/shard_map/pallas_call | solution.py:75
  90.2 1.4 %collective-permute-start.19 = (bf16[24,2048]{1,0:T(8,128)(2,1)}, bf16[24,2048]{1,0:T(8,128)(2,1)}, u32[]{:S(2)}, u32[]{:S(2)}) collective-permute-start(bf16[24,2048]{1,0:T(8,128)(2,1)} %get-tuple-element.54), channel_id=1, source_target_pairs={{0,4},{4,0},{8,12},{12,8},{1,5},{5,1},{9,13},{13,9},{2,6},{6,2},{1... | collective-permute-start | bytes 294920 | tf_op jit(solution)/shard_map/ppermute | solution.py:319
  91.6 5.2 %shard_map.90 = (f32[24,2048]{1,0:T(8,128)}, bf16[24,2048]{1,0:T(8,128)(2,1)}, bf16[14736,2048]{1,0:T(8,128)(2,1)S(1)}) custom-call(bf16[144,960]{1,0:T(8,128)(2,1)} %collective-permute-done.15.refs_0_, bf16[144,896]{1,0:T(8,128)(2,1)} %collective-permute-done.17.refs_1_, s32[10]{0:T(128)} %stack.43.refs_0_.refs_4_.refs_1_.refs_2_, ...), custom_call_target="tpu_custom_call", output_to_operand_aliasing={{2}: (3, {})} | custom-call | flops 2000000000 | tf_op jit(solution)/shard_map/pallas_call | solution.py:75
  97.6 1.0 convert_add_fusion.1
  98.6 4.3 %collective-permute-start.21 = (bf16[12,2048]{1,0:T(8,128)(2,1)S(1)}, bf16[12,2048]{1,0:T(8,128)(2,1)S(1)}, u32[]{:S(2)}, u32[]{:S(2)}) collective-permute-start(bf16[12,2048]{1,0:T(8,128)(2,1)S(1)} %slice.27), channel_id=1, source_target_pairs={{0,24},{4,28},{8,16},{12,20},{16,8},{20,12},{24,0},{28,4},{1,25},{... | collective-permute-start | bytes 147464 | tf_op jit(solution)/shard_map/ppermute | solution.py:334
  104.4 3.7 %collective-permute-start.24 = (bf16[12,2048]{1,0:T(8,128)(2,1)S(1)}, bf16[12,2048]{1,0:T(8,128)(2,1)S(1)}, u32[]{:S(2)}, u32[]{:S(2)}) collective-permute-start(bf16[12,2048]{1,0:T(8,128)(2,1)S(1)} %slice.26), channel_id=1, source_target_pairs={{0,24},{4,28},{8,16},{12,20},{16,8},{20,12},{24,0},{28,4},{1,25},{... | collective-permute-start | bytes 147464 | tf_op jit(solution)/shard_map/ppermute | solution.py:334
  109.3 1.4 %collective-permute-done.24 = bf16[12,2048]{1,0:T(8,128)(2,1)S(1)} collective-permute-done((bf16[12,2048]{1,0:T(8,128)(2,1)S(1)}, bf16[12,2048]{1,0:T(8,128)(2,1)S(1)}, u32[]{:S(2)}, u32[]{:S(2)}) %collective-permute-start.24) | collective-permute-done | bytes 49184 | tf_op jit(solution)/shard_map/ppermute | solution.py:334
  110.7 2.4 %collective-permute-done.23 = f32[12,2048]{1,0:T(8,128)S(1)} collective-permute-done((f32[12,2048]{1,0:T(8,128)S(1)}, f32[12,2048]{1,0:T(8,128)S(1)}, u32[]{:S(2)}, u32[]{:S(2)}) %collective-permute-start.23) | collective-permute-done | bytes 98336 | tf_op jit(solution)/shard_map/ppermute | solution.py:334
  (58 shorter events, 12.0 us)
Async XLA Ops:
  1.6 12.0 %collective-permute-start = (bf16[36,2048]{1,0:T(8,128)(2,1)S(1)}, bf16[36,2048]{1,0:T(8,128)(2,1)}, u32[]{:S(2)}, u32[]{:S(2)}) collective-permute-start(bf16[36,2048]{1,0:T(8,128)(2,1)S(1)} %pad_maximum_fusion.refs_0_), channel_id=1, source_target_pairs={{0,8},{4,12},{8,0},{12,4},{1,9},{5,13},{9,1},{13,5},{2,10},{6,14},... | collective-permute-start | bytes 442376 | tf_op jit(solution)/shard_map/ppermute | solution.py:319
  6.3 12.8 %collective-permute-start.1 = (bf16[36,2048]{1,0:T(8,128)(2,1)S(1)}, bf16[36,2048]{1,0:T(8,128)(2,1)}, u32[]{:S(2)}, u32[]{:S(2)}) collective-permute-start(bf16[36,2048]{1,0:T(8,128)(2,1)S(1)} %pad_maximum_fusion.refs_0_), channel_id=1, source_target_pairs={{0,4},{4,0},{8,12},{12,8},{1,5},{5,1},{9,13},{13,9},{2,6},{6,2},{1... | collective-permute-start | bytes 442376 | tf_op jit(solution)/shard_map/ppermute | solution.py:319
  13.6 5.6 %collective-permute-start.2 = (bf16[36,2048]{1,0:T(8,128)(2,1)}, bf16[36,2048]{1,0:T(8,128)(2,1)}, u32[]{:S(2)}, u32[]{:S(2)}) collective-permute-start(bf16[36,2048]{1,0:T(8,128)(2,1)} %collective-permute-done.refs_1_), channel_id=1, source_target_pairs={{0,4},{4,0},{8,12},{12,8},{1,5},{5,1},{9,13},{13,9},{2,6},{6,2},{1... | collective-permute-start | bytes 442376 | tf_op jit(solution)/shard_map/ppermute | solution.py:319
  26.7 5.9 %collective-permute-start.4 = (f32[240,960]{1,0:T(8,128)}, f32[240,960]{1,0:T(8,128)}, u32[]{:S(2)}, u32[]{:S(2)}) collective-permute-start(f32[240,960]{1,0:T(8,128)} %get-tuple-element.34), channel_id=1, source_target_pairs={{0,1},{1,0},{2,3},{3,2},{4,5},{5,4},{6,7},{7,6},{8,9},{9,8},{10,11... | collective-permute-start | bytes 2764808 | tf_op jit(solution)/shard_map/ppermute | solution.py:319
  32.1 8.6 %collective-permute-start.3 = (f32[240,896]{1,0:T(8,128)}, f32[240,896]{1,0:T(8,128)}, u32[]{:S(2)}, u32[]{:S(2)}) collective-permute-start(f32[240,896]{1,0:T(8,128)} %get-tuple-element.33), channel_id=1, source_target_pairs={{0,1},{1,0},{2,3},{3,2},{4,5},{5,4},{6,7},{7,6},{8,9},{9,8},{10,11... | collective-permute-start | bytes 2580488 | tf_op jit(solution)/shard_map/ppermute | solution.py:319
  39.1 17.5 %collective-permute-start.8 = (bf16[240,960]{1,0:T(8,128)(2,1)}, bf16[240,960]{1,0:T(8,128)(2,1)}, u32[]{:S(2)}, u32[]{:S(2)}) collective-permute-start(bf16[240,960]{1,0:T(8,128)(2,1)} %get-tuple-element.40), channel_id=1, source_target_pairs={{0,2},{1,3},{2,0},{3,1},{4,6},{5,7},{6,4},{7,5},{8,10},{9,11},{10,... | collective-permute-start | bytes 1382408 | tf_op jit(solution)/shard_map/ppermute | solution.py:324
  49.2 6.9 %collective-permute-start.5 = (f32[96,960]{1,0:T(8,128)}, f32[96,960]{1,0:T(8,128)}, u32[]{:S(2)}, u32[]{:S(2)}) collective-permute-start(f32[96,960]{1,0:T(8,128)} %get-tuple-element.37), channel_id=1, source_target_pairs={{0,1},{1,0},{2,3},{3,2},{4,5},{5,4},{6,7},{7,6},{8,9},{9,8},{10,11... | collective-permute-start | bytes 1105928 | tf_op jit(solution)/shard_map/ppermute | solution.py:319
  49.3 7.1 %collective-permute-start.6 = (f32[96,960]{1,0:T(8,128)}, f32[96,960]{1,0:T(8,128)}, u32[]{:S(2)}, u32[]{:S(2)}) collective-permute-start(f32[96,960]{1,0:T(8,128)} %get-tuple-element.38), channel_id=1, source_target_pairs={{0,1},{1,0},{2,3},{3,2},{4,5},{5,4},{6,7},{7,6},{8,9},{9,8},{10,11... | collective-permute-start | bytes 1105928 | tf_op jit(solution)/shard_map/ppermute | solution.py:319
  49.8 6.0 %collective-permute-start.7 = (f32[48,960]{1,0:T(8,128)}, f32[48,960]{1,0:T(8,128)}, u32[]{:S(2)}, u32[]{:S(2)}) collective-permute-start(f32[48,960]{1,0:T(8,128)} %get-tuple-element.39), channel_id=1, source_target_pairs={{0,1},{1,0},{2,3},{3,2},{4,5},{5,4},{6,7},{7,6},{8,9},{9,8},{10,11... | collective-permute-start | bytes 552968 | tf_op jit(solution)/shard_map/ppermute | solution.py:319
  49.9 15.4 %collective-permute-start.14 = (bf16[240,896]{1,0:T(8,128)(2,1)}, bf16[240,896]{1,0:T(8,128)(2,1)}, u32[]{:S(2)}, u32[]{:S(2)}) collective-permute-start(bf16[240,896]{1,0:T(8,128)(2,1)} %get-tuple-element.47), channel_id=1, source_target_pairs={{0,2},{1,3},{2,0},{3,1},{4,6},{5,7},{6,4},{7,5},{8,10},{9,11},{10,... | collective-permute-start | bytes 1290248 | tf_op jit(solution)/shard_map/ppermute | solution.py:324
  55.9 7.9 %collective-permute-start.13 = (f32[48,896]{1,0:T(8,128)}, f32[48,896]{1,0:T(8,128)S(1)}, u32[]{:S(2)}, u32[]{:S(2)}) collective-permute-start(f32[48,896]{1,0:T(8,128)} %get-tuple-element.46), channel_id=1, source_target_pairs={{0,1},{1,0},{2,3},{3,2},{4,5},{5,4},{6,7},{7,6},{8,9},{9,8},{10,11... | collective-permute-start | bytes 516104 | tf_op jit(solution)/shard_map/ppermute | solution.py:319
  56.1 9.2 %collective-permute-start.11 = (f32[96,896]{1,0:T(8,128)}, f32[96,896]{1,0:T(8,128)}, u32[]{:S(2)}, u32[]{:S(2)}) collective-permute-start(f32[96,896]{1,0:T(8,128)} %get-tuple-element.44), channel_id=1, source_target_pairs={{0,1},{1,0},{2,3},{3,2},{4,5},{5,4},{6,7},{7,6},{8,9},{9,8},{10,11... | collective-permute-start | bytes 1032200 | tf_op jit(solution)/shard_map/ppermute | solution.py:319
  56.4 8.8 %collective-permute-start.12 = (f32[96,896]{1,0:T(8,128)}, f32[96,896]{1,0:T(8,128)}, u32[]{:S(2)}, u32[]{:S(2)}) collective-permute-start(f32[96,896]{1,0:T(8,128)} %get-tuple-element.45), channel_id=1, source_target_pairs={{0,1},{1,0},{2,3},{3,2},{4,5},{5,4},{6,7},{7,6},{8,9},{9,8},{10,11... | collective-permute-start | bytes 1032200 | tf_op jit(solution)/shard_map/ppermute | solution.py:319
  63.3 9.1 %collective-permute-start.10 = (bf16[144,960]{1,0:T(8,128)(2,1)}, bf16[144,960]{1,0:T(8,128)(2,1)}, u32[]{:S(2)}, u32[]{:S(2)}) collective-permute-start(bf16[144,960]{1,0:T(8,128)(2,1)} %get-tuple-element.43), channel_id=1, source_target_pairs={{0,1},{1,0},{2,3},{3,2},{4,5},{5,4},{6,7},{7,6},{8,9},{9,8},{10,11... | collective-permute-start | bytes 829448 | tf_op jit(solution)/shard_map/ppermute | solution.py:319
  63.7 9.4 %collective-permute-start.9 = (bf16[144,960]{1,0:T(8,128)(2,1)}, bf16[144,960]{1,0:T(8,128)(2,1)}, u32[]{:S(2)}, u32[]{:S(2)}) collective-permute-start(bf16[144,960]{1,0:T(8,128)(2,1)} %get-tuple-element.43), channel_id=1, source_target_pairs={{0,2},{1,3},{2,0},{3,1},{4,6},{5,7},{6,4},{7,5},{8,10},{9,11},{10,... | collective-permute-start | bytes 829448 | tf_op jit(solution)/shard_map/ppermute | solution.py:324
  71.7 8.4 %collective-permute-start.16 = (bf16[144,896]{1,0:T(8,128)(2,1)}, bf16[144,896]{1,0:T(8,128)(2,1)}, u32[]{:S(2)}, u32[]{:S(2)}) collective-permute-start(bf16[144,896]{1,0:T(8,128)(2,1)} %get-tuple-element.51), channel_id=1, source_target_pairs={{0,2},{1,3},{2,0},{3,1},{4,6},{5,7},{6,4},{7,5},{8,10},{9,11},{10,... | collective-permute-start | bytes 774152 | tf_op jit(solution)/shard_map/ppermute | solution.py:324
  72.4 7.7 %collective-permute-start.18 = (bf16[144,896]{1,0:T(8,128)(2,1)}, bf16[144,896]{1,0:T(8,128)(2,1)}, u32[]{:S(2)}, u32[]{:S(2)}) collective-permute-start(bf16[144,896]{1,0:T(8,128)(2,1)} %get-tuple-element.51), channel_id=1, source_target_pairs={{0,1},{1,0},{2,3},{3,2},{4,5},{5,4},{6,7},{7,6},{8,9},{9,8},{10,11... | collective-permute-start | bytes 774152 | tf_op jit(solution)/shard_map/ppermute | solution.py:319
  79.5 6.7 %collective-permute-start.15 = (bf16[144,960]{1,0:T(8,128)(2,1)}, bf16[144,960]{1,0:T(8,128)(2,1)}, u32[]{:S(2)}, u32[]{:S(2)}) collective-permute-start(bf16[144,960]{1,0:T(8,128)(2,1)} %collective-permute-done.9.refs_1_), channel_id=1, source_target_pairs={{0,1},{1,0},{2,3},{3,2},{4,5},{5,4},{6,7},{7,6},{8,9},{9,8},{10,11... | collective-permute-start | bytes 829448 | tf_op jit(solution)/shard_map/ppermute | solution.py:319
  80.1 6.0 %collective-permute-start.17 = (bf16[144,896]{1,0:T(8,128)(2,1)}, bf16[144,896]{1,0:T(8,128)(2,1)}, u32[]{:S(2)}, u32[]{:S(2)}) collective-permute-start(bf16[144,896]{1,0:T(8,128)(2,1)} %collective-permute-done.16.refs_1_), channel_id=1, source_target_pairs={{0,1},{1,0},{2,3},{3,2},{4,5},{5,4},{6,7},{7,6},{8,9},{9,8},{10,11... | collective-permute-start | bytes 774152 | tf_op jit(solution)/shard_map/ppermute | solution.py:319
  90.2 7.4 %collective-permute-start.19 = (bf16[24,2048]{1,0:T(8,128)(2,1)}, bf16[24,2048]{1,0:T(8,128)(2,1)}, u32[]{:S(2)}, u32[]{:S(2)}) collective-permute-start(bf16[24,2048]{1,0:T(8,128)(2,1)} %get-tuple-element.54), channel_id=1, source_target_pairs={{0,4},{4,0},{8,12},{12,8},{1,5},{5,1},{9,13},{13,9},{2,6},{6,2},{1... | collective-permute-start | bytes 294920 | tf_op jit(solution)/shard_map/ppermute | solution.py:319
  96.8 6.6 %collective-permute-start.22 = (bf16[24,2048]{1,0:T(8,128)(2,1)}, bf16[24,2048]{1,0:T(8,128)(2,1)S(1)}, u32[]{:S(2)}, u32[]{:S(2)}) collective-permute-start(bf16[24,2048]{1,0:T(8,128)(2,1)} %get-tuple-element.57), channel_id=1, source_target_pairs={{0,4},{4,0},{8,12},{12,8},{1,5},{5,1},{9,13},{13,9},{2,6},{6,2},{1... | collective-permute-start | bytes 294920 | tf_op jit(solution)/shard_map/ppermute | solution.py:319
  98.6 10.0 %collective-permute-start.21 = (bf16[12,2048]{1,0:T(8,128)(2,1)S(1)}, bf16[12,2048]{1,0:T(8,128)(2,1)S(1)}, u32[]{:S(2)}, u32[]{:S(2)}) collective-permute-start(bf16[12,2048]{1,0:T(8,128)(2,1)S(1)} %slice.27), channel_id=1, source_target_pairs={{0,24},{4,28},{8,16},{12,20},{16,8},{20,12},{24,0},{28,4},{1,25},{... | collective-permute-start | bytes 147464 | tf_op jit(solution)/shard_map/ppermute | solution.py:334
  102.9 5.8 %collective-permute-start.20 = (f32[12,2048]{1,0:T(8,128)S(1)}, f32[12,2048]{1,0:T(8,128)S(1)}, u32[]{:S(2)}, u32[]{:S(2)}) collective-permute-start(f32[12,2048]{1,0:T(8,128)S(1)} %slice_add_fusion.1), channel_id=1, source_target_pairs={{0,16},{4,20},{8,24},{12,28},{16,0},{20,4},{24,8},{28,12},{1,17},{... | collective-permute-start | bytes 294920 | tf_op jit(solution)/shard_map/ppermute | solution.py:334
  104.4 6.3 %collective-permute-start.24 = (bf16[12,2048]{1,0:T(8,128)(2,1)S(1)}, bf16[12,2048]{1,0:T(8,128)(2,1)S(1)}, u32[]{:S(2)}, u32[]{:S(2)}) collective-permute-start(bf16[12,2048]{1,0:T(8,128)(2,1)S(1)} %slice.26), channel_id=1, source_target_pairs={{0,24},{4,28},{8,16},{12,20},{16,8},{20,12},{24,0},{28,4},{1,25},{... | collective-permute-start | bytes 147464 | tf_op jit(solution)/shard_map/ppermute | solution.py:334
  (5 other events, 48.6 us)

commit v4 on v3

--- a/solution.py
+++ b/solution.py
@@ -14,7 +14,7 @@
 VM = pl.BlockSpec(memory_space=pltpu.VMEM)
 HBM = pl.BlockSpec(memory_space=pltpu.HBM)
 SM = pl.BlockSpec(memory_space=pltpu.SMEM)
-STEP = 512
+STEP = 384
 SLOTS = 5
 BEGUN = 2
 SPLIT = (2, 2, 1)
@@ -261,20 +261,21 @@
                 scratch.append(pltpu.VMEM(part.shape, F32))
         got = [piece.shape[0] // tokens for piece in more]
         static.append(dict(at=at, rows=rows, got=got, others=len(others), leave=leave, entry=entry, fresh=fresh))
-    weight = sum(1 if job["entry"] is None else 2 for job in static)
+    weight = sum(1 if job["entry"] is None else 6 for job in static)
     body = functools.partial(project_body, static, tokens)
     *outs, arena = call(body, operands, shapes, scratch, arena, loads, table, stored, weight=weight)
     return outs, arena
 
 
-def expand_body(slots, parts, ends, tokens, loads, *refs):
-    operands, _, outs, arena, scratch, copies = split(refs, loads, len(slots), 2 * ends)
+def expand_body(slots, devices, tokens, loads, *refs):
+    operands, _, outs, arena, scratch, copies = split(refs, loads, len(slots), 2 if devices else 0)
     in_sems, *held = scratch
     arrivals = [pltpu.make_async_copy(operand, held[i], in_sems.at[i]) for i, operand in enumerate(operands)]
     begin(arrivals)
     leaving = []
-    if ends:
-        out_sems, *leave_refs = held[len(slots) :]
+    if devices:
+        out_sems, total_ref, gone_ref = held[len(slots) :]
+        t = tokens // devices
     for n, slot in enumerate(slots):
         if not n and len(slots) > 1:
             end(arrivals)
@@ -285,32 +286,34 @@
             end(arrivals)
         for m, (low, size) in enumerate(spans(arena.shape[1])):
             piece = pl.ds(low, size)
-            for part in parts:
+            for part in (0, 1):
                 value = products(arena, [held[n]], [slot], part, tokens, piece)
                 value = value + kept_sum(arena, part, tokens, piece)
-                if not ends or n < len(slots) - 1:
+                if not devices or n < len(slots) - 1:
                     keep(arena, value, part, tokens, piece)
                     continue
-                leave_refs[0][:, piece] = value[: tokens // 2]
-                leave_refs[1][:, piece] = value[tokens // 2 :].astype(BF16)
-                for k, source in enumerate(leave_refs):
-                    copy = pltpu.make_async_copy(source.at[:, piece], outs[k].at[:, piece], out_sems.at[k, m])
+                for i in range(devices):
+                    total_ref[pl.ds((2 * i + part) * t, t), piece] = value[i * t : (i + 1) * t]
+            if devices and n == len(slots) - 1:
+                gone_ref[:, piece] = total_ref[pl.ds(tokens, tokens), piece].astype(BF16)
+                for k, source in enumerate((total_ref.at[pl.ds(0, tokens), piece], gone_ref.at[:, piece])):
+                    copy = pltpu.make_async_copy(source, outs[k].at[:, piece], out_sems.at[k, m])
                     leaving.append(copy)
                     copy.start()
     end(leaving)
     end(copies)
 
 
-def expand(tokens, held, arena, slots, parts, ends, loads, table, stored):
+def expand(tokens, held, arena, slots, devices, loads, table, stored):
     width = arena.shape[1]
     shapes = []
     scratch = [pltpu.SemaphoreType.DMA((len(held),))]
     scratch += [pltpu.VMEM(operand.shape, operand.dtype) for operand in held]
-    if ends:
-        shapes = [jax.ShapeDtypeStruct((tokens // 2, width), dtype) for dtype in (F32, BF16)]
+    if devices:
+        shapes = [jax.ShapeDtypeStruct((tokens, width), dtype) for dtype in (F32, BF16)]
         scratch.append(pltpu.SemaphoreType.DMA((2, len(spans(width)))))
-        scratch += [pltpu.VMEM(shape.shape, shape.dtype) for shape in shapes]
-    body = functools.partial(expand_body, slots, parts, ends, tokens)
+        scratch += [pltpu.VMEM((2 * tokens, width), F32), pltpu.VMEM((tokens, width), BF16)]
+    body = functools.partial(expand_body, slots, devices, tokens)
     *outs, arena = call(body, held, shapes, scratch, arena, loads, table, stored)
     return outs, arena
 
@@ -339,8 +342,14 @@
     return [int(format(n, f"0{bits}b")[::-1], 2) if bits else 0 for n in range(count)]
 
 
-def finish(kept, got, own, step):
+def finish(kept, got, t, ahead, back):
     count = lax.axis_size("tx")
+
+    def across(value, bit):
+        if lax.axis_size("pipe") == 2:
+            return cross_pipe(value, 1, bit)
+        return jnp.concatenate([cross_pipe(value[:t], 1, bit), cross_pipe(value[t:], -1, bit)])
+
     bit = 1
     while 2 * bit < count:
         kept = kept + got.astype(F32)
@@ -349,8 +358,10 @@
         bit *= 2
         if 2 * bit < count:
             got = swap(gone, "tx", bit)
-    near = cross_pipe(kept + own.astype(F32), step, 0)
-    return (near + cross_pipe(gone, step, bit).astype(F32)).astype(BF16)
+    far = across(gone, bit)
+    near = across(kept.astype(BF16), 0)
+    total = near.astype(F32) + far.astype(F32)
+    return (total[:t] + ahead.astype(F32)).astype(BF16), (total[t:] + back.astype(F32)).astype(BF16)
 
 
 def gather_body(t, count, loads, *refs):
@@ -385,6 +396,9 @@
     if count > 1:
         near = swap(after(own, table), "tx", 1)
     arena = load(shape, loads[:-1], table, stored)
+    later = after(own, arena)
+    ahead = cross_pipe(later, 1, 0)
+    back = ahead if lax.axis_size("pipe") == 2 else cross_pipe(later, -1, 0)
     while bit > 1:
         for i in list(blocks):
             blocks[i ^ bit] = swap(blocks[i], "tx", bit)
@@ -398,7 +412,8 @@
     order = block_order(count)
     operands = [blocks[i] for i in order]
     body = functools.partial(gather_body, t, count)
-    return call(body, operands, [], [], arena, [], table, stored, VM)[0]
+    arena = call(body, operands, [], [], after(arena, (ahead, back)), [], table, stored, VM)[0]
+    return arena, ahead[:t], back[2 * t :]
 
 
 def residency(groups, quiet, slots, first):
@@ -485,7 +500,7 @@
 
     tokens = tx * section_input.shape[1]
     shape = (SLOTS * most + 7 * tokens, stored[0].shape[1])
-    arena = gathered(section_input[0], saved_input[0], out_grad[0], shape, *request(begun))
+    arena, ahead, back = gathered(section_input[0], saved_input[0], out_grad[0], shape, *request(begun))
     passed, arrived, h, forwarded = {}, {}, {}, chips == 1
     for n, (kind, group) in enumerate(steps):
         slots = [(slot * most, subs[piece[2]][1]) for slot, piece in zip(slot_at[n], group)]
@@ -497,7 +512,7 @@
                 if mine and not k:
                     jobs.append((slot, more, arrived.get(sub, []), (), F32, len(entries) + sub, not sub))
                 else:
-                    leave, dtype = ((5,), BF16) if mine else ((5,) if k else SPLIT, F32)
+                    leave, dtype = ((5,), BF16) if mine else ((5,) if k or sub else SPLIT, F32)
                     jobs.append((slot, more, [], leave, dtype, None, False))
             parts, arena = project(tokens, arena, jobs, *loads)
             for k, mine, sub in group:
@@ -510,11 +525,11 @@
                 elif mine:
                     arrived.setdefault(sub, []).append(to_chip(parts.pop(0), k))
                 else:
-                    count = 1 if k else len(SPLIT)
+                    count = 1 if k or sub else len(SPLIT)
                     passed[k, sub] = [swap(parts.pop(0), "ty", 1) for _ in range(count)]
         elif kind == "expand":
             held = [h[piece] for piece in group]
-            _, arena = expand(tokens, held, arena, slots, (0, 1), False, *loads)
+            _, arena = expand(tokens, held, arena, slots, 0, *loads)
             if not forwarded and len(h) == len(subs) * (chips + 1):
                 forwarded = True
                 for i in range(1, chips):
@@ -526,11 +541,9 @@
                     for j in range(len(subs)):
                         h[i, False, j] = swap(h[i, True, j], "ty", 1)
             held = [h[piece] for piece in group]
-            (kept, gone), arena = expand(tokens, held, arena, slots, (0,), True, *loads)
+            (kept, gone), _ = expand(tokens, held, arena, slots, tx, *loads)
             got = swap(gone, "tx", 1)
-            (kept_back, gone), _ = expand(tokens, held, arena, slots, (1,), True, *request([]))
-            next_input = finish(kept, got, section_input[0], 1)
-            prev_grad = finish(kept_back, swap(gone, "tx", 1), out_grad[0], -1)
+            next_input, prev_grad = finish(kept, got, section_input.shape[1], ahead, back)
     return (next_input[None], prev_grad[None])
 
 

time: 114 us -> 113 us (level)
  waiting for transfers between devices: 5.96 us -> 12.9 us
  starting transfers between devices: 24.2 us -> 19 us
  Pallas kernels: 77.8 us -> 75 us
    ppermute x17 -> x14, waiting for transfers between devices: 0.89 us -> 6.48 us  [swap(): lax.ppermute(value, axis, [(i, i ^ bit) for i in range(lax.axis_size(axis...]
    ppermute x4 -> x3, starting transfers between devices: 9.02 us -> 5.33 us  [cross_pipe(): return lax.ppermute(value, ('pipe', 'tx'), pairs)]
    pallas_call x14 -> x13, Pallas kernels: 77.8 us -> 75 us  [call(): pl.pallas_call(functools.partial(body, loads), in_specs=specs, out_specs=...]
    add x4 -> x1, other arithmetic: 2 us -> 0.02 us  [finish(): total = near.astype(F32) + far.astype(F32)]
    ppermute x17 -> x14, starting transfers between devices: 10.8 us -> 9.52 us  [swap(): lax.ppermute(value, axis, [(i, i ^ bit) for i in range(lax.axis_size(axis...]
    ppermute x4 -> x3, waiting for transfers between devices: 3.81 us -> 4.87 us  [cross_pipe(): return lax.ppermute(value, ('pipe', 'tx'), pairs)]
  transfers between devices with their start and end apart: 25 -> 21, of which waited for: 6 -> 6; matrix products, arithmetic and copies ran while one was open for 3% -> 1% of each run, Pallas kernels for 58% -> 55%
where the time goes in v4:
time: 113 us; the launch traced here: 112 us
  Pallas kernels  75 us (66%)
  starting transfers between devices  19 us (17%)
  waiting for transfers between devices  12.9 us (11%)
  other arithmetic  3.57 us (3%)
    pallas_call x13, Pallas kernels, call(): pl.pallas_call(functools.partial(body, loads), in_specs=specs, out_specs=...  75 us
    ppermute x14, starting transfers between devices, swap(): lax.ppermute(value, axis, [(i, i ^ bit) for i in range(lax.axis_size(axis...  9.52 us
    ppermute x14, waiting for transfers between devices, swap(): lax.ppermute(value, axis, [(i, i ^ bit) for i in range(lax.axis_size(axis...  6.48 us
    ppermute x3, starting transfers between devices, cross_pipe(): return lax.ppermute(value, ('pipe', 'tx'), pairs)  5.33 us
    ppermute x3, waiting for transfers between devices, cross_pipe(): return lax.ppermute(value, ('pipe', 'tx'), pairs)  4.87 us
    ppermute x4, starting transfers between devices, to_chip(): lax.ppermute(value, 'ty', [(i, (i + 2 * k) % count) for i in range(count)])  4.19 us
  transfers between devices with their start and end apart: 21, of which 6 were waited for; matrix products, arithmetic and copies ran while one was open for 1% of the time, Pallas kernels for 55%

profile of v4, /device:TPU:0, one launch (start us, length us, event | category | flops | bytes accessed | tf_op | source)
XLA Modules:
  0.0 112.0 jit_solution(10652415976614534782)
XLA Ops:
  1.6 4.1 %collective-permute-start = (bf16[36,2048]{1,0:T(8,128)(2,1)S(1)}, bf16[36,2048]{1,0:T(8,128)(2,1)}, u32[]{:S(2)}, u32[]{:S(2)}) collective-permute-start(bf16[36,2048]{1,0:T(8,128)(2,1)S(1)} %pad_maximum_fusion.refs_0_), channel_id=1, source_target_pairs={{0,8},{4,12},{8,0},{12,4},{1,9},{5,13},{9,1},{13,5},{2,10},{6,14},... | collective-permute-start | bytes 442376 | tf_op jit(solution)/shard_map/ppermute | solution.py:322
  6.4 1.6 %collective-permute-start.1 = (bf16[36,2048]{1,0:T(8,128)(2,1)S(1)}, bf16[36,2048]{1,0:T(8,128)(2,1)}, u32[]{:S(2)}, u32[]{:S(2)}) collective-permute-start(bf16[36,2048]{1,0:T(8,128)(2,1)S(1)} %pad_maximum_fusion.refs_0_), channel_id=1, source_target_pairs={{0,4},{4,0},{8,12},{12,8},{1,5},{5,1},{9,13},{13,9},{2,6},{6,2},{1... | collective-permute-start | bytes 442376 | tf_op jit(solution)/shard_map/ppermute | solution.py:322
  8.0 5.1 %shard_map.77.refs_4_ = bf16[14736,2048]{1,0:T(8,128)(2,1)S(1)} custom-call(s32[10]{0:T(128)} %stack.43.refs_0_.refs_4_.refs_1_.refs_2_, bf16[7392,2048]{1,0:T(8,128)(2,1)} %bitcast.24, bf16[7392,2048]{1,0:T(8,128)(2,1)} %bitcast.35, bf16[7392,2048]{1,0:T(8,128)(2,1)} %bitcast.46), custom_call_target="tpu_custom_call" | custom-call | flops 2000000000 | tf_op jit(solution)/shard_map/pallas_call | solution.py:75
  13.1 1.6 %collective-permute-start.3 = (bf16[36,2048]{1,0:T(8,128)(2,1)S(1)}, bf16[36,2048]{1,0:T(8,128)(2,1)}, u32[]{:S(2)}, u32[]{:S(2)}) collective-permute-start(bf16[36,2048]{1,0:T(8,128)(2,1)S(1)} %pad_maximum_fusion.refs_0_), channel_id=1, source_target_pairs={{0,16},{4,20},{8,24},{12,28},{16,0},{20,4},{24,8},{28,12},{1,17},{... | collective-permute-start | bytes 442376 | tf_op jit(solution)/shard_map/ppermute | solution.py:337
  15.1 4.9 %shard_map.78.refs_5_ = bf16[14736,2048]{1,0:T(8,128)(2,1)S(1)} custom-call(s32[10]{0:T(128)} %stack.43.refs_0_.refs_4_.refs_1_.refs_2_, bf16[7392,2048]{1,0:T(8,128)(2,1)} %bitcast.25, bf16[7392,2048]{1,0:T(8,128)(2,1)} %bitcast.36, bf16[7392,2048]{1,0:T(8,128)(2,1)} %bitcast.47, ...), custom_call_target="tpu_custom_call", output_to_operand_aliasing={{}: (4, {})} | custom-call | flops 2000000000 | tf_op jit(solution)/shard_map/pallas_call | solution.py:75
  20.3 2.2 %shard_map.79.refs_4_ = bf16[14736,2048]{1,0:T(8,128)(2,1)S(1)} custom-call(bf16[36,2048]{1,0:T(8,128)(2,1)} %copy-done, bf16[36,2048]{1,0:T(8,128)(2,1)} %collective-permute-done.refs_1_, bf16[36,2048]{1,0:T(8,128)(2,1)} %collective-permute-done.1.refs_2_, bf16[36,2048]{1,0:T(8,128)(2,1)} %collective-permute-done.2.refs_3_, ...), custom_call_target="tpu_custom_call", output_to_operand_aliasing={{}: (5, {})} | custom-call | flops 2000000000 | tf_op jit(solution)/shard_map/pallas_call | solution.py:75
  22.5 5.5 %shard_map.80 = (f32[240,960]{1,0:T(8,128)}, bf16[14736,2048]{1,0:T(8,128)(2,1)S(1)}) custom-call(s32[10]{0:T(128)} %stack.43.refs_0_.refs_4_.refs_1_.refs_2_, bf16[7392,2048]{1,0:T(8,128)(2,1)} %bitcast.26, bf16[7392,2048]{1,0:T(8,128)(2,1)} %bitcast.37, bf16[7392,2048]{1,0:T(8,128)(2,1)} %bitcast.48, ...), custom_call_target="tpu_custom_call", output_to_operand_aliasing={{1}: (4, {})} | custom-call | flops 2000000000 | tf_op jit(solution)/shard_map/pallas_call | solution.py:75
  28.1 5.2 %shard_map.81 = (f32[240,896]{1,0:T(8,128)}, bf16[14736,2048]{1,0:T(8,128)(2,1)S(1)}) custom-call(s32[10]{0:T(128)} %stack.43.refs_0_.refs_4_.refs_1_.refs_2_, bf16[7392,2048]{1,0:T(8,128)(2,1)} %bitcast.27, bf16[7392,2048]{1,0:T(8,128)(2,1)} %bitcast.38, bf16[7392,2048]{1,0:T(8,128)(2,1)} %bitcast.49, ...), custom_call_target="tpu_custom_call", output_to_operand_aliasing={{1}: (4, {})} | custom-call | flops 2000000000 | tf_op jit(solution)/shard_map/pallas_call | solution.py:75
  33.9 6.4 %shard_map.82 = (bf16[240,960]{1,0:T(8,128)(2,1)}, bf16[14736,2048]{1,0:T(8,128)(2,1)S(1)}) custom-call(f32[240,960]{1,0:T(8,128)} %collective-permute-done.5.refs_0_, s32[10]{0:T(128)} %stack.43.refs_0_.refs_4_.refs_1_.refs_2_, bf16[7392,2048]{1,0:T(8,128)(2,1)} %bitcast.28, bf16[7392,2048]{1,0:T(8,128)(2,1)} %bitcast.39, ...), custom_call_target="tpu_custom_call", output_to_operand_aliasing={{1}: (5, {})} | custom-call | flops 2000000000 | tf_op jit(solution)/shard_map/pallas_call | solution.py:75
  40.4 1.6 %collective-permute-start.9 = (bf16[240,960]{1,0:T(8,128)(2,1)}, bf16[240,960]{1,0:T(8,128)(2,1)}, u32[]{:S(2)}, u32[]{:S(2)}) collective-permute-start(bf16[240,960]{1,0:T(8,128)(2,1)} %get-tuple-element.39), channel_id=1, source_target_pairs={{0,2},{1,3},{2,0},{3,1},{4,6},{5,7},{6,4},{7,5},{8,10},{9,11},{10,... | collective-permute-start | bytes 1382408 | tf_op jit(solution)/shard_map/ppermute | solution.py:327
  41.9 8.5 %shard_map.83 = (bf16[240,896]{1,0:T(8,128)(2,1)}, f32[96,960]{1,0:T(8,128)}, f32[96,960]{1,0:T(8,128)}, f32[48,960]{1,0:T(8,128)}, bf16[14736,2048]{1,0:T(8,128)(2,1)S(1)}) custom-call(f32[240,896]{1,0:T(8,128)} %collective-permute-done.4.refs_0_, s32[10]{0:T(128)} %stack.43.refs_0_.refs_4_.refs_1_.refs_2_, ...), custom_call_target="tpu_custom_call", output_to_operand_aliasing={{4}: (5, {})} | custom-call | flops 4000000000 | tf_op jit(solution)/shard_map/pallas_call | solution.py:75
  51.7 5.5 %shard_map.84 = (f32[240,896]{1,0:T(8,128)}, bf16[14736,2048]{1,0:T(8,128)(2,1)S(1)}) custom-call(s32[10]{0:T(128)} %stack.43.refs_0_.refs_4_.refs_1_.refs_2_, bf16[7392,2048]{1,0:T(8,128)(2,1)} %bitcast.30, bf16[7392,2048]{1,0:T(8,128)(2,1)} %bitcast.41, bf16[7392,2048]{1,0:T(8,128)(2,1)} %bitcast.52, ...), custom_call_target="tpu_custom_call", output_to_operand_aliasing={{1}: (4, {})} | custom-call | flops 2000000000 | tf_op jit(solution)/shard_map/pallas_call | solution.py:75
  57.4 7.0 %shard_map.85 = (bf16[144,960]{1,0:T(8,128)(2,1)}, bf16[14736,2048]{1,0:T(8,128)(2,1)S(1)}) custom-call(f32[96,960]{1,0:T(8,128)} %collective-permute-done.6.refs_0_, f32[96,960]{1,0:T(8,128)} %collective-permute-done.7.refs_1_, f32[48,960]{1,0:T(8,128)} %collective-permute-done.8.refs_2_, ...), custom_call_target="tpu_custom_call", output_to_operand_aliasing={{1}: (8, {})} | custom-call | flops 12000000000 | tf_op jit(solution)/shard_map/pallas_call | solution.py:75
  64.8 1.5 %collective-permute-start.10 = (bf16[144,960]{1,0:T(8,128)(2,1)}, bf16[144,960]{1,0:T(8,128)(2,1)}, u32[]{:S(2)}, u32[]{:S(2)}) collective-permute-start(bf16[144,960]{1,0:T(8,128)(2,1)} %get-tuple-element.42), channel_id=1, source_target_pairs={{0,2},{1,3},{2,0},{3,1},{4,6},{5,7},{6,4},{7,5},{8,10},{9,11},{10,... | collective-permute-start | bytes 829448 | tf_op jit(solution)/shard_map/ppermute | solution.py:327
  66.3 6.3 %shard_map.86 = (bf16[144,896]{1,0:T(8,128)(2,1)}, bf16[14736,2048]{1,0:T(8,128)(2,1)S(1)}) custom-call(f32[240,896]{1,0:T(8,128)} %collective-permute-done.12.refs_0_, bf16[240,896]{1,0:T(8,128)(2,1)} %collective-permute-done.13.refs_1_, s32[10]{0:T(128)} %stack.43.refs_0_.refs_4_.refs_1_.refs_2_, ...), custom_call_target="tpu_custom_call", output_to_operand_aliasing={{1}: (6, {})} | custom-call | flops 12000000000 | tf_op jit(solution)/shard_map/pallas_call | solution.py:75
  74.2 6.2 %shard_map.87.refs_6_ = bf16[14736,2048]{1,0:T(8,128)(2,1)S(1)} custom-call(bf16[144,960]{1,0:T(8,128)(2,1)} %collective-permute-done.11.refs_0_, bf16[144,960]{1,0:T(8,128)(2,1)} %collective-permute-done.10.refs_1_, s32[10]{0:T(128)} %stack.43.refs_0_.refs_4_.refs_1_.refs_2_, bf16[7392,2048]{1,0:T(8,128)(2,1)} %bitcast.33, ...), custom_call_target="tpu_custom_call", output_to_operand_aliasing={{}: (6, {})} | custom-call | flops 2000000000 | tf_op jit(solution)/shard_map/pallas_call | solution.py:75
  81.0 6.0 %shard_map.88.refs_3_ = bf16[14736,2048]{1,0:T(8,128)(2,1)S(1)} custom-call(bf16[144,896]{1,0:T(8,128)(2,1)} %collective-permute-done.17.refs_0_, bf16[144,896]{1,0:T(8,128)(2,1)} %collective-permute-done.15.refs_1_, s32[10]{0:T(128)} %stack.43.refs_0_.refs_4_.refs_1_.refs_2_, bf16[7392,2048]{1,0:T(8,128)(2,1)} %bitcast.34, ...), custom_call_target="tpu_custom_call", output_to_operand_aliasing={{}: (6, {})} | custom-call | flops 2000000000 | tf_op jit(solution)/shard_map/pallas_call | solution.py:75
  87.0 6.2 %shard_map.89 = (f32[48,2048]{1,0:T(8,128)}, bf16[48,2048]{1,0:T(8,128)(2,1)}, bf16[14736,2048]{1,0:T(8,128)(2,1)S(1)}) custom-call(bf16[144,960]{1,0:T(8,128)(2,1)} %collective-permute-done.14.refs_0_, bf16[144,896]{1,0:T(8,128)(2,1)} %collective-permute-done.16.refs_1_, s32[10]{0:T(128)} %stack.43.refs_0_.refs_4_.refs_1_.refs_2_, ...), custom_call_target="tpu_custom_call", output_to_operand_aliasing={{2}: (3, {})} | custom-call | flops 2000000000 | tf_op jit(solution)/shard_map/pallas_call | solution.py:75
  93.2 1.4 %collective-permute-start.18 = (bf16[48,2048]{1,0:T(8,128)(2,1)}, bf16[48,2048]{1,0:T(8,128)(2,1)S(1)}, u32[]{:S(2)}, u32[]{:S(2)}) collective-permute-start(bf16[48,2048]{1,0:T(8,128)(2,1)} %get-tuple-element.51), channel_id=1, source_target_pairs={{0,4},{4,0},{8,12},{12,8},{1,5},{5,1},{9,13},{13,9},{2,6},{6,2},{1... | collective-permute-start | bytes 589832 | tf_op jit(solution)/shard_map/ppermute | solution.py:322
  94.6 6.2 %collective-permute-done.18 = bf16[48,2048]{1,0:T(8,128)(2,1)S(1)} collective-permute-done((bf16[48,2048]{1,0:T(8,128)(2,1)}, bf16[48,2048]{1,0:T(8,128)(2,1)S(1)}, u32[]{:S(2)}, u32[]{:S(2)}) %collective-permute-start.18) | collective-permute-done | bytes 196640 | tf_op jit(solution)/shard_map/ppermute | solution.py:322
  102.4 3.2 %collective-permute-start.20 = (bf16[24,2048]{1,0:T(8,128)(2,1)S(1)}, bf16[24,2048]{1,0:T(8,128)(2,1)S(1)}, u32[]{:S(2)}, u32[]{:S(2)}) collective-permute-start(bf16[24,2048]{1,0:T(8,128)(2,1)S(1)} %get-tuple-element.55), channel_id=1, source_target_pairs={{0,24},{4,28},{8,16},{12,20},{16,8},{20,12},{24,0},{28,4},{1,25},{... | collective-permute-start | bytes 294920 | tf_op jit(solution)/shard_map/ppermute | solution.py:337
  105.6 1.8 %collective-permute-done.19 = bf16[24,2048]{1,0:T(8,128)(2,1)S(1)} collective-permute-done((bf16[24,2048]{1,0:T(8,128)(2,1)S(1)}, bf16[24,2048]{1,0:T(8,128)(2,1)S(1)}, u32[]{:S(2)}, u32[]{:S(2)}) %collective-permute-start.19) | collective-permute-done | bytes 98336 | tf_op jit(solution)/shard_map/ppermute | solution.py:337
  107.4 3.1 %collective-permute-done.20 = bf16[24,2048]{1,0:T(8,128)(2,1)S(1)} collective-permute-done((bf16[24,2048]{1,0:T(8,128)(2,1)S(1)}, bf16[24,2048]{1,0:T(8,128)(2,1)S(1)}, u32[]{:S(2)}, u32[]{:S(2)}) %collective-permute-start.20) | collective-permute-done | bytes 98336 | tf_op jit(solution)/shard_map/ppermute | solution.py:337
  110.5 1.6 %fusion.3 = (bf16[1,12,2048]{2,1,0:T(8,128)(2,1)}, bf16[1,12,2048]{2,1,0:T(8,128)(2,1)}) fusion(f32[24,2048]{1,0:T(8,128)S(1)} %convert_add_fusion, bf16[36,2048]{1,0:T(8,128)(2,1)} %collective-permute-done.3), kind=kLoop, calls=%fused_computation.8 | loop fusion | flops 147456 | bytes 393216 | tf_op jit(solution)/shard_map/broadcast_in_dim | solution.py:547
  (39 shorter events, 8.7 us)
Async XLA Ops:
  1.6 11.5 %copy-start = (bf16[36,2048]{1,0:T(8,128)(2,1)}, bf16[36,2048]{1,0:T(8,128)(2,1)S(1)}, u32[]{:S(2)}) copy-start(bf16[36,2048]{1,0:T(8,128)(2,1)S(1)} %pad_maximum_fusion.refs_0_) | copy-start | bytes 442372
  1.6 13.1 %collective-permute-start = (bf16[36,2048]{1,0:T(8,128)(2,1)S(1)}, bf16[36,2048]{1,0:T(8,128)(2,1)}, u32[]{:S(2)}, u32[]{:S(2)}) collective-permute-start(bf16[36,2048]{1,0:T(8,128)(2,1)S(1)} %pad_maximum_fusion.refs_0_), channel_id=1, source_target_pairs={{0,8},{4,12},{8,0},{12,4},{1,9},{5,13},{9,1},{13,5},{2,10},{6,14},... | collective-permute-start | bytes 442376 | tf_op jit(solution)/shard_map/ppermute | solution.py:322
  6.4 13.7 %collective-permute-start.1 = (bf16[36,2048]{1,0:T(8,128)(2,1)S(1)}, bf16[36,2048]{1,0:T(8,128)(2,1)}, u32[]{:S(2)}, u32[]{:S(2)}) collective-permute-start(bf16[36,2048]{1,0:T(8,128)(2,1)S(1)} %pad_maximum_fusion.refs_0_), channel_id=1, source_target_pairs={{0,4},{4,0},{8,12},{12,8},{1,5},{5,1},{9,13},{13,9},{2,6},{6,2},{1... | collective-permute-start | bytes 442376 | tf_op jit(solution)/shard_map/ppermute | solution.py:322
  13.1 6.9 %collective-permute-start.3 = (bf16[36,2048]{1,0:T(8,128)(2,1)S(1)}, bf16[36,2048]{1,0:T(8,128)(2,1)}, u32[]{:S(2)}, u32[]{:S(2)}) collective-permute-start(bf16[36,2048]{1,0:T(8,128)(2,1)S(1)} %pad_maximum_fusion.refs_0_), channel_id=1, source_target_pairs={{0,16},{4,20},{8,24},{12,28},{16,0},{20,4},{24,8},{28,12},{1,17},{... | collective-permute-start | bytes 442376 | tf_op jit(solution)/shard_map/ppermute | solution.py:337
  14.7 5.6 %collective-permute-start.2 = (bf16[36,2048]{1,0:T(8,128)(2,1)}, bf16[36,2048]{1,0:T(8,128)(2,1)}, u32[]{:S(2)}, u32[]{:S(2)}) collective-permute-start(bf16[36,2048]{1,0:T(8,128)(2,1)} %collective-permute-done.refs_1_), channel_id=1, source_target_pairs={{0,4},{4,0},{8,12},{12,8},{1,5},{5,1},{9,13},{13,9},{2,6},{6,2},{1... | collective-permute-start | bytes 442376 | tf_op jit(solution)/shard_map/ppermute | solution.py:322
  28.0 5.9 %collective-permute-start.5 = (f32[240,960]{1,0:T(8,128)}, f32[240,960]{1,0:T(8,128)}, u32[]{:S(2)}, u32[]{:S(2)}) collective-permute-start(f32[240,960]{1,0:T(8,128)} %get-tuple-element.33), channel_id=1, source_target_pairs={{0,1},{1,0},{2,3},{3,2},{4,5},{5,4},{6,7},{7,6},{8,9},{9,8},{10,11... | collective-permute-start | bytes 2764808 | tf_op jit(solution)/shard_map/ppermute | solution.py:322
  33.4 8.6 %collective-permute-start.4 = (f32[240,896]{1,0:T(8,128)}, f32[240,896]{1,0:T(8,128)}, u32[]{:S(2)}, u32[]{:S(2)}) collective-permute-start(f32[240,896]{1,0:T(8,128)} %get-tuple-element.32), channel_id=1, source_target_pairs={{0,1},{1,0},{2,3},{3,2},{4,5},{5,4},{6,7},{7,6},{8,9},{9,8},{10,11... | collective-permute-start | bytes 2580488 | tf_op jit(solution)/shard_map/ppermute | solution.py:322
  40.4 17.0 %collective-permute-start.9 = (bf16[240,960]{1,0:T(8,128)(2,1)}, bf16[240,960]{1,0:T(8,128)(2,1)}, u32[]{:S(2)}, u32[]{:S(2)}) collective-permute-start(bf16[240,960]{1,0:T(8,128)(2,1)} %get-tuple-element.39), channel_id=1, source_target_pairs={{0,2},{1,3},{2,0},{3,1},{4,6},{5,7},{6,4},{7,5},{8,10},{9,11},{10,... | collective-permute-start | bytes 1382408 | tf_op jit(solution)/shard_map/ppermute | solution.py:327
  50.5 6.9 %collective-permute-start.6 = (f32[96,960]{1,0:T(8,128)}, f32[96,960]{1,0:T(8,128)}, u32[]{:S(2)}, u32[]{:S(2)}) collective-permute-start(f32[96,960]{1,0:T(8,128)} %get-tuple-element.36), channel_id=1, source_target_pairs={{0,1},{1,0},{2,3},{3,2},{4,5},{5,4},{6,7},{7,6},{8,9},{9,8},{10,11... | collective-permute-start | bytes 1105928 | tf_op jit(solution)/shard_map/ppermute | solution.py:322
  50.6 6.8 %collective-permute-start.7 = (f32[96,960]{1,0:T(8,128)}, f32[96,960]{1,0:T(8,128)}, u32[]{:S(2)}, u32[]{:S(2)}) collective-permute-start(f32[96,960]{1,0:T(8,128)} %get-tuple-element.37), channel_id=1, source_target_pairs={{0,1},{1,0},{2,3},{3,2},{4,5},{5,4},{6,7},{7,6},{8,9},{9,8},{10,11... | collective-permute-start | bytes 1105928 | tf_op jit(solution)/shard_map/ppermute | solution.py:322
  51.1 6.1 %collective-permute-start.8 = (f32[48,960]{1,0:T(8,128)}, f32[48,960]{1,0:T(8,128)}, u32[]{:S(2)}, u32[]{:S(2)}) collective-permute-start(f32[48,960]{1,0:T(8,128)} %get-tuple-element.38), channel_id=1, source_target_pairs={{0,1},{1,0},{2,3},{3,2},{4,5},{5,4},{6,7},{7,6},{8,9},{9,8},{10,11... | collective-permute-start | bytes 552968 | tf_op jit(solution)/shard_map/ppermute | solution.py:322
  51.1 15.2 %collective-permute-start.13 = (bf16[240,896]{1,0:T(8,128)(2,1)}, bf16[240,896]{1,0:T(8,128)(2,1)}, u32[]{:S(2)}, u32[]{:S(2)}) collective-permute-start(bf16[240,896]{1,0:T(8,128)(2,1)} %get-tuple-element.44), channel_id=1, source_target_pairs={{0,2},{1,3},{2,0},{3,1},{4,6},{5,7},{6,4},{7,5},{8,10},{9,11},{10,... | collective-permute-start | bytes 1290248 | tf_op jit(solution)/shard_map/ppermute | solution.py:327
  57.1 9.2 %collective-permute-start.12 = (f32[240,896]{1,0:T(8,128)}, f32[240,896]{1,0:T(8,128)}, u32[]{:S(2)}, u32[]{:S(2)}) collective-permute-start(f32[240,896]{1,0:T(8,128)} %get-tuple-element.43), channel_id=1, source_target_pairs={{0,1},{1,0},{2,3},{3,2},{4,5},{5,4},{6,7},{7,6},{8,9},{9,8},{10,11... | collective-permute-start | bytes 2580488 | tf_op jit(solution)/shard_map/ppermute | solution.py:322
  64.4 8.8 %collective-permute-start.11 = (bf16[144,960]{1,0:T(8,128)(2,1)}, bf16[144,960]{1,0:T(8,128)(2,1)}, u32[]{:S(2)}, u32[]{:S(2)}) collective-permute-start(bf16[144,960]{1,0:T(8,128)(2,1)} %get-tuple-element.42), channel_id=1, source_target_pairs={{0,1},{1,0},{2,3},{3,2},{4,5},{5,4},{6,7},{7,6},{8,9},{9,8},{10,11... | collective-permute-start | bytes 829448 | tf_op jit(solution)/shard_map/ppermute | solution.py:322
  64.8 9.4 %collective-permute-start.10 = (bf16[144,960]{1,0:T(8,128)(2,1)}, bf16[144,960]{1,0:T(8,128)(2,1)}, u32[]{:S(2)}, u32[]{:S(2)}) collective-permute-start(bf16[144,960]{1,0:T(8,128)(2,1)} %get-tuple-element.42), channel_id=1, source_target_pairs={{0,2},{1,3},{2,0},{3,1},{4,6},{5,7},{6,4},{7,5},{8,10},{9,11},{10,... | collective-permute-start | bytes 829448 | tf_op jit(solution)/shard_map/ppermute | solution.py:327
  72.6 8.4 %collective-permute-start.15 = (bf16[144,896]{1,0:T(8,128)(2,1)}, bf16[144,896]{1,0:T(8,128)(2,1)}, u32[]{:S(2)}, u32[]{:S(2)}) collective-permute-start(bf16[144,896]{1,0:T(8,128)(2,1)} %get-tuple-element.48), channel_id=1, source_target_pairs={{0,2},{1,3},{2,0},{3,1},{4,6},{5,7},{6,4},{7,5},{8,10},{9,11},{10,... | collective-permute-start | bytes 774152 | tf_op jit(solution)/shard_map/ppermute | solution.py:327
  73.2 7.8 %collective-permute-start.17 = (bf16[144,896]{1,0:T(8,128)(2,1)}, bf16[144,896]{1,0:T(8,128)(2,1)}, u32[]{:S(2)}, u32[]{:S(2)}) collective-permute-start(bf16[144,896]{1,0:T(8,128)(2,1)} %get-tuple-element.48), channel_id=1, source_target_pairs={{0,1},{1,0},{2,3},{3,2},{4,5},{5,4},{6,7},{7,6},{8,9},{9,8},{10,11... | collective-permute-start | bytes 774152 | tf_op jit(solution)/shard_map/ppermute | solution.py:322
  80.4 6.6 %collective-permute-start.14 = (bf16[144,960]{1,0:T(8,128)(2,1)}, bf16[144,960]{1,0:T(8,128)(2,1)}, u32[]{:S(2)}, u32[]{:S(2)}) collective-permute-start(bf16[144,960]{1,0:T(8,128)(2,1)} %collective-permute-done.10.refs_1_), channel_id=1, source_target_pairs={{0,1},{1,0},{2,3},{3,2},{4,5},{5,4},{6,7},{7,6},{8,9},{9,8},{10,11... | collective-permute-start | bytes 829448 | tf_op jit(solution)/shard_map/ppermute | solution.py:322
  81.0 6.0 %collective-permute-start.16 = (bf16[144,896]{1,0:T(8,128)(2,1)}, bf16[144,896]{1,0:T(8,128)(2,1)}, u32[]{:S(2)}, u32[]{:S(2)}) collective-permute-start(bf16[144,896]{1,0:T(8,128)(2,1)} %collective-permute-done.15.refs_1_), channel_id=1, source_target_pairs={{0,1},{1,0},{2,3},{3,2},{4,5},{5,4},{6,7},{7,6},{8,9},{9,8},{10,11... | collective-permute-start | bytes 774152 | tf_op jit(solution)/shard_map/ppermute | solution.py:322
  93.2 7.6 %collective-permute-start.18 = (bf16[48,2048]{1,0:T(8,128)(2,1)}, bf16[48,2048]{1,0:T(8,128)(2,1)S(1)}, u32[]{:S(2)}, u32[]{:S(2)}) collective-permute-start(bf16[48,2048]{1,0:T(8,128)(2,1)} %get-tuple-element.51), channel_id=1, source_target_pairs={{0,4},{4,0},{8,12},{12,8},{1,5},{5,1},{9,13},{13,9},{2,6},{6,2},{1... | collective-permute-start | bytes 589832 | tf_op jit(solution)/shard_map/ppermute | solution.py:322
  101.8 5.6 %collective-permute-start.19 = (bf16[24,2048]{1,0:T(8,128)(2,1)S(1)}, bf16[24,2048]{1,0:T(8,128)(2,1)S(1)}, u32[]{:S(2)}, u32[]{:S(2)}) collective-permute-start(bf16[24,2048]{1,0:T(8,128)(2,1)S(1)} %get-tuple-element.54), channel_id=1, source_target_pairs={{0,16},{4,20},{8,24},{12,28},{16,0},{20,4},{24,8},{28,12},{1,17},{... | collective-permute-start | bytes 294920 | tf_op jit(solution)/shard_map/ppermute | solution.py:337
  102.4 8.0 %collective-permute-start.20 = (bf16[24,2048]{1,0:T(8,128)(2,1)S(1)}, bf16[24,2048]{1,0:T(8,128)(2,1)S(1)}, u32[]{:S(2)}, u32[]{:S(2)}) collective-permute-start(bf16[24,2048]{1,0:T(8,128)(2,1)S(1)} %get-tuple-element.55), channel_id=1, source_target_pairs={{0,24},{4,28},{8,16},{12,20},{16,8},{20,12},{24,0},{28,4},{1,25},{... | collective-permute-start | bytes 294920 | tf_op jit(solution)/shard_map/ppermute | solution.py:337

commit v5 on v4

--- a/solution.py
+++ b/solution.py
@@ -169,6 +169,7 @@
 
     for number, (job, part_ref, out_sems, held, arrivals, h_ref, first_ref, to) in enumerate(work):
         at, rows, entry = job["at"], job["rows"], job["entry"]
+        step = 512 if job["fresh"] else STEP
         pending = (0, 1, 2) if copies and entry is None and len(work) == 1 else (0,)
         pending = pending if arrivals else ()
         if arrivals and pending == (0, 1, 2) and not number:
@@ -180,7 +181,7 @@
             return part
 
         def complete(i):
-            for low, size in spans(rows):
+            for low, size in spans(rows, step):
                 piece = pl.ds(low, size)
                 part = finished(first_ref[blocks[i], piece], i, piece)
                 part_ref[blocks[i], piece] = part.astype(part_ref.dtype)
@@ -193,7 +194,7 @@
 
         for i, (first, count) in enumerate(((0, 2), (0, 2), (2, 1))):
             lhs = arena[pl.ds(base + first * tokens, count * tokens), :]
-            for low, size in spans(rows):
+            for low, size in spans(rows, step):
                 piece = pl.ds(low, size)
                 part = contract(lhs, arena[pl.ds(at + i * rows + low, size), :], NT)
                 if i in pending:
@@ -231,7 +232,7 @@
         if entry is not None:
             leaving.append(pltpu.make_async_copy(h_ref, to[0], out_sems.at[0]))
             leaving[-1].start()
-            for low, size in spans(arena.shape[1]):
+            for low, size in spans(arena.shape[1], step):
                 piece = pl.ds(low, size)
                 for part in (0, 1):
                     value = products(arena, [h_ref], [(at, rows)], part, tokens, piece)
@@ -376,7 +377,7 @@
         jnp.where((row // t == i) & (column == source), 1.0, 0.0).astype(BF16) for i in range(count)
     ]
     base = arena.shape[0] - 7 * count * t
-    for low, size in spans(arena.shape[1]):
+    for low, size in spans(arena.shape[1], 512):
         piece = pl.ds(low, size)
         rows = sum(contract(pick, operand[:, piece], NN) for pick, operand in zip(picks, operands))
         arena[pl.ds(base, shape[0]), piece] = rows.astype(BF16)

time: 113 us -> 112 us (level)
  transfers between devices with their start and end apart: 21 -> 21, of which waited for: 6 -> 6; matrix products, arithmetic and copies ran while one was open for 1% -> 1% of each run, Pallas kernels for 55% -> 54%
where the time goes in v5:
time: 112 us
  Pallas kernels  74.3 us (66%)
  starting transfers between devices  19.2 us (17%)
  waiting for transfers between devices  12.9 us (12%)
  other arithmetic  3.57 us (3%)
    pallas_call x13, Pallas kernels, call(): pl.pallas_call(functools.partial(body, loads), in_specs=specs, out_specs=...  74.3 us
    ppermute x14, starting transfers between devices, swap(): lax.ppermute(value, axis, [(i, i ^ bit) for i in range(lax.axis_size(axis...  9.68 us
    ppermute x14, waiting for transfers between devices, swap(): lax.ppermute(value, axis, [(i, i ^ bit) for i in range(lax.axis_size(axis...  6.49 us
    ppermute x3, starting transfers between devices, cross_pipe(): return lax.ppermute(value, ('pipe', 'tx'), pairs)  5.32 us
    ppermute x3, waiting for transfers between devices, cross_pipe(): return lax.ppermute(value, ('pipe', 'tx'), pairs)  4.88 us
    ppermute x4, starting transfers between devices, to_chip(): lax.ppermute(value, 'ty', [(i, (i + 2 * k) % count) for i in range(count)])  4.17 us
  transfers between devices with their start and end apart: 21, of which 6 were waited for; matrix products, arithmetic and copies ran while one was open for 1% of the time, Pallas kernels for 54%

profile of v5, /device:TPU:0, one launch (start us, length us, event | category | flops | bytes accessed | tf_op | source)
XLA Modules:
  0.0 111.6 jit_solution(4649461128304942840)
XLA Ops:
  1.6 4.1 %collective-permute-start = (bf16[36,2048]{1,0:T(8,128)(2,1)S(1)}, bf16[36,2048]{1,0:T(8,128)(2,1)}, u32[]{:S(2)}, u32[]{:S(2)}) collective-permute-start(bf16[36,2048]{1,0:T(8,128)(2,1)S(1)} %pad_maximum_fusion.refs_0_), channel_id=1, source_target_pairs={{0,8},{4,12},{8,0},{12,4},{1,9},{5,13},{9,1},{13,5},{2,10},{6,14},... | collective-permute-start | bytes 442376 | tf_op jit(solution)/shard_map/ppermute | solution.py:323
  6.4 1.6 %collective-permute-start.1 = (bf16[36,2048]{1,0:T(8,128)(2,1)S(1)}, bf16[36,2048]{1,0:T(8,128)(2,1)}, u32[]{:S(2)}, u32[]{:S(2)}) collective-permute-start(bf16[36,2048]{1,0:T(8,128)(2,1)S(1)} %pad_maximum_fusion.refs_0_), channel_id=1, source_target_pairs={{0,4},{4,0},{8,12},{12,8},{1,5},{5,1},{9,13},{13,9},{2,6},{6,2},{1... | collective-permute-start | bytes 442376 | tf_op jit(solution)/shard_map/ppermute | solution.py:323
  8.0 5.1 %shard_map.77.refs_4_ = bf16[14736,2048]{1,0:T(8,128)(2,1)S(1)} custom-call(s32[10]{0:T(128)} %stack.43.refs_0_.refs_4_.refs_1_.refs_2_, bf16[7392,2048]{1,0:T(8,128)(2,1)} %bitcast.24, bf16[7392,2048]{1,0:T(8,128)(2,1)} %bitcast.35, bf16[7392,2048]{1,0:T(8,128)(2,1)} %bitcast.46), custom_call_target="tpu_custom_call" | custom-call | flops 2000000000 | tf_op jit(solution)/shard_map/pallas_call | solution.py:75
  13.1 1.6 %collective-permute-start.3 = (bf16[36,2048]{1,0:T(8,128)(2,1)S(1)}, bf16[36,2048]{1,0:T(8,128)(2,1)}, u32[]{:S(2)}, u32[]{:S(2)}) collective-permute-start(bf16[36,2048]{1,0:T(8,128)(2,1)S(1)} %pad_maximum_fusion.refs_0_), channel_id=1, source_target_pairs={{0,16},{4,20},{8,24},{12,28},{16,0},{20,4},{24,8},{28,12},{1,17},{... | collective-permute-start | bytes 442376 | tf_op jit(solution)/shard_map/ppermute | solution.py:338
  15.1 4.9 %shard_map.78.refs_5_ = bf16[14736,2048]{1,0:T(8,128)(2,1)S(1)} custom-call(s32[10]{0:T(128)} %stack.43.refs_0_.refs_4_.refs_1_.refs_2_, bf16[7392,2048]{1,0:T(8,128)(2,1)} %bitcast.25, bf16[7392,2048]{1,0:T(8,128)(2,1)} %bitcast.36, bf16[7392,2048]{1,0:T(8,128)(2,1)} %bitcast.47, ...), custom_call_target="tpu_custom_call", output_to_operand_aliasing={{}: (4, {})} | custom-call | flops 2000000000 | tf_op jit(solution)/shard_map/pallas_call | solution.py:75
  20.3 2.0 %shard_map.79.refs_4_ = bf16[14736,2048]{1,0:T(8,128)(2,1)S(1)} custom-call(bf16[36,2048]{1,0:T(8,128)(2,1)} %copy-done, bf16[36,2048]{1,0:T(8,128)(2,1)} %collective-permute-done.refs_1_, bf16[36,2048]{1,0:T(8,128)(2,1)} %collective-permute-done.1.refs_2_, bf16[36,2048]{1,0:T(8,128)(2,1)} %collective-permute-done.2.refs_3_, ...), custom_call_target="tpu_custom_call", output_to_operand_aliasing={{}: (5, {})} | custom-call | flops 2000000000 | tf_op jit(solution)/shard_map/pallas_call | solution.py:75
  22.3 5.5 %shard_map.80 = (f32[240,960]{1,0:T(8,128)}, bf16[14736,2048]{1,0:T(8,128)(2,1)S(1)}) custom-call(s32[10]{0:T(128)} %stack.43.refs_0_.refs_4_.refs_1_.refs_2_, bf16[7392,2048]{1,0:T(8,128)(2,1)} %bitcast.26, bf16[7392,2048]{1,0:T(8,128)(2,1)} %bitcast.37, bf16[7392,2048]{1,0:T(8,128)(2,1)} %bitcast.48, ...), custom_call_target="tpu_custom_call", output_to_operand_aliasing={{1}: (4, {})} | custom-call | flops 2000000000 | tf_op jit(solution)/shard_map/pallas_call | solution.py:75
  27.9 5.2 %shard_map.81 = (f32[240,896]{1,0:T(8,128)}, bf16[14736,2048]{1,0:T(8,128)(2,1)S(1)}) custom-call(s32[10]{0:T(128)} %stack.43.refs_0_.refs_4_.refs_1_.refs_2_, bf16[7392,2048]{1,0:T(8,128)(2,1)} %bitcast.27, bf16[7392,2048]{1,0:T(8,128)(2,1)} %bitcast.38, bf16[7392,2048]{1,0:T(8,128)(2,1)} %bitcast.49, ...), custom_call_target="tpu_custom_call", output_to_operand_aliasing={{1}: (4, {})} | custom-call | flops 2000000000 | tf_op jit(solution)/shard_map/pallas_call | solution.py:75
  33.7 6.4 %shard_map.82 = (bf16[240,960]{1,0:T(8,128)(2,1)}, bf16[14736,2048]{1,0:T(8,128)(2,1)S(1)}) custom-call(f32[240,960]{1,0:T(8,128)} %collective-permute-done.5.refs_0_, s32[10]{0:T(128)} %stack.43.refs_0_.refs_4_.refs_1_.refs_2_, bf16[7392,2048]{1,0:T(8,128)(2,1)} %bitcast.28, bf16[7392,2048]{1,0:T(8,128)(2,1)} %bitcast.39, ...), custom_call_target="tpu_custom_call", output_to_operand_aliasing={{1}: (5, {})} | custom-call | flops 2000000000 | tf_op jit(solution)/shard_map/pallas_call | solution.py:75
  40.1 1.6 %collective-permute-start.9 = (bf16[240,960]{1,0:T(8,128)(2,1)}, bf16[240,960]{1,0:T(8,128)(2,1)}, u32[]{:S(2)}, u32[]{:S(2)}) collective-permute-start(bf16[240,960]{1,0:T(8,128)(2,1)} %get-tuple-element.39), channel_id=1, source_target_pairs={{0,2},{1,3},{2,0},{3,1},{4,6},{5,7},{6,4},{7,5},{8,10},{9,11},{10,... | collective-permute-start | bytes 1382408 | tf_op jit(solution)/shard_map/ppermute | solution.py:328
  41.7 8.4 %shard_map.83 = (bf16[240,896]{1,0:T(8,128)(2,1)}, f32[96,960]{1,0:T(8,128)}, f32[96,960]{1,0:T(8,128)}, f32[48,960]{1,0:T(8,128)}, bf16[14736,2048]{1,0:T(8,128)(2,1)S(1)}) custom-call(f32[240,896]{1,0:T(8,128)} %collective-permute-done.4.refs_0_, s32[10]{0:T(128)} %stack.43.refs_0_.refs_4_.refs_1_.refs_2_, ...), custom_call_target="tpu_custom_call", output_to_operand_aliasing={{4}: (5, {})} | custom-call | flops 4000000000 | tf_op jit(solution)/shard_map/pallas_call | solution.py:75
  51.4 5.5 %shard_map.84 = (f32[240,896]{1,0:T(8,128)}, bf16[14736,2048]{1,0:T(8,128)(2,1)S(1)}) custom-call(s32[10]{0:T(128)} %stack.43.refs_0_.refs_4_.refs_1_.refs_2_, bf16[7392,2048]{1,0:T(8,128)(2,1)} %bitcast.30, bf16[7392,2048]{1,0:T(8,128)(2,1)} %bitcast.41, bf16[7392,2048]{1,0:T(8,128)(2,1)} %bitcast.52, ...), custom_call_target="tpu_custom_call", output_to_operand_aliasing={{1}: (4, {})} | custom-call | flops 2000000000 | tf_op jit(solution)/shard_map/pallas_call | solution.py:75
  57.2 6.7 %shard_map.85 = (bf16[144,960]{1,0:T(8,128)(2,1)}, bf16[14736,2048]{1,0:T(8,128)(2,1)S(1)}) custom-call(f32[96,960]{1,0:T(8,128)} %collective-permute-done.6.refs_0_, f32[96,960]{1,0:T(8,128)} %collective-permute-done.7.refs_1_, f32[48,960]{1,0:T(8,128)} %collective-permute-done.8.refs_2_, ...), custom_call_target="tpu_custom_call", output_to_operand_aliasing={{1}: (8, {})} | custom-call | flops 12000000000 | tf_op jit(solution)/shard_map/pallas_call | solution.py:75
  64.3 1.5 %collective-permute-start.10 = (bf16[144,960]{1,0:T(8,128)(2,1)}, bf16[144,960]{1,0:T(8,128)(2,1)}, u32[]{:S(2)}, u32[]{:S(2)}) collective-permute-start(bf16[144,960]{1,0:T(8,128)(2,1)} %get-tuple-element.42), channel_id=1, source_target_pairs={{0,2},{1,3},{2,0},{3,1},{4,6},{5,7},{6,4},{7,5},{8,10},{9,11},{10,... | collective-permute-start | bytes 829448 | tf_op jit(solution)/shard_map/ppermute | solution.py:328
  65.8 6.3 %shard_map.86 = (bf16[144,896]{1,0:T(8,128)(2,1)}, bf16[14736,2048]{1,0:T(8,128)(2,1)S(1)}) custom-call(f32[240,896]{1,0:T(8,128)} %collective-permute-done.12.refs_0_, bf16[240,896]{1,0:T(8,128)(2,1)} %collective-permute-done.13.refs_1_, s32[10]{0:T(128)} %stack.43.refs_0_.refs_4_.refs_1_.refs_2_, ...), custom_call_target="tpu_custom_call", output_to_operand_aliasing={{1}: (6, {})} | custom-call | flops 12000000000 | tf_op jit(solution)/shard_map/pallas_call | solution.py:75
  73.7 6.2 %shard_map.87.refs_6_ = bf16[14736,2048]{1,0:T(8,128)(2,1)S(1)} custom-call(bf16[144,960]{1,0:T(8,128)(2,1)} %collective-permute-done.11.refs_0_, bf16[144,960]{1,0:T(8,128)(2,1)} %collective-permute-done.10.refs_1_, s32[10]{0:T(128)} %stack.43.refs_0_.refs_4_.refs_1_.refs_2_, bf16[7392,2048]{1,0:T(8,128)(2,1)} %bitcast.33, ...), custom_call_target="tpu_custom_call", output_to_operand_aliasing={{}: (6, {})} | custom-call | flops 2000000000 | tf_op jit(solution)/shard_map/pallas_call | solution.py:75
  80.5 6.0 %shard_map.88.refs_3_ = bf16[14736,2048]{1,0:T(8,128)(2,1)S(1)} custom-call(bf16[144,896]{1,0:T(8,128)(2,1)} %collective-permute-done.17.refs_0_, bf16[144,896]{1,0:T(8,128)(2,1)} %collective-permute-done.15.refs_1_, s32[10]{0:T(128)} %stack.43.refs_0_.refs_4_.refs_1_.refs_2_, bf16[7392,2048]{1,0:T(8,128)(2,1)} %bitcast.34, ...), custom_call_target="tpu_custom_call", output_to_operand_aliasing={{}: (6, {})} | custom-call | flops 2000000000 | tf_op jit(solution)/shard_map/pallas_call | solution.py:75
  86.5 6.2 %shard_map.89 = (f32[48,2048]{1,0:T(8,128)}, bf16[48,2048]{1,0:T(8,128)(2,1)}, bf16[14736,2048]{1,0:T(8,128)(2,1)S(1)}) custom-call(bf16[144,960]{1,0:T(8,128)(2,1)} %collective-permute-done.14.refs_0_, bf16[144,896]{1,0:T(8,128)(2,1)} %collective-permute-done.16.refs_1_, s32[10]{0:T(128)} %stack.43.refs_0_.refs_4_.refs_1_.refs_2_, ...), custom_call_target="tpu_custom_call", output_to_operand_aliasing={{2}: (3, {})} | custom-call | flops 2000000000 | tf_op jit(solution)/shard_map/pallas_call | solution.py:75
  92.7 1.4 %collective-permute-start.18 = (bf16[48,2048]{1,0:T(8,128)(2,1)}, bf16[48,2048]{1,0:T(8,128)(2,1)S(1)}, u32[]{:S(2)}, u32[]{:S(2)}) collective-permute-start(bf16[48,2048]{1,0:T(8,128)(2,1)} %get-tuple-element.51), channel_id=1, source_target_pairs={{0,4},{4,0},{8,12},{12,8},{1,5},{5,1},{9,13},{13,9},{2,6},{6,2},{1... | collective-permute-start | bytes 589832 | tf_op jit(solution)/shard_map/ppermute | solution.py:323
  94.1 6.2 %collective-permute-done.18 = bf16[48,2048]{1,0:T(8,128)(2,1)S(1)} collective-permute-done((bf16[48,2048]{1,0:T(8,128)(2,1)}, bf16[48,2048]{1,0:T(8,128)(2,1)S(1)}, u32[]{:S(2)}, u32[]{:S(2)}) %collective-permute-start.18) | collective-permute-done | bytes 196640 | tf_op jit(solution)/shard_map/ppermute | solution.py:323
  101.9 3.2 %collective-permute-start.20 = (bf16[24,2048]{1,0:T(8,128)(2,1)S(1)}, bf16[24,2048]{1,0:T(8,128)(2,1)S(1)}, u32[]{:S(2)}, u32[]{:S(2)}) collective-permute-start(bf16[24,2048]{1,0:T(8,128)(2,1)S(1)} %get-tuple-element.55), channel_id=1, source_target_pairs={{0,24},{4,28},{8,16},{12,20},{16,8},{20,12},{24,0},{28,4},{1,25},{... | collective-permute-start | bytes 294920 | tf_op jit(solution)/shard_map/ppermute | solution.py:338
  105.1 1.8 %collective-permute-done.19 = bf16[24,2048]{1,0:T(8,128)(2,1)S(1)} collective-permute-done((bf16[24,2048]{1,0:T(8,128)(2,1)S(1)}, bf16[24,2048]{1,0:T(8,128)(2,1)S(1)}, u32[]{:S(2)}, u32[]{:S(2)}) %collective-permute-start.19) | collective-permute-done | bytes 98336 | tf_op jit(solution)/shard_map/ppermute | solution.py:338
  106.9 3.1 %collective-permute-done.20 = bf16[24,2048]{1,0:T(8,128)(2,1)S(1)} collective-permute-done((bf16[24,2048]{1,0:T(8,128)(2,1)S(1)}, bf16[24,2048]{1,0:T(8,128)(2,1)S(1)}, u32[]{:S(2)}, u32[]{:S(2)}) %collective-permute-start.20) | collective-permute-done | bytes 98336 | tf_op jit(solution)/shard_map/ppermute | solution.py:338
  110.0 1.6 %fusion.3 = (bf16[1,12,2048]{2,1,0:T(8,128)(2,1)}, bf16[1,12,2048]{2,1,0:T(8,128)(2,1)}) fusion(f32[24,2048]{1,0:T(8,128)S(1)} %convert_add_fusion, bf16[36,2048]{1,0:T(8,128)(2,1)} %collective-permute-done.3), kind=kLoop, calls=%fused_computation.8 | loop fusion | flops 147456 | bytes 393216 | tf_op jit(solution)/shard_map/broadcast_in_dim | solution.py:548
  (39 shorter events, 8.8 us)
Async XLA Ops:
  1.6 11.5 %copy-start = (bf16[36,2048]{1,0:T(8,128)(2,1)}, bf16[36,2048]{1,0:T(8,128)(2,1)S(1)}, u32[]{:S(2)}) copy-start(bf16[36,2048]{1,0:T(8,128)(2,1)S(1)} %pad_maximum_fusion.refs_0_) | copy-start | bytes 442372
  1.6 13.1 %collective-permute-start = (bf16[36,2048]{1,0:T(8,128)(2,1)S(1)}, bf16[36,2048]{1,0:T(8,128)(2,1)}, u32[]{:S(2)}, u32[]{:S(2)}) collective-permute-start(bf16[36,2048]{1,0:T(8,128)(2,1)S(1)} %pad_maximum_fusion.refs_0_), channel_id=1, source_target_pairs={{0,8},{4,12},{8,0},{12,4},{1,9},{5,13},{9,1},{13,5},{2,10},{6,14},... | collective-permute-start | bytes 442376 | tf_op jit(solution)/shard_map/ppermute | solution.py:323
  6.4 13.7 %collective-permute-start.1 = (bf16[36,2048]{1,0:T(8,128)(2,1)S(1)}, bf16[36,2048]{1,0:T(8,128)(2,1)}, u32[]{:S(2)}, u32[]{:S(2)}) collective-permute-start(bf16[36,2048]{1,0:T(8,128)(2,1)S(1)} %pad_maximum_fusion.refs_0_), channel_id=1, source_target_pairs={{0,4},{4,0},{8,12},{12,8},{1,5},{5,1},{9,13},{13,9},{2,6},{6,2},{1... | collective-permute-start | bytes 442376 | tf_op jit(solution)/shard_map/ppermute | solution.py:323
  13.1 6.9 %collective-permute-start.3 = (bf16[36,2048]{1,0:T(8,128)(2,1)S(1)}, bf16[36,2048]{1,0:T(8,128)(2,1)}, u32[]{:S(2)}, u32[]{:S(2)}) collective-permute-start(bf16[36,2048]{1,0:T(8,128)(2,1)S(1)} %pad_maximum_fusion.refs_0_), channel_id=1, source_target_pairs={{0,16},{4,20},{8,24},{12,28},{16,0},{20,4},{24,8},{28,12},{1,17},{... | collective-permute-start | bytes 442376 | tf_op jit(solution)/shard_map/ppermute | solution.py:338
  14.7 5.6 %collective-permute-start.2 = (bf16[36,2048]{1,0:T(8,128)(2,1)}, bf16[36,2048]{1,0:T(8,128)(2,1)}, u32[]{:S(2)}, u32[]{:S(2)}) collective-permute-start(bf16[36,2048]{1,0:T(8,128)(2,1)} %collective-permute-done.refs_1_), channel_id=1, source_target_pairs={{0,4},{4,0},{8,12},{12,8},{1,5},{5,1},{9,13},{13,9},{2,6},{6,2},{1... | collective-permute-start | bytes 442376 | tf_op jit(solution)/shard_map/ppermute | solution.py:323
  27.8 5.9 %collective-permute-start.5 = (f32[240,960]{1,0:T(8,128)}, f32[240,960]{1,0:T(8,128)}, u32[]{:S(2)}, u32[]{:S(2)}) collective-permute-start(f32[240,960]{1,0:T(8,128)} %get-tuple-element.33), channel_id=1, source_target_pairs={{0,1},{1,0},{2,3},{3,2},{4,5},{5,4},{6,7},{7,6},{8,9},{9,8},{10,11... | collective-permute-start | bytes 2764808 | tf_op jit(solution)/shard_map/ppermute | solution.py:323
  33.1 8.6 %collective-permute-start.4 = (f32[240,896]{1,0:T(8,128)}, f32[240,896]{1,0:T(8,128)}, u32[]{:S(2)}, u32[]{:S(2)}) collective-permute-start(f32[240,896]{1,0:T(8,128)} %get-tuple-element.32), channel_id=1, source_target_pairs={{0,1},{1,0},{2,3},{3,2},{4,5},{5,4},{6,7},{7,6},{8,9},{9,8},{10,11... | collective-permute-start | bytes 2580488 | tf_op jit(solution)/shard_map/ppermute | solution.py:323
  40.1 17.0 %collective-permute-start.9 = (bf16[240,960]{1,0:T(8,128)(2,1)}, bf16[240,960]{1,0:T(8,128)(2,1)}, u32[]{:S(2)}, u32[]{:S(2)}) collective-permute-start(bf16[240,960]{1,0:T(8,128)(2,1)} %get-tuple-element.39), channel_id=1, source_target_pairs={{0,2},{1,3},{2,0},{3,1},{4,6},{5,7},{6,4},{7,5},{8,10},{9,11},{10,... | collective-permute-start | bytes 1382408 | tf_op jit(solution)/shard_map/ppermute | solution.py:328
  50.1 7.1 %collective-permute-start.6 = (f32[96,960]{1,0:T(8,128)}, f32[96,960]{1,0:T(8,128)}, u32[]{:S(2)}, u32[]{:S(2)}) collective-permute-start(f32[96,960]{1,0:T(8,128)} %get-tuple-element.36), channel_id=1, source_target_pairs={{0,1},{1,0},{2,3},{3,2},{4,5},{5,4},{6,7},{7,6},{8,9},{9,8},{10,11... | collective-permute-start | bytes 1105928 | tf_op jit(solution)/shard_map/ppermute | solution.py:323
  50.4 6.8 %collective-permute-start.7 = (f32[96,960]{1,0:T(8,128)}, f32[96,960]{1,0:T(8,128)}, u32[]{:S(2)}, u32[]{:S(2)}) collective-permute-start(f32[96,960]{1,0:T(8,128)} %get-tuple-element.37), channel_id=1, source_target_pairs={{0,1},{1,0},{2,3},{3,2},{4,5},{5,4},{6,7},{7,6},{8,9},{9,8},{10,11... | collective-permute-start | bytes 1105928 | tf_op jit(solution)/shard_map/ppermute | solution.py:323
  50.9 6.1 %collective-permute-start.8 = (f32[48,960]{1,0:T(8,128)}, f32[48,960]{1,0:T(8,128)}, u32[]{:S(2)}, u32[]{:S(2)}) collective-permute-start(f32[48,960]{1,0:T(8,128)} %get-tuple-element.38), channel_id=1, source_target_pairs={{0,1},{1,0},{2,3},{3,2},{4,5},{5,4},{6,7},{7,6},{8,9},{9,8},{10,11... | collective-permute-start | bytes 552968 | tf_op jit(solution)/shard_map/ppermute | solution.py:323
  50.9 14.9 %collective-permute-start.13 = (bf16[240,896]{1,0:T(8,128)(2,1)}, bf16[240,896]{1,0:T(8,128)(2,1)}, u32[]{:S(2)}, u32[]{:S(2)}) collective-permute-start(bf16[240,896]{1,0:T(8,128)(2,1)} %get-tuple-element.44), channel_id=1, source_target_pairs={{0,2},{1,3},{2,0},{3,1},{4,6},{5,7},{6,4},{7,5},{8,10},{9,11},{10,... | collective-permute-start | bytes 1290248 | tf_op jit(solution)/shard_map/ppermute | solution.py:328
  56.9 8.9 %collective-permute-start.12 = (f32[240,896]{1,0:T(8,128)}, f32[240,896]{1,0:T(8,128)}, u32[]{:S(2)}, u32[]{:S(2)}) collective-permute-start(f32[240,896]{1,0:T(8,128)} %get-tuple-element.43), channel_id=1, source_target_pairs={{0,1},{1,0},{2,3},{3,2},{4,5},{5,4},{6,7},{7,6},{8,9},{9,8},{10,11... | collective-permute-start | bytes 2580488 | tf_op jit(solution)/shard_map/ppermute | solution.py:323
  63.9 8.8 %collective-permute-start.11 = (bf16[144,960]{1,0:T(8,128)(2,1)}, bf16[144,960]{1,0:T(8,128)(2,1)}, u32[]{:S(2)}, u32[]{:S(2)}) collective-permute-start(bf16[144,960]{1,0:T(8,128)(2,1)} %get-tuple-element.42), channel_id=1, source_target_pairs={{0,1},{1,0},{2,3},{3,2},{4,5},{5,4},{6,7},{7,6},{8,9},{9,8},{10,11... | collective-permute-start | bytes 829448 | tf_op jit(solution)/shard_map/ppermute | solution.py:323
  64.3 9.4 %collective-permute-start.10 = (bf16[144,960]{1,0:T(8,128)(2,1)}, bf16[144,960]{1,0:T(8,128)(2,1)}, u32[]{:S(2)}, u32[]{:S(2)}) collective-permute-start(bf16[144,960]{1,0:T(8,128)(2,1)} %get-tuple-element.42), channel_id=1, source_target_pairs={{0,2},{1,3},{2,0},{3,1},{4,6},{5,7},{6,4},{7,5},{8,10},{9,11},{10,... | collective-permute-start | bytes 829448 | tf_op jit(solution)/shard_map/ppermute | solution.py:328
  72.1 8.4 %collective-permute-start.15 = (bf16[144,896]{1,0:T(8,128)(2,1)}, bf16[144,896]{1,0:T(8,128)(2,1)}, u32[]{:S(2)}, u32[]{:S(2)}) collective-permute-start(bf16[144,896]{1,0:T(8,128)(2,1)} %get-tuple-element.48), channel_id=1, source_target_pairs={{0,2},{1,3},{2,0},{3,1},{4,6},{5,7},{6,4},{7,5},{8,10},{9,11},{10,... | collective-permute-start | bytes 774152 | tf_op jit(solution)/shard_map/ppermute | solution.py:328
  72.7 7.8 %collective-permute-start.17 = (bf16[144,896]{1,0:T(8,128)(2,1)}, bf16[144,896]{1,0:T(8,128)(2,1)}, u32[]{:S(2)}, u32[]{:S(2)}) collective-permute-start(bf16[144,896]{1,0:T(8,128)(2,1)} %get-tuple-element.48), channel_id=1, source_target_pairs={{0,1},{1,0},{2,3},{3,2},{4,5},{5,4},{6,7},{7,6},{8,9},{9,8},{10,11... | collective-permute-start | bytes 774152 | tf_op jit(solution)/shard_map/ppermute | solution.py:323
  79.9 6.6 %collective-permute-start.14 = (bf16[144,960]{1,0:T(8,128)(2,1)}, bf16[144,960]{1,0:T(8,128)(2,1)}, u32[]{:S(2)}, u32[]{:S(2)}) collective-permute-start(bf16[144,960]{1,0:T(8,128)(2,1)} %collective-permute-done.10.refs_1_), channel_id=1, source_target_pairs={{0,1},{1,0},{2,3},{3,2},{4,5},{5,4},{6,7},{7,6},{8,9},{9,8},{10,11... | collective-permute-start | bytes 829448 | tf_op jit(solution)/shard_map/ppermute | solution.py:323
  80.5 6.0 %collective-permute-start.16 = (bf16[144,896]{1,0:T(8,128)(2,1)}, bf16[144,896]{1,0:T(8,128)(2,1)}, u32[]{:S(2)}, u32[]{:S(2)}) collective-permute-start(bf16[144,896]{1,0:T(8,128)(2,1)} %collective-permute-done.15.refs_1_), channel_id=1, source_target_pairs={{0,1},{1,0},{2,3},{3,2},{4,5},{5,4},{6,7},{7,6},{8,9},{9,8},{10,11... | collective-permute-start | bytes 774152 | tf_op jit(solution)/shard_map/ppermute | solution.py:323
  92.7 7.6 %collective-permute-start.18 = (bf16[48,2048]{1,0:T(8,128)(2,1)}, bf16[48,2048]{1,0:T(8,128)(2,1)S(1)}, u32[]{:S(2)}, u32[]{:S(2)}) collective-permute-start(bf16[48,2048]{1,0:T(8,128)(2,1)} %get-tuple-element.51), channel_id=1, source_target_pairs={{0,4},{4,0},{8,12},{12,8},{1,5},{5,1},{9,13},{13,9},{2,6},{6,2},{1... | collective-permute-start | bytes 589832 | tf_op jit(solution)/shard_map/ppermute | solution.py:323
  101.3 5.5 %collective-permute-start.19 = (bf16[24,2048]{1,0:T(8,128)(2,1)S(1)}, bf16[24,2048]{1,0:T(8,128)(2,1)S(1)}, u32[]{:S(2)}, u32[]{:S(2)}) collective-permute-start(bf16[24,2048]{1,0:T(8,128)(2,1)S(1)} %get-tuple-element.54), channel_id=1, source_target_pairs={{0,16},{4,20},{8,24},{12,28},{16,0},{20,4},{24,8},{28,12},{1,17},{... | collective-permute-start | bytes 294920 | tf_op jit(solution)/shard_map/ppermute | solution.py:338
  101.9 8.0 %collective-permute-start.20 = (bf16[24,2048]{1,0:T(8,128)(2,1)S(1)}, bf16[24,2048]{1,0:T(8,128)(2,1)S(1)}, u32[]{:S(2)}, u32[]{:S(2)}) collective-permute-start(bf16[24,2048]{1,0:T(8,128)(2,1)S(1)} %get-tuple-element.55), channel_id=1, source_target_pairs={{0,24},{4,28},{8,16},{12,20},{16,8},{20,12},{24,0},{28,4},{1,25},{... | collective-permute-start | bytes 294920 | tf_op jit(solution)/shard_map/ppermute | solution.py:338
